TPU v7x, 128 devices: a whole 4x4x4 slice. The times are simulated.
128 devices in a mesh: gx: 8 (over z, x_hi), gy: 4 (over y), gz: 4 (over x_lo, core).
Axes of the slice: x: 4 (x_hi: 2, x_lo: 2; x = x_hi * 2 + x_lo), y: 4, z: 4, core: 2. Of those that a mesh axis runs over, the one named last changes fastest.
Arguments:
- tokens: bfloat16 [2048, 4096], P('gx', ('gz', 'gy')), may hold values from -6 to 6
- w_gate: bfloat16 [4096, 11264], P(('gz', 'gx'), 'gy'), may hold values from -0.09375 to 0.09375
- w_up: bfloat16 [4096, 11264], P(('gz', 'gx'), 'gy'), may hold values from -0.09375 to 0.09375
- w_down: bfloat16 [11264, 4096], P(('gy', 'gx'), 'gz'), may hold values from -0.0546875 to 0.0546875
- grad_output: bfloat16 [2048, 4096], P('gx', ('gz', 'gy')), may hold values from -6 to 6
Outputs:
- output: bfloat16 [2048, 4096], P('gx', ('gz', 'gy'))
- grad_input: bfloat16 [2048, 4096], P('gx', ('gz', 'gy'))
- grad_gate: bfloat16 [4096, 11264], P(('gz', 'gx'), 'gy')
- grad_up: bfloat16 [4096, 11264], P(('gz', 'gx'), 'gy')
- grad_down: bfloat16 [11264, 4096], P(('gy', 'gx'), 'gz')
All inputs are finite; a program needn't handle non-finite values.
Results may differ from a plain program's by a relative error of at most 0.029.
Values may be sent and summed in bfloat16 or wider, within the bound.
No kernel may reach another device: no remote copies, remote signals or barrier semaphores. Data moves between devices by JAX's collectives and lax.ppermute only.
A program may use at most 128 MiB of HBM per device.

v0:
```python
import math

import jax
import jax.numpy as jnp
from jax import lax
from jax.sharding import PartitionSpec as P


def transposed_product(left_side, right_side):
    return lax.dot_general(
        left_side, right_side, (((1,), (1,)), ((), ())), preferred_element_type=jnp.float32
    )


def leading_product(left_side, right_side):
    return lax.dot_general(
        left_side, right_side, (((0,), (0,)), ((), ())), preferred_element_type=jnp.float32
    )


def swiglu_grads(grad_hidden, gate_sum, up_sum):
    sigmoid_gate = jax.nn.sigmoid(gate_sum)
    grad_gate_act = (
        grad_hidden * up_sum * sigmoid_gate * (1.0 + gate_sum * (1.0 - sigmoid_gate))
    ).astype(jnp.bfloat16)
    grad_up_act = (grad_hidden * gate_sum * sigmoid_gate).astype(jnp.bfloat16)
    return (grad_gate_act, grad_up_act)


def on_device(tokens, w_gate, w_up, w_down, grad_output):
    tok_rows = tokens.shape[0]
    width_hidden = w_gate.shape[1]
    groups_gx = lax.axis_size("gx")
    loss_scale = 1.0 / math.sqrt(tok_rows * groups_gx)
    token_block, grad_block = (
        lax.all_gather(tokens, "gy", axis=1, tiled=True),
        lax.all_gather(grad_output, "gy", axis=1, tiled=True),
    )
    gate_rows, up_rows, down_rows = (
        lax.all_gather(w_gate, "gx", axis=0, tiled=True),
        lax.all_gather(w_up, "gx", axis=0, tiled=True),
        lax.all_gather(w_down, "gx", axis=0, tiled=True),
    )
    segment = token_block
    pair_sums = lax.psum_scatter(
        jnp.concatenate(
            [
                jnp.dot(segment, gate_rows, preferred_element_type=jnp.float32),
                jnp.dot(segment, up_rows, preferred_element_type=jnp.float32),
            ],
            axis=1,
        ).astype(jnp.bfloat16),
        "gz",
        scatter_dimension=0,
        tiled=True,
    ).astype(jnp.float32)
    gate_sum = pair_sums[:, :width_hidden]
    up_sum = pair_sums[:, width_hidden:]
    hidden = (jax.nn.silu(gate_sum) * up_sum).astype(jnp.bfloat16)
    hidden_block = lax.all_gather(hidden, "gz", axis=0, tiled=True)
    output_part = jnp.dot(hidden_block, down_rows, preferred_element_type=jnp.float32)
    output = lax.psum_scatter(
        output_part.astype(jnp.bfloat16), "gy", scatter_dimension=1, tiled=True
    )
    segment = grad_block
    grad_hidden = lax.psum_scatter(
        transposed_product(segment, down_rows).astype(jnp.bfloat16),
        "gz",
        scatter_dimension=0,
        tiled=True,
    ).astype(jnp.float32)
    grad_gate_act, grad_up_act = swiglu_grads(grad_hidden, gate_sum, up_sum)
    gate_block, up_block = (
        lax.all_gather(grad_gate_act, "gz", axis=0, tiled=True),
        lax.all_gather(grad_up_act, "gz", axis=0, tiled=True),
    )
    input_part = transposed_product(gate_block, gate_rows) + transposed_product(up_block, up_rows)
    grad_input = lax.psum_scatter(
        input_part.astype(jnp.bfloat16), "gy", scatter_dimension=1, tiled=True
    )
    columns = token_block
    pair_grads = lax.psum_scatter(
        (
            jnp.concatenate(
                [leading_product(columns, gate_block), leading_product(columns, up_block)], axis=1
            )
            * loss_scale
        ).astype(jnp.bfloat16),
        "gx",
        scatter_dimension=0,
        tiled=True,
    ).astype(jnp.float32)
    grad_gate = pair_grads[:, :width_hidden].astype(jnp.bfloat16)
    grad_up = pair_grads[:, width_hidden:].astype(jnp.bfloat16)
    columns = hidden_block
    grad_down = lax.psum_scatter(
        (leading_product(columns, grad_block) * loss_scale).astype(jnp.bfloat16),
        "gx",
        scatter_dimension=0,
        tiled=True,
    )
    return (output, grad_input, grad_gate, grad_up, grad_down)


def solution(mesh):
    placed = (
        P("gx", ("gz", "gy")),
        P(("gz", "gx"), "gy"),
        P(("gz", "gx"), "gy"),
        P(("gy", "gx"), "gz"),
        P("gx", ("gz", "gy")),
    )
    return jax.shard_map(
        on_device,
        mesh=mesh,
        in_specs=placed,
        out_specs=(
            P("gx", ("gz", "gy")),
            P("gx", ("gz", "gy")),
            P(("gz", "gx"), "gy"),
            P(("gz", "gx"), "gy"),
            P(("gy", "gx"), "gz"),
        ),
        check_vma=False,
    )
```

profile of v0, /device:TPU:0, one launch (start us, length us, event | category | flops | bytes accessed | tf_op | source)
XLA Modules:
  0.0 714.3 jit_solution(3323076860993229489)
XLA Ops:
  9.4 13.6 %all_gather.24 = bf16[256,1024]{1,0:T(8,128)(2,1)S(1)} all-gather(bf16[256,256]{1,0:T(8,128)(2,1)} %param.5), channel_id=1, replica_groups=mesh['gx'=8,'gy'=4,'gz'=4] {'gy'}, dimensions={1}, use_global_device_ids=true | all-gather | bytes 655360 | tf_op jit(solution)/shard_map/all_gather | solution.py:36
  23.0 74.5 %all-gather.9.cloned.1.call-done = bf16[1024,2816]{1,0:T(8,128)(2,1)} async-done(((bf16[128,2816]{1,0:T(8,128)(2,1)}), bf16[1024,2816]{1,0:T(8,128)(2,1)}) %all-gather.9.cloned.1.call-update) | async-done | bytes 5767184 | tf_op jit(solution)/shard_map/all_gather | solution.py:41
  97.5 4.3 convolution_convert_fusion.1
  101.8 80.5 %all-gather.7.cloned.1.call-done = bf16[1024,2816]{1,0:T(8,128)(2,1)} async-done(((bf16[128,2816]{1,0:T(8,128)(2,1)}), bf16[1024,2816]{1,0:T(8,128)(2,1)}) %all-gather.7.cloned.1.call-update) | async-done | bytes 5767184 | tf_op jit(solution)/shard_map/all_gather | solution.py:40
  182.3 4.3 convolution_convert_fusion.2
  188.4 13.1 %all_gather.29 = bf16[256,1024]{1,0:T(8,128)(2,1)S(1)} all-gather(bf16[256,256]{1,0:T(8,128)(2,1)S(1)} %copy-done.3), channel_id=1, replica_groups=mesh['gx'=8,'gy'=4,'gz'=4] {'gy'}, dimensions={1}, use_global_device_ids=true | all-gather | bytes 655360 | tf_op jit(solution)/shard_map/all_gather | solution.py:37
  201.5 65.5 %all-gather.13.cloned.1.call-done = bf16[2816,1024]{1,0:T(8,128)(2,1)} async-done(((bf16[352,1024]{1,0:T(8,128)(2,1)}), bf16[2816,1024]{1,0:T(8,128)(2,1)}) %all-gather.13.cloned.1.call-update) | async-done | bytes 5767184 | tf_op jit(solution)/shard_map/all_gather | solution.py:42
  267.1 5.4 convolution_convert_fusion
  272.6 29.2 %reduce-scatter.9.cloned.1.call-done = bf16[64,5632]{1,0:T(8,128)(2,1)} async-done(((bf16[256,5632]{1,0:T(8,128)(2,1)}), bf16[64,5632]{1,0:T(8,128)(2,1)}) %reduce-scatter.9.cloned.1.call-update) | async-done | bytes 720912 | tf_op jit(solution)/shard_map/reduce_scatter | solution.py:45
  303.0 24.9 %reduce-scatter.13.cloned.1.call-done = bf16[64,2816]{1,0:T(8,128)(2,1)} async-done(((bf16[256,2816]{1,0:T(8,128)(2,1)}), bf16[64,2816]{1,0:T(8,128)(2,1)}) %reduce-scatter.13.cloned.1.call-update) | async-done | bytes 360464 | tf_op jit(solution)/shard_map/reduce_scatter | solution.py:66
  331.9 23.1 %all-gather.17.cloned.1.call-done = bf16[256,2816]{1,0:T(8,128)(2,1)} async-done(((bf16[64,2816]{1,0:T(8,128)(2,1)}), bf16[256,2816]{1,0:T(8,128)(2,1)}) %all-gather.17.cloned.1.call-update) | async-done | bytes 1441808 | tf_op jit(solution)/shard_map/all_gather | solution.py:75
  355.0 7.4 %convolution_bitcast_fusion = f32[1024,2816]{0,1:T(8,128)} fusion(bf16[256,2816]{1,0:T(8,128)(2,1)} %all-gather.17.cloned.1.call-done, bf16[256,1024]{1,0:T(8,128)(2,1)S(1)} %all_gather.24), kind=kOutput, calls=%fused_computation.3 | convolution fusion | flops 1476395008 | bytes 13500416 | tf_op jit(solution)/shard_map/dot_general | solution.py:16
  362.3 19.5 %all-gather.15.cloned.1.call-done = bf16[256,2816]{1,0:T(8,128)(2,1)} async-done(((bf16[64,2816]{1,0:T(8,128)(2,1)}), bf16[256,2816]{1,0:T(8,128)(2,1)}) %all-gather.15.cloned.1.call-update) | async-done | bytes 1441808 | tf_op jit(solution)/shard_map/all_gather | solution.py:74
  381.8 3.2 convolution_bitcast_fusion.1
  386.6 16.4 %fusion = bf16[1024,5632]{0,1:T(8,128)(2,1)} fusion(f32[1024,2816]{0,1:T(8,128)S(1)} %copy-done, f32[1024,2816]{0,1:T(8,128)S(1)} %convolution_bitcast_fusion.1), kind=kLoop, calls=%fused_computation.1 | loop fusion | flops 17301504 | bytes 34603008 | tf_op jit(solution)/shard_map/convert_element_type | solution.py:88
  403.0 15.6 %copy.14 = bf16[1024,5632]{1,0:T(8,128)(2,1)} copy(bf16[1024,5632]{0,1:T(8,128)(2,1)} %fusion) | data formatting | bytes 23068672
  419.9 4.3 fusion.8
  424.2 5.1 fusion.1
  429.5 5.7 convolution_convert_fusion.3
  435.3 4.2 multiply_convert_fusion
  439.5 122.7 %reduce-scatter.19.cloned.1.call-done = bf16[128,5632]{1,0:T(8,128)(2,1)} async-done(((bf16[1024,5632]{1,0:T(8,128)(2,1)}), bf16[128,5632]{1,0:T(8,128)(2,1)}) %reduce-scatter.19.cloned.1.call-update) | async-done | bytes 1441808
  564.7 19.5 %reduce-scatter.15.cloned.1.call-done = bf16[256,256]{1,0:T(8,128)(2,1)} async-done(((bf16[256,1024]{1,0:T(8,128)(2,1)}), bf16[256,256]{1,0:T(8,128)(2,1)}) %reduce-scatter.15.cloned.1.call-update) | async-done | bytes 131088 | tf_op jit(solution)/shard_map/reduce_scatter | solution.py:78
  584.3 24.2 %reduce-scatter.11.cloned.1.call-done = bf16[256,256]{1,0:T(8,128)(2,1)} async-done(((bf16[256,1024]{1,0:T(8,128)(2,1)}), bf16[256,256]{1,0:T(8,128)(2,1)}) %reduce-scatter.11.cloned.1.call-update) | async-done | bytes 131088 | tf_op jit(solution)/shard_map/reduce_scatter | solution.py:62
  608.4 99.0 %reduce-scatter.17.cloned.1.call-done = bf16[352,1024]{1,0:T(8,128)(2,1)} async-done(((bf16[2816,1024]{1,0:T(8,128)(2,1)}), bf16[352,1024]{1,0:T(8,128)(2,1)}) %reduce-scatter.17.cloned.1.call-update) | async-done | bytes 720912 | tf_op jit(solution)/shard_map/reduce_scatter | solution.py:96
  (39 shorter events, 14.8 us)
Async XLA Ops:
  7.2 90.3 %all-gather.9.cloned.1.call-start = ((), (), s32[]{:S(2)}) async-start(), calls=%async_computation.7 | async-start | bytes 6488064 | tf_op jit(solution)/shard_map/all_gather | solution.py:41
  7.9 174.4 %all-gather.7.cloned.1.call-start = ((), (), s32[]{:S(2)}) async-start(), calls=%async_computation.6 | async-start | bytes 6488064 | tf_op jit(solution)/shard_map/all_gather | solution.py:40
  8.6 258.4 %all-gather.13.cloned.1.call-start = ((), (), s32[]{:S(2)}) async-start(), calls=%async_computation.10 | async-start | bytes 6488064 | tf_op jit(solution)/shard_map/all_gather | solution.py:42
  9.4 292.4 %reduce-scatter.9.cloned.1.call-start = ((), (), s32[]{:S(2)}) async-start(), calls=%async_computation.8 | async-start | bytes 3604480 | tf_op jit(solution)/shard_map/reduce_scatter | solution.py:45
  186.6 1.8 copy-start.3
  188.4 139.5 %reduce-scatter.13.cloned.1.call-start = ((), (), s32[]{:S(2)}) async-start(), calls=%async_computation.12 | async-start | bytes 1802240 | tf_op jit(solution)/shard_map/reduce_scatter | solution.py:66
  272.5 82.4 %all-gather.17.cloned.1.call-start = ((), (), s32[]{:S(2)}) async-start(), calls=%async_computation.14 | async-start | bytes 1802240 | tf_op jit(solution)/shard_map/all_gather | solution.py:75
  330.2 51.7 %all-gather.15.cloned.1.call-start = ((), (), s32[]{:S(2)}) async-start(), calls=%async_computation.13 | async-start | bytes 1802240 | tf_op jit(solution)/shard_map/all_gather | solution.py:74
  330.9 98.6 %all-gather.11.cloned.1.call-start = ((), (), s32[]{:S(2)}) async-start(), calls=%async_computation.9 | async-start | bytes 1802240 | tf_op jit(solution)/shard_map/all_gather | solution.py:60
  331.7 230.6 %reduce-scatter.19.cloned.1.call-start = ((), (), s32[]{:S(2)}) async-start(), calls=%async_computation.17 | async-start | bytes 12976128
  381.8 4.7 copy-start
  418.6 1.4 copy-start.2
  418.6 5.7 copy-start.1
  418.6 165.7 %reduce-scatter.15.cloned.1.call-start = ((), (), s32[]{:S(2)}) async-start(), calls=%async_computation.15 | async-start | bytes 655360 | tf_op jit(solution)/shard_map/reduce_scatter | solution.py:78
  429.4 179.0 %reduce-scatter.11.cloned.1.call-start = ((), (), s32[]{:S(2)}) async-start(), calls=%async_computation.11 | async-start | bytes 655360 | tf_op jit(solution)/shard_map/reduce_scatter | solution.py:62
  429.5 5.8 copy-start.4
  435.3 272.2 %reduce-scatter.17.cloned.1.call-start = ((), (), s32[]{:S(2)}) async-start(), calls=%async_computation.16 | async-start | bytes 6488064 | tf_op jit(solution)/shard_map/reduce_scatter | solution.py:96
Sparse Core Ops, SparseCore 0:
  10.3 87.1 all-gather.8
  99.8 82.4 all-gather.6
  184.6 82.4 all-gather.12
  269.3 32.3 reduce-scatter.8
  304.0 23.7 reduce-scatter.12
  330.3 24.6 all-gather.16
  357.2 24.6 all-gather.14
  384.1 24.6 all-gather.10
  418.7 143.4 reduce-scatter.18
  565.0 19.2 reduce-scatter.14
  587.2 21.1 reduce-scatter.10
  612.8 94.6 reduce-scatter.16
where the time goes:
time: 715 us; the launch traced here: 714 us
  waiting for transfers between devices  586 us (82%)
  matrix products  43.9 us (6%)
  blocking collectives  26.7 us (4%)
  other arithmetic  21.7 us (3%)
  local copies, waits for them, and re-layouts  20.9 us (3%)
  between operations  14.3 us (2%)
    unnamed x13, waiting for transfers between devices  126 us
    reduce_scatter x1, waiting for transfers between devices, on_device(): lax.psum_scatter((leading_product(columns, grad_block) * loss_scale).asty...  99 us
    all_gather x1, waiting for transfers between devices, on_device(): lax.all_gather(w_gate, 'gx', axis=0, tiled=True)  80.5 us
    all_gather x1, waiting for transfers between devices, on_device(): lax.all_gather(w_up, 'gx', axis=0, tiled=True)  74.5 us
    all_gather x1, waiting for transfers between devices, on_device(): lax.all_gather(w_down, 'gx', axis=0, tiled=True)  65.5 us
    reduce_scatter x1, waiting for transfers between devices, on_device(): lax.psum_scatter(jnp.concatenate([jnp.dot(segment, gate_rows, preferred_e...  29.2 us
    reduce_scatter x1, waiting for transfers between devices, on_device(): lax.psum_scatter(transposed_product(segment, down_rows).astype(jnp.bfloat...  24.9 us
    reduce_scatter x1, waiting for transfers between devices, on_device(): lax.psum_scatter(output_part.astype(jnp.bfloat16), 'gy', scatter_dimensio...  24.2 us
  transfers between devices with their start and end apart: 12, of which 11 were waited for; matrix products, arithmetic and copies ran while one was open for 11% of the time, Pallas kernels for 0%

commit v1 on v0

v1 whole, which is shorter than its diff:
```python
import functools
import math

import jax
import jax.numpy as jnp
from jax import lax
from jax.experimental import pallas as pl
from jax.experimental.pallas import tpu as pltpu
from jax.sharding import PartitionSpec as P


BF16 = jnp.bfloat16
F32 = jnp.float32
LANES = 128


def shift_z(array, steps):
    return lax.ppermute(
        array, "gx", [(i, ((i // 2 + steps) % 4) * 2 + i % 2) for i in range(8)]
    )


def shift_y(array, steps):
    return lax.ppermute(array, "gy", [(i, (i + steps) % 4) for i in range(4)])


def swap_x_hi(array):
    return lax.ppermute(array, "gx", [(i, i ^ 1) for i in range(8)])


def swap_x_lo(array):
    return lax.ppermute(array, "gz", [(i, i ^ 2) for i in range(4)])


def swap_x(array):
    return lax.ppermute(array, ("gx", "gz"), [(i, i ^ 6) for i in range(32)])


def swap_core(array):
    return lax.ppermute(array, "gz", [(i, i ^ 1) for i in range(4)])


def add(left_side, right_side):
    return left_side.astype(F32) + right_side.astype(F32)


def dot(left_side, right_side, left_dim, right_dim):
    return lax.dot_general(
        left_side,
        right_side,
        (((left_dim,), (right_dim,)), ((), ())),
        preferred_element_type=F32,
    )


class Operand:
    def __init__(self, source, held, semaphore):
        self.copy = pltpu.make_async_copy(source, held, semaphore)
        self.copy.start()
        self.held = held
        self.shape = held.shape

    def ready(self):
        if self.copy is not None:
            self.copy.wait()
            self.copy = None
        return self.held

    def __getitem__(self, index):
        return self.ready()[index]


def local_call(kernel, out_shapes, operands, scratch_shapes=(), vmem=40):
    count, outs = len(operands), len(out_shapes)

    def body(*refs):
        sources, refs = refs[:count], refs[count:]
        results, refs = refs[:outs], refs[outs:]
        held, semaphores, scratch = refs[:count], refs[count], refs[count + 1 :]
        inputs = [
            Operand(source, place, semaphores.at[i])
            for i, (source, place) in enumerate(zip(sources, held))
        ]
        kernel(*inputs, *results, *scratch)
        for operand in inputs:
            operand.ready()

    return list(
        pl.pallas_call(
            body,
            out_shape=[jax.ShapeDtypeStruct(shape, BF16) for shape in out_shapes],
            in_specs=[pl.BlockSpec(memory_space=pl.ANY)] * count,
            out_specs=[pl.BlockSpec(memory_space=pltpu.VMEM)] * outs,
            scratch_shapes=[
                *(pltpu.VMEM(array.shape, BF16) for array in operands),
                pltpu.SemaphoreType.DMA((count,)),
                *scratch_shapes,
            ],
            compiler_params=pltpu.CompilerParams(vmem_limit_bytes=vmem * 2**20),
        )(*operands)
    )


def assembled_call(kernel, out_shapes, operands, buffers, copies, vmem=40):
    count, outs = len(operands), len(out_shapes)

    def body(*refs):
        sources, refs = refs[:count], refs[count:]
        results, (*held, semaphores) = refs[:outs], refs[outs:]
        started = []

        def copy(source, target):
            started.append(pltpu.make_async_copy(source, target, semaphores.at[len(started)]))
            started[-1].start()
            return started[-1]

        kernel(copy, sources, results, *held)

    return list(
        pl.pallas_call(
            body,
            out_shape=[jax.ShapeDtypeStruct(shape, BF16) for shape in out_shapes],
            in_specs=[pl.BlockSpec(memory_space=pl.ANY)] * count,
            out_specs=[pl.BlockSpec(memory_space=pltpu.VMEM)] * outs,
            scratch_shapes=[
                *(pltpu.VMEM(shape, BF16) for shape in buffers),
                pltpu.SemaphoreType.DMA((copies,)),
            ],
            compiler_params=pltpu.CompilerParams(vmem_limit_bytes=vmem * 2**20),
        )(*operands)
    )


def wait_all(copies):
    for copy in copies:
        copy.wait()


def after(array, *earlier):
    return lax.optimization_barrier((array, *earlier))[0]


def core_index():
    return lax.rem(lax.axis_index("gz"), 2)


def x_lo_index():
    return lax.div(lax.axis_index("gz"), 2)


def block(index, count):
    return pl.ds(pl.multiple_of(index * count, count), count)


def feature_block(k, count):
    return block(lax.rem(lax.axis_index("gy") + (4 - k), 4), count)


def split_rows(tokens, grads, mine, theirs):
    half, count = mine.shape[0], tokens.shape[1]
    for out, index in ((mine, x_lo_index()), (theirs, 1 - x_lo_index())):
        out[:, :count] = tokens[block(index, half)]
        out[:, count:] = grads[block(index, half)]


def arrange_rows(near, far, near_x, far_x, tokens, grads):
    half, count = near.shape[0], near.shape[1] // 2
    core = core_index()
    for index, left, right in ((core, near, far), (1 - core, near_x, far_x)):
        tokens[block(index, half), :count] = left[:, :count]
        tokens[block(index, half), count:] = right[:, :count]
        grads[block(index, half), :count] = left[:, count:]
        grads[block(index, half), count:] = right[:, count:]


def split_pair(w_gate, w_up, out):
    groups, own = out.shape[0], out.shape[1] // 2
    for first, array in ((0, w_gate), (own, w_up)):
        for g in range(groups):
            out[g, first : first + own] = array[:, g * own : (g + 1) * own].T


def join_blocks(pieces, out):
    groups, own, _ = pieces.shape
    for g in range(groups):
        out[:, g * own : (g + 1) * own] = pieces[g].T


def join_features(*refs):
    *blocks, out = refs
    count, features = blocks[0].shape[1] // 2, out.shape[1] // 2
    for k, part in enumerate(blocks):
        place = lax.rem(lax.axis_index("gy") + (4 - k), 4) * count
        out[:, pl.ds(pl.multiple_of(place, count), count)] = part[:, :count]
        out[:, pl.ds(pl.multiple_of(features + place, count), count)] = part[:, count:]


def pick_features(whole, *outs):
    count, features = outs[0].shape[1] // 2, whole.shape[1] // 2
    for k, out in enumerate(outs):
        place = lax.rem(lax.axis_index("gy") + (4 - k), 4) * count
        out[:, :count] = whole[:, pl.ds(pl.multiple_of(place, count), count)]
        out[:, count:] = whole[:, pl.ds(pl.multiple_of(features + place, count), count)]


def own_place(k, count):
    return lax.rem(lax.axis_index("gy") + (4 - k), 4) * count


def copy_tokens(copy, refs, held):
    copies, first = [], 0
    for ref in refs:
        copies.append(copy(ref, held.at[pl.ds(first, ref.shape[0])]))
        first += ref.shape[0]
    return copies


def copy_grads(copy, refs, held):
    copies = []
    count, features = refs[0].shape[1] // 2, held.shape[1] // 2
    for ref, k, first in zip(refs, (0, 1, 2, 2, 3), (0, 0, 0, refs[2].shape[0], 0)):
        for side in (0, 1):
            place = side * features + own_place(k, count)
            target = held.at[
                pl.ds(first, ref.shape[0]), pl.ds(pl.multiple_of(place, count), count)
            ]
            copies.append(copy(ref.at[:, pl.ds(side * count, count)], target))
    return copies


def copy_pair(copy, near, far, held):
    copies = []
    groups, _, count = near.shape
    for side, ref in enumerate((near, far)):
        for g in range(groups):
            target = held.at[:, pl.ds((side * groups + g) * count, count)]
            copies.append(copy(ref.at[g], target))
    return copies


def copy_down(copy, near, far, held):
    features = near.shape[1]
    return [
        copy(ref, held.at[:, pl.ds(side * features, features)])
        for side, ref in enumerate((near, far))
    ]


def copy_part(copy, mine, other, first, held):
    rows, width = mine.shape[1], held.shape[1]
    return [
        copy(
            ref.at[i, :, pl.ds(first, width)], held.at[pl.ds((2 * i + side) * rows, rows)]
        )
        for i in range(mine.shape[0])
        for side, ref in enumerate((mine, other))
    ]


def sums_products(copy, sources, results, tokens, grads, pair, down):
    keep, send = results
    half, width = keep.shape[1], keep.shape[2] // 3
    own = down.shape[0]
    copies = copy_tokens(copy, sources[:5], tokens)
    copies += copy_pair(copy, *sources[10:12], pair)
    later = copy_grads(copy, sources[5:10], grads) + copy_down(copy, *sources[12:], down)
    padding = jnp.zeros((half, width - own), BF16)
    wait_all(copies)
    for step, (left, right) in enumerate(((tokens, pair), (grads, down))):
        if step == 1:
            wait_all(later)
        for i in (0, 2):
            part = dot(left[pl.ds(2 * i * half, 4 * half)], right[...], 1, 1).astype(BF16)
            for j in (0, 1):
                for out, at in ((keep, 2 * j * half), (send, (2 * j + 1) * half)):
                    rows = part[at : at + half]
                    for k in (0, 1) if step == 0 else (2,):
                        first = k * own if step == 0 else 0
                        out[i + j, :, k * width : k * width + own] = rows[:, first : first + own]
                        out[i + j, :, k * width + own : (k + 1) * width] = padding


def activate(keep, got, out):
    width = out.shape[2] // 3
    for i in range(out.shape[0]):
        gate_sum, up_sum, grad_hidden = (
            add(keep[i, :, k * width : (k + 1) * width], got[i, :, k * width : (k + 1) * width])
            for k in range(3)
        )
        sigmoid_gate = jax.nn.sigmoid(gate_sum)
        out[i, :, :width] = (gate_sum * sigmoid_gate * up_sum).astype(BF16)
        out[i, :, width : 2 * width] = (
            grad_hidden * up_sum * sigmoid_gate * (1.0 + gate_sum * (1.0 - sigmoid_gate))
        ).astype(BF16)
        out[i, :, 2 * width :] = (grad_hidden * gate_sum * sigmoid_gate).astype(BF16)


def output_products(copy, sources, results, hidden, down):
    copies = copy_part(copy, sources[0], sources[1], 0, hidden)
    wait_all(copies + copy_down(copy, *sources[2:], down))
    own, first = down.shape[0], 0
    for out in results:
        rows = out.shape[0]
        out[...] = dot(hidden[pl.ds(first, rows), :own], down[...], 1, 0).astype(BF16)
        first += rows


def input_products(copy, sources, results, acts, pair):
    width, own = acts.shape[1] // 2, pair.shape[0] // 2
    copies = copy_part(copy, sources[0], sources[1], width, acts)
    wait_all(copies + copy_pair(copy, *sources[2:], pair))
    count, features = results[0].shape[1] // 2, pair.shape[1] // 2
    for out, k, first in zip(results, (0, 1, 2, 2, 3), (0, 0, 0, results[2].shape[0], 0)):
        rows = pl.ds(first, out.shape[0])
        for side in (0, 1):
            place = pl.ds(pl.multiple_of(side * features + own_place(k, count), count), count)
            part = dot(acts[rows, :own], pair[:own, place], 1, 0)
            part += dot(acts[rows, width : width + own], pair[own:, place], 1, 0)
            out[:, side * count : (side + 1) * count] = part.astype(BF16)


def pair_gradients(scale, part, copy, sources, results, tokens, acts):
    width = acts.shape[1]
    copies = copy_tokens(copy, sources[:5], tokens)
    wait_all(copies + copy_part(copy, *sources[5:], part * width, acts))
    near, far = results
    groups, own, count = near.shape
    features = groups * count
    for out, first in ((far, features), (near, 0)):
        total = dot(acts[:, :own], tokens[:, pl.ds(first, features)], 0, 0) * scale
        for g in range(groups):
            out[g] = total[:, g * count : (g + 1) * count].astype(BF16)


def down_gradients(scale, copy, sources, results, grads, hidden):
    copies = copy_grads(copy, sources[:5], grads)
    wait_all(copies + copy_part(copy, *sources[5:], 0, hidden))
    near, far = results
    own, features = near.shape
    for out, first in ((far, features), (near, 0)):
        total = dot(hidden[:, :own], grads[:, pl.ds(first, features)], 0, 0)
        out[...] = (total * scale).astype(BF16)


def split_result(output, grad_input, near, far, near_x, far_x):
    half, count = near.shape[0], near.shape[1] // 2
    core = core_index()
    for index, left, right in ((core, near, far), (1 - core, near_x, far_x)):
        for first, array in ((0, output), (count, grad_input)):
            rows = array[block(index, half)]
            left[:, first : first + count] = rows[:, :count]
            right[:, first : first + count] = rows[:, count:]


def join_result(mine, theirs, output, grad_input):
    half, count = mine.shape[0], mine.shape[1] // 2
    for rows, index in ((mine, x_lo_index()), (theirs, 1 - x_lo_index())):
        output[block(index, half)] = rows[:, :count]
        grad_input[block(index, half)] = rows[:, count:]


def ring_gather(shift, array):
    half = array.shape[0] // 2
    before, after = shift(array, 1), shift(array, -1)
    return [array, before, shift(before[:half], 1), shift(after[half:], -1), after]


def ring_scatter(shift, own, before, low, high, after):
    half = low.shape[0]
    from_before, from_after = shift(low, 1), shift(high, -1)
    after = lax.dynamic_update_slice(after, add(after[:half], from_before).astype(BF16), (0, 0))
    before = lax.dynamic_update_slice(
        before, add(before[half:], from_after).astype(BF16), (half, 0)
    )
    return own.astype(F32) + shift(after, 1).astype(F32) + shift(before, -1).astype(F32)


def direct_gather(shift, array):
    return [array, shift(array, 1), shift(array, 2), shift(array, -1)]


def direct_scatter(shift, own, before, opposite, after):
    return (
        own.astype(F32)
        + shift(after, 1).astype(F32)
        + shift(before, -1).astype(F32)
        + shift(opposite, 2).astype(F32)
    )


def on_device(tokens, w_gate, w_up, w_down, grad_output):
    tok_rows, tok_columns = tokens.shape
    rows_in, width_hidden = w_gate.shape
    own = width_hidden // 8
    width = -(-own // LANES) * LANES
    features = 8 * rows_in
    loss_scale = 1.0 / math.sqrt(tok_rows * 8)
    rows, columns = tok_rows // 2, 2 * tok_columns

    mine, theirs = local_call(split_rows, [(rows, columns)] * 2, [tokens, grad_output])
    four = [mine, swap_x_lo(theirs), swap_x_hi(mine), swap_x(theirs)]
    t_block, g_block = local_call(arrange_rows, [(2 * rows, columns)] * 2, four)

    (pieces,) = local_call(split_pair, [(8, 2 * own, rows_in)], [w_gate, w_up])
    pieces, w_down = lax.optimization_barrier((pieces, w_down, *four))[:2]
    w_near = lax.all_to_all(pieces, "gx", 0, 0, tiled=True)
    d_near, d_far = w_down, swap_x_lo(w_down)
    w_far = swap_x_lo(after(w_near, d_far))

    (t_own,) = local_call(
        join_features, [(2 * rows, 2 * features)], direct_gather(shift_y, t_block)
    )
    g_own = jnp.concatenate(direct_gather(shift_z, g_block), axis=0)
    t_own, g_own = lax.optimization_barrier((t_own, g_own))
    t_all = ring_gather(shift_z, t_own)
    g_all = ring_gather(shift_y, g_own)

    all_tokens, all_features = 8 * rows, 2 * features
    whole = (all_tokens, all_features)
    keep, send = assembled_call(
        sums_products,
        [(4, rows, 3 * width)] * 2,
        [*t_all, *g_all, w_near, w_far, d_near, d_far],
        [whole, whole, (2 * own, all_features), (own, all_features)],
        33,
    )
    (mine,) = local_call(activate, [(4, rows, 3 * width)], [keep, swap_core(send)])
    both = [mine, swap_core(mine)]

    grad_pair = []
    for part in (1, 2):
        near, far = assembled_call(
            functools.partial(pair_gradients, loss_scale, part),
            [(8, own, rows_in)] * 2,
            [*t_all, *both],
            [whole, (all_tokens, width)],
            13,
        )
        total = add(near, swap_x_lo(far)).astype(BF16)
        total = lax.all_to_all(total, "gx", 0, 0, tiled=True)
        grad_pair += local_call(join_blocks, [(rows_in, width_hidden)], [total])
        if part == 1:
            both[1] = after(both[1], near)
    near, far = assembled_call(
        functools.partial(down_gradients, loss_scale),
        [(own, features)] * 2,
        [*g_all, *both],
        [whole, (all_tokens, width)],
        18,
    )
    grad_down = add(near, swap_x_lo(far)).astype(BF16)

    shape, half_shape = (2 * rows, all_features), (rows, all_features)
    parts = assembled_call(
        output_products,
        [shape, shape, half_shape, half_shape, shape],
        [*both, d_near, d_far],
        [(all_tokens, width), (own, all_features)],
        10,
    )
    output = ring_scatter(shift_z, *parts).astype(BF16)
    shape, half_shape = (all_tokens, columns), (all_tokens // 2, columns)
    parts = assembled_call(
        input_products,
        [shape, shape, half_shape, half_shape, shape],
        [*both, w_near, w_far],
        [(all_tokens, 2 * width), (2 * own, all_features)],
        24,
    )
    grad_input = ring_scatter(shift_y, *parts).astype(BF16)
    parts = local_call(pick_features, [(2 * rows, columns)] * 4, [output])
    output = direct_scatter(shift_y, *parts).astype(BF16)
    parts = [grad_input[2 * k * rows : 2 * (k + 1) * rows] for k in range(4)]
    grad_input = direct_scatter(shift_z, *parts).astype(BF16)
    near, far, near_x, far_x = local_call(
        split_result, [(rows, columns)] * 4, [output, grad_input]
    )
    mine = add(near, swap_x_hi(near_x)).astype(BF16)
    theirs = add(swap_x_lo(far), swap_x(far_x)).astype(BF16)
    output, grad_input = local_call(join_result, [tokens.shape] * 2, [mine, theirs])
    return (output, grad_input, *grad_pair, grad_down)


def solution(mesh):
    placed = (
        P("gx", ("gz", "gy")),
        P(("gz", "gx"), "gy"),
        P(("gz", "gx"), "gy"),
        P(("gy", "gx"), "gz"),
        P("gx", ("gz", "gy")),
    )
    return jax.shard_map(
        on_device,
        mesh=mesh,
        in_specs=placed,
        out_specs=(
            P("gx", ("gz", "gy")),
            P("gx", ("gz", "gy")),
            P(("gz", "gx"), "gy"),
            P(("gz", "gx"), "gy"),
            P(("gy", "gx"), "gz"),
        ),
        check_vma=False,
    )
```

time: 715 us -> 239 us (0.33)
  waiting for transfers between devices: 586 us -> 79.9 us
  starting transfers between devices: 0.66 us -> 84.1 us
  matrix products: 43.9 us -> 0 us
  Pallas kernels: 0 us -> 40.1 us
  blocking collectives: 26.7 us -> 0 us
  between operations: 14.3 us -> 1.2 us
  local copies, waits for them, and re-layouts: 20.9 us -> 12.8 us
    all_gather x6 -> x0, waiting for transfers between devices: 263 us -> none  [the longest x1 80.5 us: on_device(): lax.all_gather(w_gate, 'gx', axis=0, tiled=True)]
    reduce_scatter x5 -> x0, waiting for transfers between devices: 197 us -> none  [the longest x1 99 us: on_device(): lax.psum_scatter((leading_product(columns, grad_block) * loss_scale).asty...]
    unnamed x13 -> x0, waiting for transfers between devices: 126 us -> none
    ppermute x0 -> x41, waiting for transfers between devices: none -> 78.4 us  [the longest x14 30.4 us: shift_y(): return lax.ppermute(array, 'gy', [(i, (i + steps) % 4) for i in range(4)])]
    ppermute x0 -> x41, starting transfers between devices: none -> 59.7 us  [the longest x14 22 us: shift_y(): return lax.ppermute(array, 'gy', [(i, (i + steps) % 4) for i in range(4)])]
    dot_general x9 -> x0, matrix products: 43.9 us -> none  [the longest x3 14.9 us: transposed_product(): lax.dot_general(left_side, right_side, (((1,), (1,)), ((), ())), preferre...]
    pallas_call x0 -> x16, Pallas kernels: none -> 40.1 us  [the longest x6 29.6 us: assembled_call(): pl.pallas_call(body, out_shape=[jax.ShapeDtypeStruct(shape, BF16) for sha...]
    all_gather x2 -> x0, blocking collectives: 26.7 us -> none  [the longest x1 13.6 us: on_device(): lax.all_gather(tokens, 'gy', axis=1, tiled=True)]
  transfers between devices with their start and end apart: 12 -> 44, of which waited for: 11 -> 18; matrix products, arithmetic and copies ran while one was open for 11% -> 10% of each run, Pallas kernels for 0% -> 8%
where the time goes in v1:
time: 239 us; the launch traced here: 238 us
  starting transfers between devices  84.1 us (35%)
  waiting for transfers between devices  79.9 us (33%)
  Pallas kernels  40.1 us (17%)
  other arithmetic  19.9 us (8%)
  local copies, waits for them, and re-layouts  12.8 us (5%)
    ppermute x14, waiting for transfers between devices, shift_y(): return lax.ppermute(array, 'gy', [(i, (i + steps) % 4) for i in range(4)])  30.4 us
    pallas_call x6, Pallas kernels, assembled_call(): pl.pallas_call(body, out_shape=[jax.ShapeDtypeStruct(shape, BF16) for sha...  29.6 us
    ppermute x14, waiting for transfers between devices, shift_z(): lax.ppermute(array, 'gx', [(i, (i // 2 + steps) % 4 * 2 + i % 2) for i in...  28.6 us
    ppermute x14, starting transfers between devices, shift_y(): return lax.ppermute(array, 'gy', [(i, (i + steps) % 4) for i in range(4)])  22 us
    ppermute x14, starting transfers between devices, shift_z(): lax.ppermute(array, 'gx', [(i, (i // 2 + steps) % 4 * 2 + i % 2) for i in...  20.6 us
    all_to_all x2, starting transfers between devices, on_device(): total = lax.all_to_all(total, 'gx', 0, 0, tiled=True)  17.7 us
    ppermute x7, waiting for transfers between devices, swap_x_lo(): return lax.ppermute(array, 'gz', [(i, i ^ 2) for i in range(4)])  12.2 us
    pallas_call x10, Pallas kernels, local_call(): pl.pallas_call(body, out_shape=[jax.ShapeDtypeStruct(shape, BF16) for sha...  10.4 us
  transfers between devices with their start and end apart: 44, of which 18 were waited for; matrix products, arithmetic and copies ran while one was open for 10% of the time, Pallas kernels for 8%

profile of v1, /device:TPU:0, one launch (start us, length us, event | category | flops | bytes accessed | tf_op | source)
XLA Modules:
  0.0 238.0 jit_solution(1153475111412471582)
XLA Ops:
  9.8 3.2 %shard_map.95 = bf16[8,704,128]{2,1,0:T(8,128)(2,1)} custom-call(bf16[128,2816]{1,0:T(8,128)(2,1)S(1)} %copy-done.8, bf16[128,2816]{1,0:T(8,128)(2,1)S(1)} %copy-done.9), custom_call_target="tpu_custom_call" | custom-call | tf_op jit(solution)/shard_map/pallas_call | solution.py:89
  13.3 6.7 %all-to-all-start = ((bf16[8,704,128]{2,1,0:T(8,128)(2,1)}), bf16[8,704,128]{2,1,0:T(8,128)(2,1)S(1)}, u32[]{:S(2)}, u32[]{:S(2)}) async-start(bf16[8,704,128]{2,1,0:T(8,128)(2,1)} %shard_map.95), calls=%async_computation | async-start | bytes 2883584 | tf_op jit(solution)/shard_map/all_to_all | solution.py:406
  27.2 3.2 %collective-permute-start.8 = (bf16[256,512]{1,0:T(8,128)(2,1)S(1)}, bf16[256,512]{1,0:T(8,128)(2,1)S(1)}, u32[]{:S(2)}, u32[]{:S(2)}) collective-permute-start(bf16[256,512]{1,0:T(8,128)(2,1)S(1)} %get-tuple-element.46), channel_id=1, source_target_pairs={{0,96},{16,112},{32,0},{48,16},{64,32},{80,48},{96,64},{112,80},{1... | collective-permute-start | bytes 786440 | tf_op jit(solution)/shard_map/ppermute | solution.py:18
  30.4 3.2 %collective-permute-done.5.refs_3_ = bf16[256,512]{1,0:T(8,128)(2,1)S(1)} collective-permute-done((bf16[256,512]{1,0:T(8,128)(2,1)S(1)}, bf16[256,512]{1,0:T(8,128)(2,1)S(1)}, u32[]{:S(2)}, u32[]{:S(2)}) %collective-permute-start.5) | collective-permute-done | bytes 262176 | tf_op jit(solution)/shard_map/ppermute | solution.py:24
  33.7 3.2 %collective-permute-start.7 = (bf16[256,512]{1,0:T(8,128)(2,1)S(1)}, bf16[256,512]{1,0:T(8,128)(2,1)S(1)}, u32[]{:S(2)}, u32[]{:S(2)}) collective-permute-start(bf16[256,512]{1,0:T(8,128)(2,1)S(1)} %get-tuple-element.46), channel_id=1, source_target_pairs={{0,64},{16,80},{32,96},{48,112},{64,0},{80,16},{96,32},{112,48},{1... | collective-permute-start | bytes 786440 | tf_op jit(solution)/shard_map/ppermute | solution.py:18
  37.8 7.2 %collective-permute-done.8 = bf16[256,512]{1,0:T(8,128)(2,1)S(1)} collective-permute-done((bf16[256,512]{1,0:T(8,128)(2,1)S(1)}, bf16[256,512]{1,0:T(8,128)(2,1)S(1)}, u32[]{:S(2)}, u32[]{:S(2)}) %collective-permute-start.8) | collective-permute-done | bytes 262176 | tf_op jit(solution)/shard_map/ppermute | solution.py:18
  58.2 17.6 %collective-permute-done.15.refs_9_.refs_4_ = bf16[1024,512]{1,0:T(8,128)(2,1)} collective-permute-done((bf16[1024,512]{1,0:T(8,128)(2,1)}, bf16[1024,512]{1,0:T(8,128)(2,1)}, u32[]{:S(2)}, u32[]{:S(2)}) %collective-permute-start.15) | collective-permute-done | bytes 1048608 | tf_op jit(solution)/shard_map/ppermute | solution.py:24
  76.9 3.5 %collective-permute-start.16 = (bf16[512,512]{1,0:T(8,128)(2,1)S(1)}, bf16[512,512]{1,0:T(8,128)(2,1)S(1)}, u32[]{:S(2)}, u32[]{:S(2)}) collective-permute-start(bf16[512,512]{1,0:T(8,128)(2,1)S(1)} %slice.51), channel_id=1, source_target_pairs={{0,12},{4,0},{8,4},{12,8},{1,13},{5,1},{9,5},{13,9},{2,14},{6,2},{... | collective-permute-start | bytes 1572872 | tf_op jit(solution)/shard_map/ppermute | solution.py:24
  85.1 4.9 %collective-permute-done.16.refs_8_.refs_3_ = bf16[512,512]{1,0:T(8,128)(2,1)S(1)} collective-permute-done((bf16[512,512]{1,0:T(8,128)(2,1)S(1)}, bf16[512,512]{1,0:T(8,128)(2,1)S(1)}, u32[]{:S(2)}, u32[]{:S(2)}) %collective-permute-start.16) | collective-permute-done | bytes 524320 | tf_op jit(solution)/shard_map/ppermute | solution.py:24
  90.0 4.6 %collective-permute-done.14.refs_7_.refs_2_ = bf16[512,512]{1,0:T(8,128)(2,1)S(1)} collective-permute-done((bf16[512,512]{1,0:T(8,128)(2,1)S(1)}, bf16[512,512]{1,0:T(8,128)(2,1)S(1)}, u32[]{:S(2)}, u32[]{:S(2)}) %collective-permute-start.14) | collective-permute-done | bytes 524320 | tf_op jit(solution)/shard_map/ppermute | solution.py:24
  97.2 8.2 %shard_map.96 = (bf16[4,128,1152]{2,1,0:T(8,128)(2,1)S(1)}, bf16[4,128,1152]{2,1,0:T(8,128)(2,1)S(1)}) custom-call(bf16[256,2048]{1,0:T(8,128)(2,1)S(1)} %shard_map.94.refs_0_, bf16[256,2048]{1,0:T(8,128)(2,1)} %collective-permute-done.9.refs_1_, bf16[128,2048]{1,0:T(8,128)(2,1)S(1)} %collective-permute-done.10.refs_2_, ...), custom_call_target="tpu_custom_call" | custom-call | tf_op jit(solution)/shard_map/pallas_call | solution.py:120
  117.2 6.8 %shard_map.101 = (bf16[1024,512]{1,0:T(8,128)(2,1)S(1)}, bf16[1024,512]{1,0:T(8,128)(2,1)}, bf16[512,512]{1,0:T(8,128)(2,1)S(1)}, bf16[512,512]{1,0:T(8,128)(2,1)S(1)}, bf16[1024,512]{1,0:T(8,128)(2,1)}) custom-call(bf16[4,128,1152]{2,1,0:T(8,128)(2,1)S(1)} %shard_map.97.refs_5_.refs_0_, bf16[4,128,1152]{2,1,0:T(8,128)(2,1)S(1)} %collective-permute-done.20.refs_6_.refs_1_, ...), custom_call_target="tpu_custom_call" | custom-call | tf_op jit(solution)/shard_map/pallas_call | solution.py:120
  132.9 4.6 %shard_map.99 = (bf16[256,2048]{1,0:T(8,128)(2,1)S(1)}, bf16[256,2048]{1,0:T(8,128)(2,1)}, bf16[128,2048]{1,0:T(8,128)(2,1)S(1)}, bf16[128,2048]{1,0:T(8,128)(2,1)S(1)}, bf16[256,2048]{1,0:T(8,128)(2,1)}) custom-call(bf16[4,128,1152]{2,1,0:T(8,128)(2,1)S(1)} %shard_map.97.refs_5_.refs_0_, bf16[4,128,1152]{2,1,0:T(8,128)(2,1)S(1)} %collective-permute-done.20.refs_6_.refs_1_, ...), custom_call_target="tpu_custom_call" | custom-call | tf_op jit(solution)/shard_map/pallas_call | solution.py:120
  142.8 3.2 %collective-permute-start.31 = (bf16[1024,512]{1,0:T(8,128)(2,1)}, bf16[1024,512]{1,0:T(8,128)(2,1)}, u32[]{:S(2)}, u32[]{:S(2)}) collective-permute-start(bf16[1024,512]{1,0:T(8,128)(2,1)} %fusion.3), channel_id=1, source_target_pairs={{0,12},{4,0},{8,4},{12,8},{1,13},{5,1},{9,5},{13,9},{2,14},{6,2},{... | collective-permute-start | bytes 3145736 | tf_op jit(solution)/shard_map/ppermute | solution.py:24
  148.0 3.4 %collective-permute-done.23 = bf16[128,2048]{1,0:T(8,128)(2,1)S(1)} collective-permute-done((bf16[128,2048]{1,0:T(8,128)(2,1)S(1)}, bf16[128,2048]{1,0:T(8,128)(2,1)S(1)}, u32[]{:S(2)}, u32[]{:S(2)}) %collective-permute-start.23) | collective-permute-done | bytes 524320 | tf_op jit(solution)/shard_map/ppermute | solution.py:18
  153.4 3.7 %collective-permute-start.24 = (bf16[256,2048]{1,0:T(8,128)(2,1)}, bf16[256,2048]{1,0:T(8,128)(2,1)}, u32[]{:S(2)}, u32[]{:S(2)}) collective-permute-start(bf16[256,2048]{1,0:T(8,128)(2,1)} %fusion.1), channel_id=1, source_target_pairs={{0,96},{16,112},{32,0},{48,16},{64,32},{80,48},{96,64},{112,80},{1... | collective-permute-start | bytes 3145736 | tf_op jit(solution)/shard_map/ppermute | solution.py:18
  159.1 3.9 %shard_map.107 = (bf16[352,1024]{1,0:T(8,128)(2,1)S(1)}, bf16[352,1024]{1,0:T(8,128)(2,1)}) custom-call(bf16[1024,512]{1,0:T(8,128)(2,1)} %pad_maximum_fusion.refs_5_.refs_0_, bf16[1024,512]{1,0:T(8,128)(2,1)} %collective-permute-done.13.refs_6_.refs_1_, bf16[512,512]{1,0:T(8,128)(2,1)S(1)} %collective-permute-done.14.refs_7_.refs_2_, ...), custom_call_target="tpu_custom_call" | custom-call | tf_op jit(solution)/shard_map/pallas_call | solution.py:120
  164.4 9.0 %all-to-all-start.2 = ((bf16[8,352,128]{2,1,0:T(8,128)(2,1)}), bf16[8,352,128]{2,1,0:T(8,128)(2,1)S(1)}, u32[]{:S(2)}, u32[]{:S(2)}) async-start(bf16[8,352,128]{2,1,0:T(8,128)(2,1)} %add_convert_fusion.3), calls=%async_computation.2 | async-start | bytes 1441792 | tf_op jit(solution)/shard_map/all_to_all | solution.py:440
  179.4 8.3 %collective-permute-done.24 = bf16[256,2048]{1,0:T(8,128)(2,1)} collective-permute-done((bf16[256,2048]{1,0:T(8,128)(2,1)}, bf16[256,2048]{1,0:T(8,128)(2,1)}, u32[]{:S(2)}, u32[]{:S(2)}) %collective-permute-start.24) | collective-permute-done | bytes 1048608 | tf_op jit(solution)/shard_map/ppermute | solution.py:18
  187.7 3.6 %collective-permute-done.22 = bf16[256,2048]{1,0:T(8,128)(2,1)} collective-permute-done((bf16[256,2048]{1,0:T(8,128)(2,1)}, bf16[256,2048]{1,0:T(8,128)(2,1)}, u32[]{:S(2)}, u32[]{:S(2)}) %collective-permute-start.22) | collective-permute-done | bytes 1048608 | tf_op jit(solution)/shard_map/ppermute | solution.py:18
  193.9 8.7 %collective-permute-done.38 = bf16[8,352,128]{2,1,0:T(8,128)(2,1)S(1)} collective-permute-done((bf16[8,352,128]{2,1,0:T(8,128)(2,1)}, bf16[8,352,128]{2,1,0:T(8,128)(2,1)S(1)}, u32[]{:S(2)}, u32[]{:S(2)}) %collective-permute-start.38) | collective-permute-done | bytes 720928 | tf_op jit(solution)/shard_map/ppermute | solution.py:32
  208.2 8.7 %all-to-all-start.1 = ((bf16[8,352,128]{2,1,0:T(8,128)(2,1)}), bf16[8,352,128]{2,1,0:T(8,128)(2,1)S(1)}, u32[]{:S(2)}, u32[]{:S(2)}) async-start(bf16[8,352,128]{2,1,0:T(8,128)(2,1)} %add_convert_fusion.4), calls=%async_computation.1 | async-start | bytes 1441792 | tf_op jit(solution)/shard_map/all_to_all | solution.py:440
  219.6 3.6 %collective-permute-start.35 = (bf16[128,512]{1,0:T(8,128)(2,1)S(1)}, bf16[128,512]{1,0:T(8,128)(2,1)S(1)}, u32[]{:S(2)}, u32[]{:S(2)}) collective-permute-start(bf16[128,512]{1,0:T(8,128)(2,1)S(1)} %get-tuple-element.71), channel_id=1, source_target_pairs={{0,16},{16,0},{32,48},{48,32},{64,80},{80,64},{96,112},{112,96},{1... | collective-permute-start | bytes 393224 | tf_op jit(solution)/shard_map/ppermute | solution.py:28
  231.8 3.4 %collective-permute-done.36 = bf16[128,512]{1,0:T(8,128)(2,1)S(1)} collective-permute-done((bf16[128,512]{1,0:T(8,128)(2,1)S(1)}, bf16[128,512]{1,0:T(8,128)(2,1)S(1)}, u32[]{:S(2)}, u32[]{:S(2)}) %collective-permute-start.36) | collective-permute-done | bytes 131104 | tf_op jit(solution)/shard_map/ppermute | solution.py:32
  (129 shorter events, 100.2 us)
Async XLA Ops:
  13.3 43.1 %all-to-all-start = ((bf16[8,704,128]{2,1,0:T(8,128)(2,1)}), bf16[8,704,128]{2,1,0:T(8,128)(2,1)S(1)}, u32[]{:S(2)}, u32[]{:S(2)}) async-start(bf16[8,704,128]{2,1,0:T(8,128)(2,1)} %shard_map.95), calls=%async_computation | async-start | bytes 2883584 | tf_op jit(solution)/shard_map/all_to_all | solution.py:406
  24.5 31.1 %collective-permute-start.17 = (bf16[352,1024]{1,0:T(8,128)(2,1)}, bf16[352,1024]{1,0:T(8,128)(2,1)S(1)}, u32[]{:S(2)}, u32[]{:S(2)}) collective-permute-start(bf16[352,1024]{1,0:T(8,128)(2,1)} %refs_2_), channel_id=1, source_target_pairs={{0,2},{1,3},{2,0},{3,1},{4,6},{5,7},{6,4},{7,5},{8,10},{9,11},{10,... | collective-permute-start | bytes 2162696 | tf_op jit(solution)/shard_map/ppermute | solution.py:32
  27.2 17.7 %collective-permute-start.8 = (bf16[256,512]{1,0:T(8,128)(2,1)S(1)}, bf16[256,512]{1,0:T(8,128)(2,1)S(1)}, u32[]{:S(2)}, u32[]{:S(2)}) collective-permute-start(bf16[256,512]{1,0:T(8,128)(2,1)S(1)} %get-tuple-element.46), channel_id=1, source_target_pairs={{0,96},{16,112},{32,0},{48,16},{64,32},{80,48},{96,64},{112,80},{1... | collective-permute-start | bytes 786440 | tf_op jit(solution)/shard_map/ppermute | solution.py:18
  50.5 25.3 %collective-permute-start.15 = (bf16[1024,512]{1,0:T(8,128)(2,1)}, bf16[1024,512]{1,0:T(8,128)(2,1)}, u32[]{:S(2)}, u32[]{:S(2)}) collective-permute-start(bf16[1024,512]{1,0:T(8,128)(2,1)} %pad_maximum_fusion.refs_5_.refs_0_), channel_id=1, source_target_pairs={{0,12},{4,0},{8,4},{12,8},{1,13},{5,1},{9,5},{13,9},{2,14},{6,2},{... | collective-permute-start | bytes 3145736 | tf_op jit(solution)/shard_map/ppermute | solution.py:24
  53.5 26.9 %collective-permute-start.13 = (bf16[1024,512]{1,0:T(8,128)(2,1)}, bf16[1024,512]{1,0:T(8,128)(2,1)}, u32[]{:S(2)}, u32[]{:S(2)}) collective-permute-start(bf16[1024,512]{1,0:T(8,128)(2,1)} %pad_maximum_fusion.refs_5_.refs_0_), channel_id=1, source_target_pairs={{0,4},{4,8},{8,12},{12,0},{1,5},{5,9},{9,13},{13,1},{2,6},{6,10},{... | collective-permute-start | bytes 3145736 | tf_op jit(solution)/shard_map/ppermute | solution.py:24
  53.5 28.1 %collective-permute-start.11 = (bf16[256,2048]{1,0:T(8,128)(2,1)S(1)}, bf16[256,2048]{1,0:T(8,128)(2,1)S(1)}, u32[]{:S(2)}, u32[]{:S(2)}) collective-permute-start(bf16[256,2048]{1,0:T(8,128)(2,1)S(1)} %shard_map.94.refs_0_), channel_id=1, source_target_pairs={{0,96},{16,112},{32,0},{48,16},{64,32},{80,48},{96,64},{112,80},{1... | collective-permute-start | bytes 3145736 | tf_op jit(solution)/shard_map/ppermute | solution.py:18
  54.7 27.0 %collective-permute-start.9 = (bf16[256,2048]{1,0:T(8,128)(2,1)S(1)}, bf16[256,2048]{1,0:T(8,128)(2,1)}, u32[]{:S(2)}, u32[]{:S(2)}) collective-permute-start(bf16[256,2048]{1,0:T(8,128)(2,1)S(1)} %shard_map.94.refs_0_), channel_id=1, source_target_pairs={{0,32},{16,48},{32,64},{48,80},{64,96},{80,112},{96,0},{112,16},{1... | collective-permute-start | bytes 3145736 | tf_op jit(solution)/shard_map/ppermute | solution.py:18
  56.4 39.6 %collective-permute-start.18 = (bf16[8,704,128]{2,1,0:T(8,128)(2,1)S(1)}, bf16[8,704,128]{2,1,0:T(8,128)(2,1)S(1)}, u32[]{:S(2)}, u32[]{:S(2)}) collective-permute-start(bf16[8,704,128]{2,1,0:T(8,128)(2,1)S(1)} %all-to-all-done.refs_10_.refs_2_), channel_id=1, source_target_pairs={{0,2},{1,3},{2,0},{3,1},{4,6},{5,7},{6,4},{7,5},{8,10},{9,11},{10,... | collective-permute-start | bytes 4325384 | tf_op jit(solution)/shard_map/ppermute | solution.py:32
  125.0 15.8 %collective-permute-start.30 = (bf16[512,512]{1,0:T(8,128)(2,1)S(1)}, bf16[512,512]{1,0:T(8,128)(2,1)S(1)}, u32[]{:S(2)}, u32[]{:S(2)}) collective-permute-start(bf16[512,512]{1,0:T(8,128)(2,1)S(1)} %get-tuple-element.69), channel_id=1, source_target_pairs={{0,12},{4,0},{8,4},{12,8},{1,13},{5,1},{9,5},{13,9},{2,14},{6,2},{... | collective-permute-start | bytes 1572872 | tf_op jit(solution)/shard_map/ppermute | solution.py:24
  127.9 18.1 %collective-permute-start.28 = (bf16[512,512]{1,0:T(8,128)(2,1)S(1)}, bf16[512,512]{1,0:T(8,128)(2,1)S(1)}, u32[]{:S(2)}, u32[]{:S(2)}) collective-permute-start(bf16[512,512]{1,0:T(8,128)(2,1)S(1)} %get-tuple-element.67), channel_id=1, source_target_pairs={{0,4},{4,8},{8,12},{12,0},{1,5},{5,9},{9,13},{13,1},{2,6},{6,10},{... | collective-permute-start | bytes 1572872 | tf_op jit(solution)/shard_map/ppermute | solution.py:24
  131.0 31.9 %collective-permute-start.39 = (bf16[8,352,128]{2,1,0:T(8,128)(2,1)S(1)}, bf16[8,352,128]{2,1,0:T(8,128)(2,1)S(1)}, u32[]{:S(2)}, u32[]{:S(2)}) collective-permute-start(bf16[8,352,128]{2,1,0:T(8,128)(2,1)S(1)} %get-tuple-element.78), channel_id=1, source_target_pairs={{0,2},{1,3},{2,0},{3,1},{4,6},{5,7},{6,4},{7,5},{8,10},{9,11},{10,... | collective-permute-start | bytes 2162696 | tf_op jit(solution)/shard_map/ppermute | solution.py:32
  137.5 19.6 %collective-permute-start.21 = (bf16[128,2048]{1,0:T(8,128)(2,1)S(1)}, bf16[128,2048]{1,0:T(8,128)(2,1)S(1)}, u32[]{:S(2)}, u32[]{:S(2)}) collective-permute-start(bf16[128,2048]{1,0:T(8,128)(2,1)S(1)} %get-tuple-element.58), channel_id=1, source_target_pairs={{0,32},{16,48},{32,64},{48,80},{64,96},{80,112},{96,0},{112,16},{1... | collective-permute-start | bytes 1572872 | tf_op jit(solution)/shard_map/ppermute | solution.py:18
  142.8 30.6 %collective-permute-start.31 = (bf16[1024,512]{1,0:T(8,128)(2,1)}, bf16[1024,512]{1,0:T(8,128)(2,1)}, u32[]{:S(2)}, u32[]{:S(2)}) collective-permute-start(bf16[1024,512]{1,0:T(8,128)(2,1)} %fusion.3), channel_id=1, source_target_pairs={{0,12},{4,0},{8,4},{12,8},{1,13},{5,1},{9,5},{13,9},{2,14},{6,2},{... | collective-permute-start | bytes 3145736 | tf_op jit(solution)/shard_map/ppermute | solution.py:24
  148.0 26.6 %collective-permute-start.29 = (bf16[1024,512]{1,0:T(8,128)(2,1)}, bf16[1024,512]{1,0:T(8,128)(2,1)}, u32[]{:S(2)}, u32[]{:S(2)}) collective-permute-start(bf16[1024,512]{1,0:T(8,128)(2,1)} %fusion.2), channel_id=1, source_target_pairs={{0,4},{4,8},{8,12},{12,0},{1,5},{5,9},{9,13},{13,1},{2,6},{6,10},{... | collective-permute-start | bytes 3145736 | tf_op jit(solution)/shard_map/ppermute | solution.py:24
  153.4 34.3 %collective-permute-start.24 = (bf16[256,2048]{1,0:T(8,128)(2,1)}, bf16[256,2048]{1,0:T(8,128)(2,1)}, u32[]{:S(2)}, u32[]{:S(2)}) collective-permute-start(bf16[256,2048]{1,0:T(8,128)(2,1)} %fusion.1), channel_id=1, source_target_pairs={{0,96},{16,112},{32,0},{48,16},{64,32},{80,48},{96,64},{112,80},{1... | collective-permute-start | bytes 3145736 | tf_op jit(solution)/shard_map/ppermute | solution.py:18
  159.0 32.3 %collective-permute-start.22 = (bf16[256,2048]{1,0:T(8,128)(2,1)}, bf16[256,2048]{1,0:T(8,128)(2,1)}, u32[]{:S(2)}, u32[]{:S(2)}) collective-permute-start(bf16[256,2048]{1,0:T(8,128)(2,1)} %fusion), channel_id=1, source_target_pairs={{0,32},{16,48},{32,64},{48,80},{64,96},{80,112},{96,0},{112,16},{1... | collective-permute-start | bytes 3145736 | tf_op jit(solution)/shard_map/ppermute | solution.py:18
  162.9 60.3 %collective-permute-start.40 = (bf16[352,1024]{1,0:T(8,128)(2,1)}, bf16[352,1024]{1,0:T(8,128)(2,1)}, u32[]{:S(2)}, u32[]{:S(2)}) collective-permute-start(bf16[352,1024]{1,0:T(8,128)(2,1)} %get-tuple-element.80), channel_id=1, source_target_pairs={{0,2},{1,3},{2,0},{3,1},{4,6},{5,7},{6,4},{7,5},{8,10},{9,11},{10,... | collective-permute-start | bytes 2162696 | tf_op jit(solution)/shard_map/ppermute | solution.py:32
  164.4 43.8 %all-to-all-start.2 = ((bf16[8,352,128]{2,1,0:T(8,128)(2,1)}), bf16[8,352,128]{2,1,0:T(8,128)(2,1)S(1)}, u32[]{:S(2)}, u32[]{:S(2)}) async-start(bf16[8,352,128]{2,1,0:T(8,128)(2,1)} %add_convert_fusion.3), calls=%async_computation.2 | async-start | bytes 1441792 | tf_op jit(solution)/shard_map/all_to_all | solution.py:440
  173.4 29.2 %collective-permute-start.38 = (bf16[8,352,128]{2,1,0:T(8,128)(2,1)}, bf16[8,352,128]{2,1,0:T(8,128)(2,1)S(1)}, u32[]{:S(2)}, u32[]{:S(2)}) collective-permute-start(bf16[8,352,128]{2,1,0:T(8,128)(2,1)} %copy-done.12), channel_id=1, source_target_pairs={{0,2},{1,3},{2,0},{3,1},{4,6},{5,7},{6,4},{7,5},{8,10},{9,11},{10,... | collective-permute-start | bytes 2162696 | tf_op jit(solution)/shard_map/ppermute | solution.py:32
  177.4 25.3 %collective-permute-start.32 = (bf16[256,512]{1,0:T(8,128)(2,1)S(1)}, bf16[256,512]{1,0:T(8,128)(2,1)S(1)}, u32[]{:S(2)}, u32[]{:S(2)}) collective-permute-start(bf16[256,512]{1,0:T(8,128)(2,1)S(1)} %get-tuple-element.81), channel_id=1, source_target_pairs={{0,32},{16,48},{32,64},{48,80},{64,96},{80,112},{96,0},{112,16},{1... | collective-permute-start | bytes 786440 | tf_op jit(solution)/shard_map/ppermute | solution.py:18
  187.7 18.2 %collective-permute-start.34 = (bf16[256,512]{1,0:T(8,128)(2,1)S(1)}, bf16[256,512]{1,0:T(8,128)(2,1)S(1)}, u32[]{:S(2)}, u32[]{:S(2)}) collective-permute-start(bf16[256,512]{1,0:T(8,128)(2,1)S(1)} %get-tuple-element.82), channel_id=1, source_target_pairs={{0,64},{16,80},{32,96},{48,112},{64,0},{80,16},{96,32},{112,48},{1... | collective-permute-start | bytes 786440 | tf_op jit(solution)/shard_map/ppermute | solution.py:18
  191.3 25.6 %collective-permute-start.33 = (bf16[256,512]{1,0:T(8,128)(2,1)}, bf16[256,512]{1,0:T(8,128)(2,1)}, u32[]{:S(2)}, u32[]{:S(2)}) collective-permute-start(bf16[256,512]{1,0:T(8,128)(2,1)} %get-tuple-element.83), channel_id=1, source_target_pairs={{0,96},{16,112},{32,0},{48,16},{64,32},{80,48},{96,64},{112,80},{1... | collective-permute-start | bytes 786440 | tf_op jit(solution)/shard_map/ppermute | solution.py:18
  202.6 15.6 %collective-permute-start.25 = (bf16[256,512]{1,0:T(8,128)(2,1)S(1)}, bf16[256,512]{1,0:T(8,128)(2,1)}, u32[]{:S(2)}, u32[]{:S(2)}) collective-permute-start(bf16[256,512]{1,0:T(8,128)(2,1)S(1)} %get-tuple-element.62), channel_id=1, source_target_pairs={{0,4},{4,8},{8,12},{12,0},{1,5},{5,9},{9,13},{13,1},{2,6},{6,10},{... | collective-permute-start | bytes 786440 | tf_op jit(solution)/shard_map/ppermute | solution.py:24
  208.2 20.3 %all-to-all-start.1 = ((bf16[8,352,128]{2,1,0:T(8,128)(2,1)}), bf16[8,352,128]{2,1,0:T(8,128)(2,1)S(1)}, u32[]{:S(2)}, u32[]{:S(2)}) async-start(bf16[8,352,128]{2,1,0:T(8,128)(2,1)} %add_convert_fusion.4), calls=%async_computation.1 | async-start | bytes 1441792 | tf_op jit(solution)/shard_map/all_to_all | solution.py:440
  (35 other events, 289.0 us)

commit v2 on v1

--- a/solution.py
+++ b/solution.py
@@ -101,8 +101,9 @@
     )
 
 
-def assembled_call(kernel, out_shapes, operands, buffers, copies, vmem=40):
+def assembled_call(kernel, out_shapes, operands, buffers, copies, vmem=40, dtype=BF16):
     count, outs = len(operands), len(out_shapes)
+    buffers = [buffer if len(buffer) == 2 and isinstance(buffer[0], tuple) else (buffer, BF16) for buffer in buffers]
 
     def body(*refs):
         sources, refs = refs[:count], refs[count:]
@@ -119,11 +120,11 @@
     return list(
         pl.pallas_call(
             body,
-            out_shape=[jax.ShapeDtypeStruct(shape, BF16) for shape in out_shapes],
+            out_shape=[jax.ShapeDtypeStruct(shape, dtype) for shape in out_shapes],
             in_specs=[pl.BlockSpec(memory_space=pl.ANY)] * count,
             out_specs=[pl.BlockSpec(memory_space=pltpu.VMEM)] * outs,
             scratch_shapes=[
-                *(pltpu.VMEM(shape, BF16) for shape in buffers),
+                *(pltpu.VMEM(*buffer) for buffer in buffers),
                 pltpu.SemaphoreType.DMA((copies,)),
             ],
             compiler_params=pltpu.CompilerParams(vmem_limit_bytes=vmem * 2**20),
@@ -180,10 +181,12 @@
             out[g, first : first + own] = array[:, g * own : (g + 1) * own].T
 
 
-def join_blocks(pieces, out):
-    groups, own, _ = pieces.shape
+def join_blocks(pieces, gate, up):
+    groups, both, _ = pieces.shape
+    own = both // 2
     for g in range(groups):
-        out[:, g * own : (g + 1) * own] = pieces[g].T
+        gate[:, g * own : (g + 1) * own] = pieces[g, :own].T
+        up[:, g * own : (g + 1) * own] = pieces[g, own:].T
 
 
 def join_features(*refs):
@@ -228,14 +231,15 @@
     return copies
 
 
+def copy_blocks(copy, ref, held):
+    groups, _, count = ref.shape
+    return [copy(ref.at[g], held.at[:, pl.ds(g * count, count)]) for g in range(groups)]
+
+
 def copy_pair(copy, near, far, held):
-    copies = []
-    groups, _, count = near.shape
-    for side, ref in enumerate((near, far)):
-        for g in range(groups):
-            target = held.at[:, pl.ds((side * groups + g) * count, count)]
-            copies.append(copy(ref.at[g], target))
-    return copies
+    features = held.shape[1] // 2
+    copies = copy_blocks(copy, near, held.at[:, pl.ds(0, features)])
+    return copies + copy_blocks(copy, far, held.at[:, pl.ds(features, features)])
 
 
 def copy_down(copy, near, far, held):
@@ -257,42 +261,73 @@
     ]
 
 
-def sums_products(copy, sources, results, tokens, grads, pair, down):
+def near_products(copy, sources, results, tokens, pair):
+    features = tokens.shape[1]
+    copies = copy_blocks(copy, sources[5], pair)
+    copies += copy_tokens(copy, [ref.at[:, pl.ds(0, features)] for ref in sources[:5]], tokens)
+    wait_all(copies)
+    results[0][...] = dot(tokens[...], pair[...], 1, 1)
+
+
+def pair_products(copy, sources, results, tokens, pair, share):
     keep, send = results
-    half, width = keep.shape[1], keep.shape[2] // 3
+    half, width = keep.shape[1], keep.shape[2] // 2
+    own = pair.shape[0] // 2
+    features = tokens.shape[1]
+    copies = copy_blocks(copy, sources[5], pair)
+    far = [ref.at[:, pl.ds(features, features)] for ref in sources[:5]]
+    chunks = copy_tokens(copy, far, tokens)
+    rows = 4 * half
+    shares = [
+        copy(sources[6].at[pl.ds(first, rows)], share.at[pl.ds(first, rows)]) for first in (0, rows)
+    ]
+    wait_all(copies)
+    padding = jnp.zeros((half, width - own), BF16)
+    for i, arrived in ((0, chunks[:2]), (2, chunks[2:])):
+        here = pl.ds(2 * i * half, rows)
+        wait_all(arrived)
+        part = dot(tokens[here], pair[...], 1, 1)
+        shares[i // 2].wait()
+        part = (part + share[here]).astype(BF16)
+        for j in (0, 1):
+            for out, at in ((keep, 2 * j * half), (send, (2 * j + 1) * half)):
+                piece = part[at : at + half]
+                for k in (0, 1):
+                    out[i + j, :, k * width : k * width + own] = piece[:, k * own : (k + 1) * own]
+                    out[i + j, :, k * width + own : (k + 1) * width] = padding
+
+
+def hidden_products(copy, sources, results, grads, down):
+    keep, send = results
+    half, width = keep.shape[1:]
     own = down.shape[0]
-    copies = copy_tokens(copy, sources[:5], tokens)
-    copies += copy_pair(copy, *sources[10:12], pair)
-    later = copy_grads(copy, sources[5:10], grads) + copy_down(copy, *sources[12:], down)
+    copies = copy_down(copy, *sources[5:], down)
+    wait_all(copies + copy_grads(copy, sources[:5], grads))
     padding = jnp.zeros((half, width - own), BF16)
-    wait_all(copies)
-    for step, (left, right) in enumerate(((tokens, pair), (grads, down))):
-        if step == 1:
-            wait_all(later)
-        for i in (0, 2):
-            part = dot(left[pl.ds(2 * i * half, 4 * half)], right[...], 1, 1).astype(BF16)
-            for j in (0, 1):
-                for out, at in ((keep, 2 * j * half), (send, (2 * j + 1) * half)):
-                    rows = part[at : at + half]
-                    for k in (0, 1) if step == 0 else (2,):
-                        first = k * own if step == 0 else 0
-                        out[i + j, :, k * width : k * width + own] = rows[:, first : first + own]
-                        out[i + j, :, k * width + own : (k + 1) * width] = padding
-
-
-def activate(keep, got, out):
+    for i in (0, 2):
+        part = dot(grads[pl.ds(2 * i * half, 4 * half)], down[...], 1, 1).astype(BF16)
+        for j in (0, 1):
+            for out, at in ((keep, 2 * j * half), (send, (2 * j + 1) * half)):
+                out[i + j, :, :own] = part[at : at + half]
+                out[i + j, :, own:] = padding
+
+
+def activate(own, keep, got, keep_hidden, got_hidden, out):
     width = out.shape[2] // 3
+    padding = jnp.zeros((out.shape[1], 3 * width - (width + 2 * own)), BF16)
     for i in range(out.shape[0]):
-        gate_sum, up_sum, grad_hidden = (
+        gate_sum, up_sum = (
             add(keep[i, :, k * width : (k + 1) * width], got[i, :, k * width : (k + 1) * width])
-            for k in range(3)
+            for k in range(2)
         )
+        grad_hidden = add(keep_hidden[i], got_hidden[i])
         sigmoid_gate = jax.nn.sigmoid(gate_sum)
         out[i, :, :width] = (gate_sum * sigmoid_gate * up_sum).astype(BF16)
-        out[i, :, width : 2 * width] = (
-            grad_hidden * up_sum * sigmoid_gate * (1.0 + gate_sum * (1.0 - sigmoid_gate))
-        ).astype(BF16)
-        out[i, :, 2 * width :] = (grad_hidden * gate_sum * sigmoid_gate).astype(BF16)
+        grad_gate_act = grad_hidden * up_sum * sigmoid_gate * (1.0 + gate_sum * (1.0 - sigmoid_gate))
+        out[i, :, width : 2 * width] = grad_gate_act.astype(BF16)
+        grad_up_act = (grad_hidden * gate_sum * sigmoid_gate).astype(BF16)
+        out[i, :, width + own : width + 2 * own] = grad_up_act[:, :own]
+        out[i, :, width + 2 * own :] = padding
 
 
 def output_products(copy, sources, results, hidden, down):
@@ -306,28 +341,25 @@
 
 
 def input_products(copy, sources, results, acts, pair):
-    width, own = acts.shape[1] // 2, pair.shape[0] // 2
-    copies = copy_part(copy, sources[0], sources[1], width, acts)
+    copies = copy_part(copy, sources[0], sources[1], acts.shape[1] // 2, acts)
     wait_all(copies + copy_pair(copy, *sources[2:], pair))
+    both = pair.shape[0]
     count, features = results[0].shape[1] // 2, pair.shape[1] // 2
-    for out, k, first in zip(results, (0, 1, 2, 2, 3), (0, 0, 0, results[2].shape[0], 0)):
-        rows = pl.ds(first, out.shape[0])
+    for k, out in enumerate(results):
         for side in (0, 1):
             place = pl.ds(pl.multiple_of(side * features + own_place(k, count), count), count)
-            part = dot(acts[rows, :own], pair[:own, place], 1, 0)
-            part += dot(acts[rows, width : width + own], pair[own:, place], 1, 0)
+            part = dot(acts[:, :both], pair[:, place], 1, 0)
             out[:, side * count : (side + 1) * count] = part.astype(BF16)
 
 
-def pair_gradients(scale, part, copy, sources, results, tokens, acts):
-    width = acts.shape[1]
+def pair_gradients(scale, copy, sources, results, tokens, acts):
     copies = copy_tokens(copy, sources[:5], tokens)
-    wait_all(copies + copy_part(copy, *sources[5:], part * width, acts))
+    wait_all(copies + copy_part(copy, *sources[5:], acts.shape[1] // 2, acts))
     near, far = results
-    groups, own, count = near.shape
+    groups, both, count = near.shape
     features = groups * count
     for out, first in ((far, features), (near, 0)):
-        total = dot(acts[:, :own], tokens[:, pl.ds(first, features)], 0, 0) * scale
+        total = dot(acts[:, :both], tokens[:, pl.ds(first, features)], 0, 0) * scale
         for g in range(groups):
             out[g] = total[:, g * count : (g + 1) * count].astype(BF16)
 
@@ -342,19 +374,21 @@
         out[...] = (total * scale).astype(BF16)
 
 
-def split_result(output, grad_input, near, far, near_x, far_x):
+def split_result(*refs):
+    *parts, near, far, near_x, far_x = refs
     half, count = near.shape[0], near.shape[1] // 2
     core = core_index()
-    for index, left, right in ((core, near, far), (1 - core, near_x, far_x)):
-        for first, array in ((0, output), (count, grad_input)):
-            rows = array[block(index, half)]
+    for first, arrays in ((0, parts[:4]), (count, parts[4:])):
+        for index, left, right in ((core, near, far), (1 - core, near_x, far_x)):
+            rows = sum(array[block(index, half)].astype(F32) for array in arrays).astype(BF16)
             left[:, first : first + count] = rows[:, :count]
             right[:, first : first + count] = rows[:, count:]
 
 
-def join_result(mine, theirs, output, grad_input):
-    half, count = mine.shape[0], mine.shape[1] // 2
-    for rows, index in ((mine, x_lo_index()), (theirs, 1 - x_lo_index())):
+def join_result(near, near_x, far, far_x, output, grad_input):
+    half, count = near.shape[0], near.shape[1] // 2
+    for parts, index in (((near, near_x), x_lo_index()), ((far, far_x), 1 - x_lo_index())):
+        rows = add(parts[0][...], parts[1][...]).astype(BF16)
         output[block(index, half)] = rows[:, :count]
         grad_input[block(index, half)] = rows[:, count:]
 
@@ -365,27 +399,12 @@
     return [array, before, shift(before[:half], 1), shift(after[half:], -1), after]
 
 
-def ring_scatter(shift, own, before, low, high, after):
-    half = low.shape[0]
-    from_before, from_after = shift(low, 1), shift(high, -1)
-    after = lax.dynamic_update_slice(after, add(after[:half], from_before).astype(BF16), (0, 0))
-    before = lax.dynamic_update_slice(
-        before, add(before[half:], from_after).astype(BF16), (half, 0)
-    )
-    return own.astype(F32) + shift(after, 1).astype(F32) + shift(before, -1).astype(F32)
-
-
 def direct_gather(shift, array):
     return [array, shift(array, 1), shift(array, 2), shift(array, -1)]
 
 
 def direct_scatter(shift, own, before, opposite, after):
-    return (
-        own.astype(F32)
-        + shift(after, 1).astype(F32)
-        + shift(before, -1).astype(F32)
-        + shift(opposite, 2).astype(F32)
-    )
+    return [own, shift(before, -1), shift(after, 1), shift(opposite, 2)]
 
 
 def on_device(tokens, w_gate, w_up, w_down, grad_output):
@@ -402,83 +421,119 @@
     t_block, g_block = local_call(arrange_rows, [(2 * rows, columns)] * 2, four)
 
     (pieces,) = local_call(split_pair, [(8, 2 * own, rows_in)], [w_gate, w_up])
-    pieces, w_down = lax.optimization_barrier((pieces, w_down, *four))[:2]
-    w_near = lax.all_to_all(pieces, "gx", 0, 0, tiled=True)
-    d_near, d_far = w_down, swap_x_lo(w_down)
-    w_far = swap_x_lo(after(w_near, d_far))
+    w_near = lax.all_to_all(after(pieces, *four), "gx", 0, 0, tiled=True)
+    d_near, d_far = w_down, swap_x_lo(after(w_down, *four))
 
     (t_own,) = local_call(
         join_features, [(2 * rows, 2 * features)], direct_gather(shift_y, t_block)
     )
     g_own = jnp.concatenate(direct_gather(shift_z, g_block), axis=0)
-    t_own, g_own = lax.optimization_barrier((t_own, g_own))
+    t_own, g_own, w_near, d_far = lax.optimization_barrier((t_own, g_own, w_near, d_far))
+    w_far = swap_x_lo(w_near)
     t_all = ring_gather(shift_z, t_own)
     g_all = ring_gather(shift_y, g_own)
 
     all_tokens, all_features = 8 * rows, 2 * features
     whole = (all_tokens, all_features)
+    keep_hidden, send_hidden = assembled_call(
+        hidden_products,
+        [(4, rows, width)] * 2,
+        [*g_all, d_near, d_far],
+        [whole, (own, all_features)],
+        12,
+    )
+    got_hidden = swap_core(send_hidden)
+    half_features = (all_tokens, features)
+    (share,) = assembled_call(
+        near_products,
+        [(all_tokens, 2 * own)],
+        [*t_all, w_near],
+        [half_features, (2 * own, features)],
+        13,
+        dtype=F32,
+    )
     keep, send = assembled_call(
-        sums_products,
-        [(4, rows, 3 * width)] * 2,
-        [*t_all, *g_all, w_near, w_far, d_near, d_far],
-        [whole, whole, (2 * own, all_features), (own, all_features)],
-        33,
-    )
-    (mine,) = local_call(activate, [(4, rows, 3 * width)], [keep, swap_core(send)])
+        pair_products,
+        [(4, rows, 2 * width)] * 2,
+        [*t_all[:4], after(t_all[4], got_hidden), w_far, share],
+        [half_features, (2 * own, features), ((all_tokens, 2 * own), F32)],
+        15,
+    )
+    (mine,) = local_call(
+        functools.partial(activate, own),
+        [(4, rows, 3 * width)],
+        [keep, swap_core(send), keep_hidden, got_hidden],
+    )
     both = [mine, swap_core(mine)]
 
-    grad_pair = []
-    for part in (1, 2):
-        near, far = assembled_call(
-            functools.partial(pair_gradients, loss_scale, part),
-            [(8, own, rows_in)] * 2,
-            [*t_all, *both],
-            [whole, (all_tokens, width)],
-            13,
-        )
-        total = add(near, swap_x_lo(far)).astype(BF16)
-        total = lax.all_to_all(total, "gx", 0, 0, tiled=True)
-        grad_pair += local_call(join_blocks, [(rows_in, width_hidden)], [total])
-        if part == 1:
-            both[1] = after(both[1], near)
     near, far = assembled_call(
+        functools.partial(pair_gradients, loss_scale),
+        [(8, 2 * own, rows_in)] * 2,
+        [*t_all, *both],
+        [whole, (all_tokens, 2 * width)],
+        13,
+    )
+    both[1] = after(both[1], near)
+    output_parts = assembled_call(
+        output_products,
+        [(size * rows, all_features) for size in (2, 2, 1, 1, 2)],
+        [*both, d_near, d_far],
+        [(all_tokens, width), (own, all_features)],
+        10,
+    )
+    both[1] = after(both[1], output_parts[2])
+    input_parts = assembled_call(
+        input_products,
+        [(all_tokens, columns)] * 4,
+        [*both, w_near, w_far],
+        [(all_tokens, 2 * width), (2 * own, all_features)],
+        24,
+    )
+    both[1] = after(both[1], input_parts[2])
+    down_near, down_far = assembled_call(
         functools.partial(down_gradients, loss_scale),
         [(own, features)] * 2,
         [*g_all, *both],
         [whole, (all_tokens, width)],
         18,
     )
-    grad_down = add(near, swap_x_lo(far)).astype(BF16)
-
-    shape, half_shape = (2 * rows, all_features), (rows, all_features)
-    parts = assembled_call(
-        output_products,
-        [shape, shape, half_shape, half_shape, shape],
-        [*both, d_near, d_far],
-        [(all_tokens, width), (own, all_features)],
-        10,
-    )
-    output = ring_scatter(shift_z, *parts).astype(BF16)
-    shape, half_shape = (all_tokens, columns), (all_tokens // 2, columns)
-    parts = assembled_call(
-        input_products,
-        [shape, shape, half_shape, half_shape, shape],
-        [*both, w_near, w_far],
-        [(all_tokens, 2 * width), (2 * own, all_features)],
-        24,
-    )
-    grad_input = ring_scatter(shift_y, *parts).astype(BF16)
+
+    grad_pair = add(near, swap_x_lo(far)).astype(BF16)
+    down_far = after(down_far, grad_pair)
+    total = lax.all_to_all(after(grad_pair, down_near), "gx", 0, 0, tiled=True)
+    grad_down = add(down_near, swap_x_lo(down_far)).astype(BF16)
+
+    own, before, low, high, after_it = output_parts
+    from_z = shift_z(low, 1), shift_z(high, -1)
+    after_it = lax.dynamic_update_slice(
+        after_it, add(after_it[:rows], from_z[0]).astype(BF16), (0, 0)
+    )
+    before = lax.dynamic_update_slice(
+        before, add(before[rows:], from_z[1]).astype(BF16), (rows, 0)
+    )
+    output = own.astype(F32) + shift_z(after_it, 1).astype(F32)
+    output = (output + shift_z(before, -1).astype(F32)).astype(BF16)
+    own, before, opposite, after_it = input_parts
+    from_y = shift_y(before, -1), shift_y(after_it, 1)
+    opposite = after(opposite, *from_y, *from_z)
+    grad_input = own.astype(F32) + from_y[0].astype(F32) + from_y[1].astype(F32)
+    grad_input = (grad_input + shift_y(opposite, 2).astype(F32)).astype(BF16)
+    output = after(output, grad_input)
+    grad_input = after(grad_input, total)
+    parts = [grad_input[2 * k * rows : 2 * (k + 1) * rows] for k in range(4)]
+    input_parts = direct_scatter(shift_z, *parts)
     parts = local_call(pick_features, [(2 * rows, columns)] * 4, [output])
-    output = direct_scatter(shift_y, *parts).astype(BF16)
-    parts = [grad_input[2 * k * rows : 2 * (k + 1) * rows] for k in range(4)]
-    grad_input = direct_scatter(shift_z, *parts).astype(BF16)
+    output_parts = direct_scatter(shift_y, *parts)
+    grads = local_call(join_blocks, [(rows_in, width_hidden)] * 2, [total])
+    output_parts[0], grad_down, *grads = lax.optimization_barrier(
+        (output_parts[0], grad_down, *grads)
+    )
     near, far, near_x, far_x = local_call(
-        split_result, [(rows, columns)] * 4, [output, grad_input]
-    )
-    mine = add(near, swap_x_hi(near_x)).astype(BF16)
-    theirs = add(swap_x_lo(far), swap_x(far_x)).astype(BF16)
-    output, grad_input = local_call(join_result, [tokens.shape] * 2, [mine, theirs])
-    return (output, grad_input, *grad_pair, grad_down)
+        split_result, [(rows, columns)] * 4, [*output_parts, *input_parts]
+    )
+    four = [near, swap_x_hi(near_x), swap_x_lo(far), swap_x(far_x)]
+    output, grad_input = local_call(join_result, [tokens.shape] * 2, four)
+    return (output, grad_input, *grads, grad_down)
 
 
 def solution(mesh):

time: 239 us -> 214 us (0.90)
  starting transfers between devices: 84.1 us -> 67.9 us
  waiting for transfers between devices: 79.9 us -> 88.1 us
  other arithmetic: 19.9 us -> 12.8 us
  local copies, waits for them, and re-layouts: 12.8 us -> 6.33 us
  Pallas kernels: 40.1 us -> 36.9 us
    ppermute x14 -> x13, waiting for transfers between devices: 30.4 us -> 52 us  [shift_y(): return lax.ppermute(array, 'gy', [(i, (i + steps) % 4) for i in range(4)])]
    all_to_all x3 -> x2, starting transfers between devices: 24.4 us -> 12.9 us  [the longest x1 6.69 us: on_device(): w_near = lax.all_to_all(after(pieces, *four), 'gx', 0, 0, tiled=True)]
    ppermute x14, waiting for transfers between devices: 28.6 us -> 17.6 us  [shift_z(): lax.ppermute(array, 'gx', [(i, (i // 2 + steps) % 4 * 2 + i % 2) for i in...]
    ppermute x14 -> x13, starting transfers between devices: 22 us -> 17.4 us  [shift_y(): return lax.ppermute(array, 'gy', [(i, (i + steps) % 4) for i in range(4)])]
    ppermute x7 -> x6, starting transfers between devices: 7.37 us -> 3.41 us  [swap_x_lo(): return lax.ppermute(array, 'gz', [(i, i ^ 2) for i in range(4)])]
    dynamic_update_slice x4 -> x2, other arithmetic: 7.92 us -> 3.98 us  [the longest x1 2 us: on_device(): lax.dynamic_update_slice(before, add(before[rows:], from_z[1]).astype(BF1...]
    pallas_call x6 -> x7, Pallas kernels: 29.6 us -> 25.9 us  [assembled_call(): pl.pallas_call(body, out_shape=[jax.ShapeDtypeStruct(shape, dtype) for sh...]
    unnamed x30, local copies, waits for them, and re-layouts: 8.68 us -> 4.92 us
  transfers between devices with their start and end apart: 44 -> 42, of which waited for: 18 -> 22; matrix products, arithmetic and copies ran while one was open for 10% -> 7% of each run, Pallas kernels for 8% -> 10%
where the time goes in v2:
time: 214 us; the launch traced here: 213 us
  waiting for transfers between devices  88.1 us (41%)
  starting transfers between devices  67.9 us (32%)
  Pallas kernels  36.9 us (17%)
  other arithmetic  12.8 us (6%)
  local copies, waits for them, and re-layouts  6.33 us (3%)
    ppermute x13, waiting for transfers between devices, shift_y(): return lax.ppermute(array, 'gy', [(i, (i + steps) % 4) for i in range(4)])  52 us
    pallas_call x7, Pallas kernels, assembled_call(): pl.pallas_call(body, out_shape=[jax.ShapeDtypeStruct(shape, dtype) for sh...  25.9 us
    ppermute x14, starting transfers between devices, shift_z(): lax.ppermute(array, 'gx', [(i, (i // 2 + steps) % 4 * 2 + i % 2) for i in...  24.1 us
    ppermute x14, waiting for transfers between devices, shift_z(): lax.ppermute(array, 'gx', [(i, (i // 2 + steps) % 4 * 2 + i % 2) for i in...  17.6 us
    ppermute x13, starting transfers between devices, shift_y(): return lax.ppermute(array, 'gy', [(i, (i + steps) % 4) for i in range(4)])  17.4 us
    pallas_call x9, Pallas kernels, local_call(): pl.pallas_call(body, out_shape=[jax.ShapeDtypeStruct(shape, BF16) for sha...  11 us
    ppermute x6, waiting for transfers between devices, swap_x_lo(): return lax.ppermute(array, 'gz', [(i, i ^ 2) for i in range(4)])  10.1 us
    all_to_all x1, starting transfers between devices, on_device(): w_near = lax.all_to_all(after(pieces, *four), 'gx', 0, 0, tiled=True)  6.69 us
  transfers between devices with their start and end apart: 42, of which 22 were waited for; matrix products, arithmetic and copies ran while one was open for 7% of the time, Pallas kernels for 10%

profile of v2, /device:TPU:0, one launch (start us, length us, event | category | flops | bytes accessed | tf_op | source)
XLA Modules:
  0.0 213.2 jit_solution(10802748617624124626)
XLA Ops:
  9.8 3.2 %shard_map.95 = bf16[8,704,128]{2,1,0:T(8,128)(2,1)} custom-call(bf16[128,2816]{1,0:T(8,128)(2,1)S(1)} %copy-done.6, bf16[128,2816]{1,0:T(8,128)(2,1)S(1)} %copy-done.7), custom_call_target="tpu_custom_call" | custom-call | tf_op jit(solution)/shard_map/pallas_call | solution.py:89
  13.3 6.7 %all-to-all-start = ((bf16[8,704,128]{2,1,0:T(8,128)(2,1)}), bf16[8,704,128]{2,1,0:T(8,128)(2,1)S(1)}, u32[]{:S(2)}, u32[]{:S(2)}) async-start(bf16[8,704,128]{2,1,0:T(8,128)(2,1)} %shard_map.95), calls=%async_computation | async-start | bytes 2883584 | tf_op jit(solution)/shard_map/all_to_all | solution.py:424
  22.5 3.1 %collective-permute-start.5 = (bf16[256,512]{1,0:T(8,128)(2,1)S(1)}, bf16[256,512]{1,0:T(8,128)(2,1)S(1)}, u32[]{:S(2)}, u32[]{:S(2)}) collective-permute-start(bf16[256,512]{1,0:T(8,128)(2,1)S(1)} %get-tuple-element.59.refs_0_), channel_id=1, source_target_pairs={{0,12},{4,0},{8,4},{12,8},{1,13},{5,1},{9,5},{13,9},{2,14},{6,2},{... | collective-permute-start | bytes 786440 | tf_op jit(solution)/shard_map/ppermute | solution.py:24
  27.2 3.2 %collective-permute-start.8 = (bf16[256,512]{1,0:T(8,128)(2,1)S(1)}, bf16[256,512]{1,0:T(8,128)(2,1)S(1)}, u32[]{:S(2)}, u32[]{:S(2)}) collective-permute-start(bf16[256,512]{1,0:T(8,128)(2,1)S(1)} %get-tuple-element.60), channel_id=1, source_target_pairs={{0,96},{16,112},{32,0},{48,16},{64,32},{80,48},{96,64},{112,80},{1... | collective-permute-start | bytes 786440 | tf_op jit(solution)/shard_map/ppermute | solution.py:18
  30.4 4.7 %collective-permute-done.5.refs_3_ = bf16[256,512]{1,0:T(8,128)(2,1)S(1)} collective-permute-done((bf16[256,512]{1,0:T(8,128)(2,1)S(1)}, bf16[256,512]{1,0:T(8,128)(2,1)S(1)}, u32[]{:S(2)}, u32[]{:S(2)}) %collective-permute-start.5) | collective-permute-done | bytes 262176 | tf_op jit(solution)/shard_map/ppermute | solution.py:24
  35.1 3.2 %collective-permute-start.7 = (bf16[256,512]{1,0:T(8,128)(2,1)S(1)}, bf16[256,512]{1,0:T(8,128)(2,1)S(1)}, u32[]{:S(2)}, u32[]{:S(2)}) collective-permute-start(bf16[256,512]{1,0:T(8,128)(2,1)S(1)} %get-tuple-element.60), channel_id=1, source_target_pairs={{0,64},{16,80},{32,96},{48,112},{64,0},{80,16},{96,32},{112,48},{1... | collective-permute-start | bytes 786440 | tf_op jit(solution)/shard_map/ppermute | solution.py:18
  39.2 5.7 %collective-permute-done.8 = bf16[256,512]{1,0:T(8,128)(2,1)S(1)} collective-permute-done((bf16[256,512]{1,0:T(8,128)(2,1)S(1)}, bf16[256,512]{1,0:T(8,128)(2,1)S(1)}, u32[]{:S(2)}, u32[]{:S(2)}) %collective-permute-start.8) | collective-permute-done | bytes 262176 | tf_op jit(solution)/shard_map/ppermute | solution.py:18
  53.1 3.0 %collective-permute-start.16 = (bf16[1024,512]{1,0:T(8,128)(2,1)S(1)}, bf16[1024,512]{1,0:T(8,128)(2,1)S(1)}, u32[]{:S(2)}, u32[]{:S(2)}) collective-permute-start(bf16[1024,512]{1,0:T(8,128)(2,1)S(1)} %pad_maximum_fusion.refs_0_), channel_id=1, source_target_pairs={{0,12},{4,0},{8,4},{12,8},{1,13},{5,1},{9,5},{13,9},{2,14},{6,2},{... | collective-permute-start | bytes 3145736 | tf_op jit(solution)/shard_map/ppermute | solution.py:24
  59.4 17.2 %collective-permute-done.16.refs_4_ = bf16[1024,512]{1,0:T(8,128)(2,1)S(1)} collective-permute-done((bf16[1024,512]{1,0:T(8,128)(2,1)S(1)}, bf16[1024,512]{1,0:T(8,128)(2,1)S(1)}, u32[]{:S(2)}, u32[]{:S(2)}) %collective-permute-start.16) | collective-permute-done | bytes 1048608 | tf_op jit(solution)/shard_map/ppermute | solution.py:24
  76.6 3.8 %collective-permute-start.17 = (bf16[512,512]{1,0:T(8,128)(2,1)S(1)}, bf16[512,512]{1,0:T(8,128)(2,1)S(1)}, u32[]{:S(2)}, u32[]{:S(2)}) collective-permute-start(bf16[512,512]{1,0:T(8,128)(2,1)S(1)} %slice.43), channel_id=1, source_target_pairs={{0,12},{4,0},{8,4},{12,8},{1,13},{5,1},{9,5},{13,9},{2,14},{6,2},{... | collective-permute-start | bytes 1572872 | tf_op jit(solution)/shard_map/ppermute | solution.py:24
  83.4 5.2 %collective-permute-done.17.refs_3_ = bf16[512,512]{1,0:T(8,128)(2,1)S(1)} collective-permute-done((bf16[512,512]{1,0:T(8,128)(2,1)S(1)}, bf16[512,512]{1,0:T(8,128)(2,1)S(1)}, u32[]{:S(2)}, u32[]{:S(2)}) %collective-permute-start.17) | collective-permute-done | bytes 524320 | tf_op jit(solution)/shard_map/ppermute | solution.py:24
  88.6 3.5 %collective-permute-done.15.refs_2_ = bf16[512,512]{1,0:T(8,128)(2,1)S(1)} collective-permute-done((bf16[512,512]{1,0:T(8,128)(2,1)S(1)}, bf16[512,512]{1,0:T(8,128)(2,1)S(1)}, u32[]{:S(2)}, u32[]{:S(2)}) %collective-permute-start.15) | collective-permute-done | bytes 524320 | tf_op jit(solution)/shard_map/ppermute | solution.py:24
  92.1 3.6 %shard_map.96 = (bf16[4,128,384]{2,1,0:T(8,128)(2,1)S(1)}, bf16[4,128,384]{2,1,0:T(8,128)(2,1)S(1)}) custom-call(bf16[1024,512]{1,0:T(8,128)(2,1)S(1)} %pad_maximum_fusion.refs_0_, bf16[1024,512]{1,0:T(8,128)(2,1)S(1)} %collective-permute-done.14.refs_1_, bf16[512,512]{1,0:T(8,128)(2,1)S(1)} %collective-permute-done.15.refs_2_, ...), custom_call_target="tpu_custom_call" | custom-call | tf_op jit(solution)/shard_map/pallas_call | solution.py:121
  98.6 4.0 %shard_map.98 = (bf16[4,128,768]{2,1,0:T(8,128)(2,1)S(1)}, bf16[4,128,768]{2,1,0:T(8,128)(2,1)S(1)}) custom-call(bf16[256,2048]{1,0:T(8,128)(2,1)S(1)} %shard_map.94.refs_0_, bf16[256,2048]{1,0:T(8,128)(2,1)S(1)} %collective-permute-done.10.refs_1_, bf16[128,2048]{1,0:T(8,128)(2,1)S(1)} %collective-permute-done.11.refs_2_, ...), custom_call_target="tpu_custom_call" | custom-call | tf_op jit(solution)/shard_map/pallas_call | solution.py:121
  109.2 3.7 %shard_map.100 = (bf16[8,704,128]{2,1,0:T(8,128)(2,1)S(1)}, bf16[8,704,128]{2,1,0:T(8,128)(2,1)S(1)}) custom-call(bf16[256,2048]{1,0:T(8,128)(2,1)S(1)} %shard_map.94.refs_0_, bf16[256,2048]{1,0:T(8,128)(2,1)S(1)} %collective-permute-done.10.refs_1_, bf16[128,2048]{1,0:T(8,128)(2,1)S(1)} %collective-permute-done.11.refs_2_, ...), custom_call_target="tpu_custom_call" | custom-call | tf_op jit(solution)/shard_map/pallas_call | solution.py:121
  112.9 4.6 %shard_map.101 = (bf16[256,2048]{1,0:T(8,128)(2,1)S(1)}, bf16[256,2048]{1,0:T(8,128)(2,1)}, bf16[128,2048]{1,0:T(8,128)(2,1)S(1)}, bf16[128,2048]{1,0:T(8,128)(2,1)S(1)}, bf16[256,2048]{1,0:T(8,128)(2,1)}) custom-call(bf16[4,128,1152]{2,1,0:T(8,128)(2,1)S(1)} %shard_map.99.refs_5_.refs_0_, bf16[4,128,1152]{2,1,0:T(8,128)(2,1)S(1)} %collective-permute-done.21.refs_6_.refs_1_, ...), custom_call_target="tpu_custom_call" | custom-call | tf_op jit(solution)/shard_map/pallas_call | solution.py:121
  121.8 4.8 %shard_map.102 = (bf16[1024,512]{1,0:T(8,128)(2,1)S(1)}, bf16[1024,512]{1,0:T(8,128)(2,1)S(1)}, bf16[1024,512]{1,0:T(8,128)(2,1)}, bf16[1024,512]{1,0:T(8,128)(2,1)S(1)}) custom-call(bf16[4,128,1152]{2,1,0:T(8,128)(2,1)S(1)} %shard_map.99.refs_5_.refs_0_, bf16[4,128,1152]{2,1,0:T(8,128)(2,1)S(1)} %collective-permute-done.21.refs_6_.refs_1_, ...), custom_call_target="tpu_custom_call" | custom-call | tf_op jit(solution)/shard_map/pallas_call | solution.py:121
  128.7 4.3 %collective-permute-done.22 = bf16[128,2048]{1,0:T(8,128)(2,1)S(1)} collective-permute-done((bf16[128,2048]{1,0:T(8,128)(2,1)S(1)}, bf16[128,2048]{1,0:T(8,128)(2,1)S(1)}, u32[]{:S(2)}, u32[]{:S(2)}) %collective-permute-start.22) | collective-permute-done | bytes 524320 | tf_op jit(solution)/shard_map/ppermute | solution.py:18
  137.0 3.2 %collective-permute-start.25 = (bf16[256,2048]{1,0:T(8,128)(2,1)}, bf16[256,2048]{1,0:T(8,128)(2,1)}, u32[]{:S(2)}, u32[]{:S(2)}) collective-permute-start(bf16[256,2048]{1,0:T(8,128)(2,1)} %fusion.1), channel_id=1, source_target_pairs={{0,96},{16,112},{32,0},{48,16},{64,32},{80,48},{96,64},{112,80},{1... | collective-permute-start | bytes 3145736 | tf_op jit(solution)/shard_map/ppermute | solution.py:18
  142.9 8.4 %collective-permute-done.26 = bf16[1024,512]{1,0:T(8,128)(2,1)S(1)} collective-permute-done((bf16[1024,512]{1,0:T(8,128)(2,1)S(1)}, bf16[1024,512]{1,0:T(8,128)(2,1)S(1)}, u32[]{:S(2)}, u32[]{:S(2)}) %collective-permute-start.26) | collective-permute-done | bytes 1048608 | tf_op jit(solution)/shard_map/ppermute | solution.py:24
  154.9 6.2 %all-to-all-start.1 = ((bf16[8,704,128]{2,1,0:T(8,128)(2,1)}), bf16[8,704,128]{2,1,0:T(8,128)(2,1)S(1)}, u32[]{:S(2)}, u32[]{:S(2)}) async-start(bf16[8,704,128]{2,1,0:T(8,128)(2,1)} %add_convert_fusion), calls=%async_computation.1 | async-start | bytes 2883584 | tf_op jit(solution)/shard_map/all_to_all | solution.py:503
  166.4 11.4 %collective-permute-done.28 = bf16[1024,512]{1,0:T(8,128)(2,1)} collective-permute-done((bf16[1024,512]{1,0:T(8,128)(2,1)}, bf16[1024,512]{1,0:T(8,128)(2,1)}, u32[]{:S(2)}, u32[]{:S(2)}) %collective-permute-start.28) | collective-permute-done | bytes 1048608 | tf_op jit(solution)/shard_map/ppermute | solution.py:24
  187.1 5.8 %collective-permute-done.30 = bf16[352,1024]{1,0:T(8,128)(2,1)} collective-permute-done((bf16[352,1024]{1,0:T(8,128)(2,1)}, bf16[352,1024]{1,0:T(8,128)(2,1)}, u32[]{:S(2)}, u32[]{:S(2)}) %collective-permute-start.30) | collective-permute-done | bytes 720928 | tf_op jit(solution)/shard_map/ppermute | solution.py:32
  201.5 3.7 %collective-permute-start.37 = (bf16[128,512]{1,0:T(8,128)(2,1)S(1)}, bf16[128,512]{1,0:T(8,128)(2,1)S(1)}, u32[]{:S(2)}, u32[]{:S(2)}) collective-permute-start(bf16[128,512]{1,0:T(8,128)(2,1)S(1)} %get-tuple-element.101), channel_id=1, source_target_pairs={{0,16},{16,0},{32,48},{48,32},{64,80},{80,64},{96,112},{112,96},{1... | collective-permute-start | bytes 393224 | tf_op jit(solution)/shard_map/ppermute | solution.py:28
  (118 shorter events, 85.6 us)
Async XLA Ops:
  13.3 39.7 %all-to-all-start = ((bf16[8,704,128]{2,1,0:T(8,128)(2,1)}), bf16[8,704,128]{2,1,0:T(8,128)(2,1)S(1)}, u32[]{:S(2)}, u32[]{:S(2)}) async-start(bf16[8,704,128]{2,1,0:T(8,128)(2,1)} %shard_map.95), calls=%async_computation | async-start | bytes 2883584 | tf_op jit(solution)/shard_map/all_to_all | solution.py:424
  20.0 32.2 %collective-permute-start.9 = (bf16[352,1024]{1,0:T(8,128)(2,1)}, bf16[352,1024]{1,0:T(8,128)(2,1)S(1)}, u32[]{:S(2)}, u32[]{:S(2)}) collective-permute-start(bf16[352,1024]{1,0:T(8,128)(2,1)} %refs_2_.1), channel_id=1, source_target_pairs={{0,2},{1,3},{2,0},{3,1},{4,6},{5,7},{6,4},{7,5},{8,10},{9,11},{10,... | collective-permute-start | bytes 2162696 | tf_op jit(solution)/shard_map/ppermute | solution.py:32
  25.6 12.8 %collective-permute-start.4 = (bf16[256,512]{1,0:T(8,128)(2,1)S(1)}, bf16[256,512]{1,0:T(8,128)(2,1)S(1)}, u32[]{:S(2)}, u32[]{:S(2)}) collective-permute-start(bf16[256,512]{1,0:T(8,128)(2,1)S(1)} %get-tuple-element.59.refs_0_), channel_id=1, source_target_pairs={{0,8},{4,12},{8,0},{12,4},{1,9},{5,13},{9,1},{13,5},{2,10},{6,14},... | collective-permute-start | bytes 786440 | tf_op jit(solution)/shard_map/ppermute | solution.py:24
  27.2 17.7 %collective-permute-start.8 = (bf16[256,512]{1,0:T(8,128)(2,1)S(1)}, bf16[256,512]{1,0:T(8,128)(2,1)S(1)}, u32[]{:S(2)}, u32[]{:S(2)}) collective-permute-start(bf16[256,512]{1,0:T(8,128)(2,1)S(1)} %get-tuple-element.60), channel_id=1, source_target_pairs={{0,96},{16,112},{32,0},{48,16},{64,32},{80,48},{96,64},{112,80},{1... | collective-permute-start | bytes 786440 | tf_op jit(solution)/shard_map/ppermute | solution.py:18
  53.1 23.4 %collective-permute-start.16 = (bf16[1024,512]{1,0:T(8,128)(2,1)S(1)}, bf16[1024,512]{1,0:T(8,128)(2,1)S(1)}, u32[]{:S(2)}, u32[]{:S(2)}) collective-permute-start(bf16[1024,512]{1,0:T(8,128)(2,1)S(1)} %pad_maximum_fusion.refs_0_), channel_id=1, source_target_pairs={{0,12},{4,0},{8,4},{12,8},{1,13},{5,1},{9,5},{13,9},{2,14},{6,2},{... | collective-permute-start | bytes 3145736 | tf_op jit(solution)/shard_map/ppermute | solution.py:24
  56.1 24.2 %collective-permute-start.14 = (bf16[1024,512]{1,0:T(8,128)(2,1)S(1)}, bf16[1024,512]{1,0:T(8,128)(2,1)S(1)}, u32[]{:S(2)}, u32[]{:S(2)}) collective-permute-start(bf16[1024,512]{1,0:T(8,128)(2,1)S(1)} %pad_maximum_fusion.refs_0_), channel_id=1, source_target_pairs={{0,4},{4,8},{8,12},{12,0},{1,5},{5,9},{9,13},{13,1},{2,6},{6,10},{... | collective-permute-start | bytes 3145736 | tf_op jit(solution)/shard_map/ppermute | solution.py:24
  56.1 24.4 %collective-permute-start.12 = (bf16[256,2048]{1,0:T(8,128)(2,1)S(1)}, bf16[256,2048]{1,0:T(8,128)(2,1)S(1)}, u32[]{:S(2)}, u32[]{:S(2)}) collective-permute-start(bf16[256,2048]{1,0:T(8,128)(2,1)S(1)} %shard_map.94.refs_0_), channel_id=1, source_target_pairs={{0,96},{16,112},{32,0},{48,16},{64,32},{80,48},{96,64},{112,80},{1... | collective-permute-start | bytes 3145736 | tf_op jit(solution)/shard_map/ppermute | solution.py:18
  59.1 24.2 %collective-permute-start.10 = (bf16[256,2048]{1,0:T(8,128)(2,1)S(1)}, bf16[256,2048]{1,0:T(8,128)(2,1)S(1)}, u32[]{:S(2)}, u32[]{:S(2)}) collective-permute-start(bf16[256,2048]{1,0:T(8,128)(2,1)S(1)} %shard_map.94.refs_0_), channel_id=1, source_target_pairs={{0,32},{16,48},{32,64},{48,80},{64,96},{80,112},{96,0},{112,16},{1... | collective-permute-start | bytes 3145736 | tf_op jit(solution)/shard_map/ppermute | solution.py:18
  59.1 39.5 %collective-permute-start.19 = (bf16[8,704,128]{2,1,0:T(8,128)(2,1)S(1)}, bf16[8,704,128]{2,1,0:T(8,128)(2,1)S(1)}, u32[]{:S(2)}, u32[]{:S(2)}) collective-permute-start(bf16[8,704,128]{2,1,0:T(8,128)(2,1)S(1)} %all-to-all-done.refs_5_.refs_2_), channel_id=1, source_target_pairs={{0,2},{1,3},{2,0},{3,1},{4,6},{5,7},{6,4},{7,5},{8,10},{9,11},{10,... | collective-permute-start | bytes 4325384 | tf_op jit(solution)/shard_map/ppermute | solution.py:32
  80.5 15.5 %collective-permute-start.13 = (bf16[128,2048]{1,0:T(8,128)(2,1)S(1)}, bf16[128,2048]{1,0:T(8,128)(2,1)S(1)}, u32[]{:S(2)}, u32[]{:S(2)}) collective-permute-start(bf16[128,2048]{1,0:T(8,128)(2,1)S(1)} %slice.41), channel_id=1, source_target_pairs={{0,96},{16,112},{32,0},{48,16},{64,32},{80,48},{96,64},{112,80},{1... | collective-permute-start | bytes 1572872 | tf_op jit(solution)/shard_map/ppermute | solution.py:18
  117.6 15.5 %collective-permute-start.22 = (bf16[128,2048]{1,0:T(8,128)(2,1)S(1)}, bf16[128,2048]{1,0:T(8,128)(2,1)S(1)}, u32[]{:S(2)}, u32[]{:S(2)}) collective-permute-start(bf16[128,2048]{1,0:T(8,128)(2,1)S(1)} %get-tuple-element.76), channel_id=1, source_target_pairs={{0,32},{16,48},{32,64},{48,80},{64,96},{80,112},{96,0},{112,16},{1... | collective-permute-start | bytes 1572872 | tf_op jit(solution)/shard_map/ppermute | solution.py:18
  118.8 34.5 %collective-permute-start.29 = (bf16[8,704,128]{2,1,0:T(8,128)(2,1)S(1)}, bf16[8,704,128]{2,1,0:T(8,128)(2,1)S(1)}, u32[]{:S(2)}, u32[]{:S(2)}) collective-permute-start(bf16[8,704,128]{2,1,0:T(8,128)(2,1)S(1)} %get-tuple-element.90), channel_id=1, source_target_pairs={{0,2},{1,3},{2,0},{3,1},{4,6},{5,7},{6,4},{7,5},{8,10},{9,11},{10,... | collective-permute-start | bytes 4325384 | tf_op jit(solution)/shard_map/ppermute | solution.py:32
  119.1 15.9 %collective-permute-start.24 = (bf16[128,2048]{1,0:T(8,128)(2,1)S(1)}, bf16[128,2048]{1,0:T(8,128)(2,1)S(1)}, u32[]{:S(2)}, u32[]{:S(2)}) collective-permute-start(bf16[128,2048]{1,0:T(8,128)(2,1)S(1)} %get-tuple-element.78), channel_id=1, source_target_pairs={{0,96},{16,112},{32,0},{48,16},{64,32},{80,48},{96,64},{112,80},{1... | collective-permute-start | bytes 1572872 | tf_op jit(solution)/shard_map/ppermute | solution.py:18
  126.6 24.7 %collective-permute-start.26 = (bf16[1024,512]{1,0:T(8,128)(2,1)S(1)}, bf16[1024,512]{1,0:T(8,128)(2,1)S(1)}, u32[]{:S(2)}, u32[]{:S(2)}) collective-permute-start(bf16[1024,512]{1,0:T(8,128)(2,1)S(1)} %get-tuple-element.81), channel_id=1, source_target_pairs={{0,12},{4,0},{8,4},{12,8},{1,13},{5,1},{9,5},{13,9},{2,14},{6,2},{... | collective-permute-start | bytes 3145736 | tf_op jit(solution)/shard_map/ppermute | solution.py:24
  127.5 25.3 %collective-permute-start.27 = (bf16[1024,512]{1,0:T(8,128)(2,1)S(1)}, bf16[1024,512]{1,0:T(8,128)(2,1)S(1)}, u32[]{:S(2)}, u32[]{:S(2)}) collective-permute-start(bf16[1024,512]{1,0:T(8,128)(2,1)S(1)} %get-tuple-element.82), channel_id=1, source_target_pairs={{0,4},{4,8},{8,12},{12,0},{1,5},{5,9},{9,13},{13,1},{2,6},{6,10},{... | collective-permute-start | bytes 3145736 | tf_op jit(solution)/shard_map/ppermute | solution.py:24
  135.0 26.7 %collective-permute-start.23 = (bf16[256,2048]{1,0:T(8,128)(2,1)}, bf16[256,2048]{1,0:T(8,128)(2,1)}, u32[]{:S(2)}, u32[]{:S(2)}) collective-permute-start(bf16[256,2048]{1,0:T(8,128)(2,1)} %fusion), channel_id=1, source_target_pairs={{0,32},{16,48},{32,64},{48,80},{64,96},{80,112},{96,0},{112,16},{1... | collective-permute-start | bytes 3145736 | tf_op jit(solution)/shard_map/ppermute | solution.py:18
  137.0 27.1 %collective-permute-start.25 = (bf16[256,2048]{1,0:T(8,128)(2,1)}, bf16[256,2048]{1,0:T(8,128)(2,1)}, u32[]{:S(2)}, u32[]{:S(2)}) collective-permute-start(bf16[256,2048]{1,0:T(8,128)(2,1)} %fusion.1), channel_id=1, source_target_pairs={{0,96},{16,112},{32,0},{48,16},{64,32},{80,48},{96,64},{112,80},{1... | collective-permute-start | bytes 3145736 | tf_op jit(solution)/shard_map/ppermute | solution.py:18
  152.7 25.1 %collective-permute-start.28 = (bf16[1024,512]{1,0:T(8,128)(2,1)}, bf16[1024,512]{1,0:T(8,128)(2,1)}, u32[]{:S(2)}, u32[]{:S(2)}) collective-permute-start(bf16[1024,512]{1,0:T(8,128)(2,1)} %get-tuple-element.84), channel_id=1, source_target_pairs={{0,8},{4,12},{8,0},{12,4},{1,9},{5,13},{9,1},{13,5},{2,10},{6,14},... | collective-permute-start | bytes 3145736 | tf_op jit(solution)/shard_map/ppermute | solution.py:24
  154.9 30.0 %all-to-all-start.1 = ((bf16[8,704,128]{2,1,0:T(8,128)(2,1)}), bf16[8,704,128]{2,1,0:T(8,128)(2,1)S(1)}, u32[]{:S(2)}, u32[]{:S(2)}) async-start(bf16[8,704,128]{2,1,0:T(8,128)(2,1)} %add_convert_fusion), calls=%async_computation.1 | async-start | bytes 2883584 | tf_op jit(solution)/shard_map/all_to_all | solution.py:503
  161.0 31.8 %collective-permute-start.30 = (bf16[352,1024]{1,0:T(8,128)(2,1)}, bf16[352,1024]{1,0:T(8,128)(2,1)}, u32[]{:S(2)}, u32[]{:S(2)}) collective-permute-start(bf16[352,1024]{1,0:T(8,128)(2,1)} %copy-done.10), channel_id=1, source_target_pairs={{0,2},{1,3},{2,0},{3,1},{4,6},{5,7},{6,4},{7,5},{8,10},{9,11},{10,... | collective-permute-start | bytes 2162696 | tf_op jit(solution)/shard_map/ppermute | solution.py:32
  181.6 13.0 %collective-permute-start.31 = (bf16[256,512]{1,0:T(8,128)(2,1)}, bf16[256,512]{1,0:T(8,128)(2,1)S(1)}, u32[]{:S(2)}, u32[]{:S(2)}) collective-permute-start(bf16[256,512]{1,0:T(8,128)(2,1)} %get-tuple-element.96), channel_id=1, source_target_pairs={{0,12},{4,0},{8,4},{12,8},{1,13},{5,1},{9,5},{13,9},{2,14},{6,2},{... | collective-permute-start | bytes 786440 | tf_op jit(solution)/shard_map/ppermute | solution.py:24
  182.3 18.2 %collective-permute-start.32 = (bf16[256,512]{1,0:T(8,128)(2,1)}, bf16[256,512]{1,0:T(8,128)(2,1)S(1)}, u32[]{:S(2)}, u32[]{:S(2)}) collective-permute-start(bf16[256,512]{1,0:T(8,128)(2,1)} %get-tuple-element.97), channel_id=1, source_target_pairs={{0,4},{4,8},{8,12},{12,0},{1,5},{5,9},{9,13},{13,1},{2,6},{6,10},{... | collective-permute-start | bytes 786440 | tf_op jit(solution)/shard_map/ppermute | solution.py:24
  183.7 16.9 %collective-permute-start.33 = (bf16[256,512]{1,0:T(8,128)(2,1)S(1)}, bf16[256,512]{1,0:T(8,128)(2,1)S(1)}, u32[]{:S(2)}, u32[]{:S(2)}) collective-permute-start(bf16[256,512]{1,0:T(8,128)(2,1)S(1)} %get-tuple-element.98), channel_id=1, source_target_pairs={{0,8},{4,12},{8,0},{12,4},{1,9},{5,13},{9,1},{13,5},{2,10},{6,14},... | collective-permute-start | bytes 786440 | tf_op jit(solution)/shard_map/ppermute | solution.py:24
  186.1 14.5 %collective-permute-start.36 = (bf16[256,512]{1,0:T(8,128)(2,1)S(1)}, bf16[256,512]{1,0:T(8,128)(2,1)S(1)}, u32[]{:S(2)}, u32[]{:S(2)}) collective-permute-start(bf16[256,512]{1,0:T(8,128)(2,1)S(1)} %get-tuple-element.109), channel_id=1, source_target_pairs={{0,64},{16,80},{32,96},{48,112},{64,0},{80,16},{96,32},{112,48},{1... | collective-permute-start | bytes 786440 | tf_op jit(solution)/shard_map/ppermute | solution.py:18
  (33 other events, 285.2 us)

commit v3 on v2

--- a/solution.py
+++ b/solution.py
@@ -263,32 +263,37 @@
 
 def near_products(copy, sources, results, tokens, pair):
     features = tokens.shape[1]
-    copies = copy_blocks(copy, sources[5], pair)
-    copies += copy_tokens(copy, [ref.at[:, pl.ds(0, features)] for ref in sources[:5]], tokens)
+    copies = copy_blocks(copy, sources[3], pair)
+    copies += copy_tokens(copy, [ref.at[:, pl.ds(0, features)] for ref in sources[:3]], tokens)
     wait_all(copies)
     results[0][...] = dot(tokens[...], pair[...], 1, 1)
 
 
-def pair_products(copy, sources, results, tokens, pair, share):
+def pair_products(copy, sources, results, tokens, pair, share, opposite, near):
     keep, send = results
     half, width = keep.shape[1], keep.shape[2] // 2
     own = pair.shape[0] // 2
     features = tokens.shape[1]
     copies = copy_blocks(copy, sources[5], pair)
-    far = [ref.at[:, pl.ds(features, features)] for ref in sources[:5]]
-    chunks = copy_tokens(copy, far, tokens)
-    rows = 4 * half
-    shares = [
-        copy(sources[6].at[pl.ds(first, rows)], share.at[pl.ds(first, rows)]) for first in (0, rows)
-    ]
-    wait_all(copies)
+    chunks = copy_tokens(
+        copy, [ref.at[:, pl.ds(features, features)] for ref in sources[:5]], tokens
+    )
+    chunks.append(copy(sources[6], share))
+    later = copy_blocks(copy, sources[7], near)
+    later += copy_tokens(
+        copy, [ref.at[:, pl.ds(0, features)] for ref in sources[2:4]], opposite
+    )
+    wait_all(copies + chunks)
     padding = jnp.zeros((half, width - own), BF16)
-    for i, arrived in ((0, chunks[:2]), (2, chunks[2:])):
-        here = pl.ds(2 * i * half, rows)
-        wait_all(arrived)
-        part = dot(tokens[here], pair[...], 1, 1)
-        shares[i // 2].wait()
-        part = (part + share[here]).astype(BF16)
+    for i in (0, 2):
+        part = dot(tokens[pl.ds(2 * i * half, 4 * half)], pair[...], 1, 1)
+        if i == 0:
+            part = part + share[pl.ds(0, 4 * half)]
+        else:
+            wait_all(later)
+            first = part[: 2 * half] + dot(opposite[...], near[...], 1, 1)
+            part = jnp.concatenate([first, part[2 * half :] + share[pl.ds(4 * half, 2 * half)]])
+        part = part.astype(BF16)
         for j in (0, 1):
             for out, at in ((keep, 2 * j * half), (send, (2 * j + 1) * half)):
                 piece = part[at : at + half]
@@ -297,15 +302,39 @@
                     out[i + j, :, k * width + own : (k + 1) * width] = padding
 
 
-def hidden_products(copy, sources, results, grads, down):
+def copy_down_blocks(copy, near, far, blocks, held):
+    count = held.shape[1] // (2 * len(blocks))
+    return [
+        copy(
+            ref.at[:, feature_block(k, count)],
+            held.at[:, pl.ds((2 * i + side) * count, count)],
+        )
+        for i, k in enumerate(blocks)
+        for side, ref in enumerate((near, far))
+    ]
+
+
+def early_hidden_products(copy, sources, results, grads, down):
+    columns = sources[0].shape[1]
+    copies = copy_down_blocks(copy, *sources[3:], (0, 1, 3), down)
+    copies += [
+        copy(ref, grads.at[:, pl.ds(i * columns, columns)]) for i, ref in enumerate(sources[:3])
+    ]
+    wait_all(copies)
+    results[0][...] = dot(grads[...], down[...], 1, 1)
+
+
+def hidden_products(copy, sources, results, grads, down, share):
     keep, send = results
     half, width = keep.shape[1:]
     own = down.shape[0]
-    copies = copy_down(copy, *sources[5:], down)
-    wait_all(copies + copy_grads(copy, sources[:5], grads))
+    copies = copy_down_blocks(copy, *sources[2:4], (2,), down)
+    copies += copy_tokens(copy, sources[:2], grads)
+    wait_all(copies + [copy(sources[4], share)])
     padding = jnp.zeros((half, width - own), BF16)
     for i in (0, 2):
-        part = dot(grads[pl.ds(2 * i * half, 4 * half)], down[...], 1, 1).astype(BF16)
+        here = pl.ds(2 * i * half, 4 * half)
+        part = (dot(grads[here], down[...], 1, 1) + share[here]).astype(BF16)
         for j in (0, 1):
             for out, at in ((keep, 2 * j * half), (send, (2 * j + 1) * half)):
                 out[i + j, :, :own] = part[at : at + half]
@@ -352,16 +381,15 @@
             out[:, side * count : (side + 1) * count] = part.astype(BF16)
 
 
-def pair_gradients(scale, copy, sources, results, tokens, acts):
-    copies = copy_tokens(copy, sources[:5], tokens)
+def pair_gradients(scale, side, copy, sources, results, tokens, acts):
+    groups, both, count = results[0].shape
+    features = groups * count
+    columns = [ref.at[:, pl.ds(side * features, features)] for ref in sources[:5]]
+    copies = copy_tokens(copy, columns, tokens)
     wait_all(copies + copy_part(copy, *sources[5:], acts.shape[1] // 2, acts))
-    near, far = results
-    groups, both, count = near.shape
-    features = groups * count
-    for out, first in ((far, features), (near, 0)):
-        total = dot(acts[:, :both], tokens[:, pl.ds(first, features)], 0, 0) * scale
-        for g in range(groups):
-            out[g] = total[:, g * count : (g + 1) * count].astype(BF16)
+    total = dot(acts[:, :both], tokens[...], 0, 0) * scale
+    for g in range(groups):
+        results[0][g] = total[:, g * count : (g + 1) * count].astype(BF16)
 
 
 def down_gradients(scale, copy, sources, results, grads, hidden):
@@ -435,29 +463,38 @@
 
     all_tokens, all_features = 8 * rows, 2 * features
     whole = (all_tokens, all_features)
+    (share,) = assembled_call(
+        near_products,
+        [(6 * rows, 2 * own)],
+        [t_all[0], t_all[1], t_all[4], w_near],
+        [(6 * rows, features), (2 * own, features)],
+        11,
+        dtype=F32,
+    )
+    half_features = (all_tokens, features)
+    (early,) = assembled_call(
+        early_hidden_products,
+        [(all_tokens, own)],
+        [g_all[0], g_all[1], g_all[4], d_near, d_far],
+        [(all_tokens, 3 * columns), (own, 3 * columns)],
+        9,
+        dtype=F32,
+    )
     keep_hidden, send_hidden = assembled_call(
         hidden_products,
         [(4, rows, width)] * 2,
-        [*g_all, d_near, d_far],
-        [whole, (own, all_features)],
-        12,
+        [g_all[2], after(g_all[3], share), d_near, d_far, early],
+        [(all_tokens, columns), (own, columns), ((all_tokens, own), F32)],
+        5,
     )
     got_hidden = swap_core(send_hidden)
-    half_features = (all_tokens, features)
-    (share,) = assembled_call(
-        near_products,
-        [(all_tokens, 2 * own)],
-        [*t_all, w_near],
-        [half_features, (2 * own, features)],
-        13,
-        dtype=F32,
-    )
+    weights = (2 * own, features)
     keep, send = assembled_call(
         pair_products,
         [(4, rows, 2 * width)] * 2,
-        [*t_all[:4], after(t_all[4], got_hidden), w_far, share],
-        [half_features, (2 * own, features), ((all_tokens, 2 * own), F32)],
-        15,
+        [*t_all[:4], after(t_all[4], keep_hidden), w_far, share, w_near],
+        [half_features, weights, ((6 * rows, 2 * own), F32), (2 * rows, features), weights],
+        24,
     )
     (mine,) = local_call(
         functools.partial(activate, own),
@@ -466,14 +503,17 @@
     )
     both = [mine, swap_core(mine)]
 
-    near, far = assembled_call(
-        functools.partial(pair_gradients, loss_scale),
-        [(8, 2 * own, rows_in)] * 2,
-        [*t_all, *both],
-        [whole, (all_tokens, 2 * width)],
-        13,
-    )
-    both[1] = after(both[1], near)
+    def pair_gradient(side):
+        return assembled_call(
+            functools.partial(pair_gradients, loss_scale, side),
+            [(8, 2 * own, rows_in)],
+            [*t_all, *both],
+            [half_features, (all_tokens, 2 * width)],
+            13,
+        )[0]
+
+    far = pair_gradient(1)
+    both[1] = after(both[1], far)
     output_parts = assembled_call(
         output_products,
         [(size * rows, all_features) for size in (2, 2, 1, 1, 2)],
@@ -490,6 +530,7 @@
         24,
     )
     both[1] = after(both[1], input_parts[2])
+    near = pair_gradient(0)
     down_near, down_far = assembled_call(
         functools.partial(down_gradients, loss_scale),
         [(own, features)] * 2,

time: 214 us -> 210 us (0.981)
  waiting for transfers between devices: 88.1 us -> 84.8 us
  starting transfers between devices: 67.9 us -> 65 us
    ppermute x13, waiting for transfers between devices: 52 us -> 46.4 us  [shift_y(): return lax.ppermute(array, 'gy', [(i, (i + steps) % 4) for i in range(4)])]
    pallas_call x7 -> x9, Pallas kernels: 25.9 us -> 27.5 us  [assembled_call(): pl.pallas_call(body, out_shape=[jax.ShapeDtypeStruct(shape, dtype) for sh...]
    unnamed x30 -> x32, local copies, waits for them, and re-layouts: 4.92 us -> 5.93 us
  transfers between devices with their start and end apart: 42 -> 42, of which waited for: 22 -> 21; matrix products, arithmetic and copies ran while one was open for 7% -> 6% of each run, Pallas kernels for 10% -> 11%
where the time goes in v3:
time: 210 us; the launch traced here: 208 us
  waiting for transfers between devices  84.8 us (40%)
  starting transfers between devices  65 us (31%)
  Pallas kernels  38.5 us (18%)
  other arithmetic  11.6 us (6%)
  local copies, waits for them, and re-layouts  7.34 us (3%)
    ppermute x13, waiting for transfers between devices, shift_y(): return lax.ppermute(array, 'gy', [(i, (i + steps) % 4) for i in range(4)])  46.4 us
    pallas_call x9, Pallas kernels, assembled_call(): pl.pallas_call(body, out_shape=[jax.ShapeDtypeStruct(shape, dtype) for sh...  27.5 us
    ppermute x14, starting transfers between devices, shift_z(): lax.ppermute(array, 'gx', [(i, (i // 2 + steps) % 4 * 2 + i % 2) for i in...  23.1 us
    ppermute x14, waiting for transfers between devices, shift_z(): lax.ppermute(array, 'gx', [(i, (i // 2 + steps) % 4 * 2 + i % 2) for i in...  19 us
    ppermute x13, starting transfers between devices, shift_y(): return lax.ppermute(array, 'gy', [(i, (i + steps) % 4) for i in range(4)])  16.9 us
    pallas_call x9, Pallas kernels, local_call(): pl.pallas_call(body, out_shape=[jax.ShapeDtypeStruct(shape, BF16) for sha...  11 us
    ppermute x6, waiting for transfers between devices, swap_x_lo(): return lax.ppermute(array, 'gz', [(i, i ^ 2) for i in range(4)])  10.4 us
    all_to_all x1, starting transfers between devices, on_device(): w_near = lax.all_to_all(after(pieces, *four), 'gx', 0, 0, tiled=True)  6.69 us
  transfers between devices with their start and end apart: 42, of which 21 were waited for; matrix products, arithmetic and copies ran while one was open for 6% of the time, Pallas kernels for 11%

profile of v3, /device:TPU:0, one launch (start us, length us, event | category | flops | bytes accessed | tf_op | source)
XLA Modules:
  0.0 208.5 jit_solution(10773692369237531199)
XLA Ops:
  9.8 3.2 %shard_map.95 = bf16[8,704,128]{2,1,0:T(8,128)(2,1)} custom-call(bf16[128,2816]{1,0:T(8,128)(2,1)S(1)} %copy-done.8, bf16[128,2816]{1,0:T(8,128)(2,1)S(1)} %copy-done.9), custom_call_target="tpu_custom_call" | custom-call | tf_op jit(solution)/shard_map/pallas_call | solution.py:89
  13.3 6.7 %all-to-all-start = ((bf16[8,704,128]{2,1,0:T(8,128)(2,1)}), bf16[8,704,128]{2,1,0:T(8,128)(2,1)S(1)}, u32[]{:S(2)}, u32[]{:S(2)}) async-start(bf16[8,704,128]{2,1,0:T(8,128)(2,1)} %shard_map.95), calls=%async_computation | async-start | bytes 2883584 | tf_op jit(solution)/shard_map/all_to_all | solution.py:452
  22.5 3.1 %collective-permute-start.5 = (bf16[256,512]{1,0:T(8,128)(2,1)S(1)}, bf16[256,512]{1,0:T(8,128)(2,1)S(1)}, u32[]{:S(2)}, u32[]{:S(2)}) collective-permute-start(bf16[256,512]{1,0:T(8,128)(2,1)S(1)} %get-tuple-element.58.refs_0_), channel_id=1, source_target_pairs={{0,12},{4,0},{8,4},{12,8},{1,13},{5,1},{9,5},{13,9},{2,14},{6,2},{... | collective-permute-start | bytes 786440 | tf_op jit(solution)/shard_map/ppermute | solution.py:24
  27.2 3.2 %collective-permute-start.8 = (bf16[256,512]{1,0:T(8,128)(2,1)S(1)}, bf16[256,512]{1,0:T(8,128)(2,1)S(1)}, u32[]{:S(2)}, u32[]{:S(2)}) collective-permute-start(bf16[256,512]{1,0:T(8,128)(2,1)S(1)} %get-tuple-element.59), channel_id=1, source_target_pairs={{0,96},{16,112},{32,0},{48,16},{64,32},{80,48},{96,64},{112,80},{1... | collective-permute-start | bytes 786440 | tf_op jit(solution)/shard_map/ppermute | solution.py:18
  30.4 4.7 %collective-permute-done.5.refs_3_ = bf16[256,512]{1,0:T(8,128)(2,1)S(1)} collective-permute-done((bf16[256,512]{1,0:T(8,128)(2,1)S(1)}, bf16[256,512]{1,0:T(8,128)(2,1)S(1)}, u32[]{:S(2)}, u32[]{:S(2)}) %collective-permute-start.5) | collective-permute-done | bytes 262176 | tf_op jit(solution)/shard_map/ppermute | solution.py:24
  35.1 3.2 %collective-permute-start.7 = (bf16[256,512]{1,0:T(8,128)(2,1)S(1)}, bf16[256,512]{1,0:T(8,128)(2,1)S(1)}, u32[]{:S(2)}, u32[]{:S(2)}) collective-permute-start(bf16[256,512]{1,0:T(8,128)(2,1)S(1)} %get-tuple-element.59), channel_id=1, source_target_pairs={{0,64},{16,80},{32,96},{48,112},{64,0},{80,16},{96,32},{112,48},{1... | collective-permute-start | bytes 786440 | tf_op jit(solution)/shard_map/ppermute | solution.py:18
  39.2 5.7 %collective-permute-done.8 = bf16[256,512]{1,0:T(8,128)(2,1)S(1)} collective-permute-done((bf16[256,512]{1,0:T(8,128)(2,1)S(1)}, bf16[256,512]{1,0:T(8,128)(2,1)S(1)}, u32[]{:S(2)}, u32[]{:S(2)}) %collective-permute-start.8) | collective-permute-done | bytes 262176 | tf_op jit(solution)/shard_map/ppermute | solution.py:18
  53.1 3.0 %collective-permute-start.16 = (bf16[1024,512]{1,0:T(8,128)(2,1)S(1)}, bf16[1024,512]{1,0:T(8,128)(2,1)S(1)}, u32[]{:S(2)}, u32[]{:S(2)}) collective-permute-start(bf16[1024,512]{1,0:T(8,128)(2,1)S(1)} %pad_maximum_fusion.refs_0_), channel_id=1, source_target_pairs={{0,12},{4,0},{8,4},{12,8},{1,13},{5,1},{9,5},{13,9},{2,14},{6,2},{... | collective-permute-start | bytes 3145736 | tf_op jit(solution)/shard_map/ppermute | solution.py:24
  59.4 17.2 %collective-permute-done.16.refs_2_.refs_4_ = bf16[1024,512]{1,0:T(8,128)(2,1)S(1)} collective-permute-done((bf16[1024,512]{1,0:T(8,128)(2,1)S(1)}, bf16[1024,512]{1,0:T(8,128)(2,1)S(1)}, u32[]{:S(2)}, u32[]{:S(2)}) %collective-permute-start.16) | collective-permute-done | bytes 1048608 | tf_op jit(solution)/shard_map/ppermute | solution.py:24
  76.6 3.8 %collective-permute-start.17 = (bf16[512,512]{1,0:T(8,128)(2,1)S(1)}, bf16[512,512]{1,0:T(8,128)(2,1)S(1)}, u32[]{:S(2)}, u32[]{:S(2)}) collective-permute-start(bf16[512,512]{1,0:T(8,128)(2,1)S(1)} %slice.43), channel_id=1, source_target_pairs={{0,12},{4,0},{8,4},{12,8},{1,13},{5,1},{9,5},{13,9},{2,14},{6,2},{... | collective-permute-start | bytes 1572872 | tf_op jit(solution)/shard_map/ppermute | solution.py:24
  85.7 3.0 %shard_map.97.refs_4_ = f32[1024,352]{1,0:T(8,128)S(1)} custom-call(bf16[1024,512]{1,0:T(8,128)(2,1)S(1)} %pad_maximum_fusion.refs_0_, bf16[1024,512]{1,0:T(8,128)(2,1)S(1)} %collective-permute-done.14.refs_1_, bf16[1024,512]{1,0:T(8,128)(2,1)S(1)} %collective-permute-done.16.refs_2_.refs_4_, bf16[352,1024]{1,0:T(8,128)(2,1)} %refs_2_.3, ...), custom_call_target="tpu_custom_call" | custom-call | tf_op jit(solution)/shard_map/pallas_call | solution.py:121
  88.7 3.4 %collective-permute-done.15.refs_0_.refs_2_ = bf16[512,512]{1,0:T(8,128)(2,1)S(1)} collective-permute-done((bf16[512,512]{1,0:T(8,128)(2,1)S(1)}, bf16[512,512]{1,0:T(8,128)(2,1)S(1)}, u32[]{:S(2)}, u32[]{:S(2)}) %collective-permute-start.15) | collective-permute-done | bytes 524320 | tf_op jit(solution)/shard_map/ppermute | solution.py:24
  94.7 4.3 %shard_map.99 = (bf16[4,128,768]{2,1,0:T(8,128)(2,1)S(1)}, bf16[4,128,768]{2,1,0:T(8,128)(2,1)S(1)}) custom-call(bf16[256,2048]{1,0:T(8,128)(2,1)S(1)} %shard_map.94.refs_0_, bf16[256,2048]{1,0:T(8,128)(2,1)S(1)} %collective-permute-done.10.refs_1_, bf16[128,2048]{1,0:T(8,128)(2,1)S(1)} %collective-permute-done.11.refs_2_, ...), custom_call_target="tpu_custom_call" | custom-call | tf_op jit(solution)/shard_map/pallas_call | solution.py:121
  108.2 4.6 %shard_map.102 = (bf16[256,2048]{1,0:T(8,128)(2,1)S(1)}, bf16[256,2048]{1,0:T(8,128)(2,1)}, bf16[128,2048]{1,0:T(8,128)(2,1)S(1)}, bf16[128,2048]{1,0:T(8,128)(2,1)S(1)}, bf16[256,2048]{1,0:T(8,128)(2,1)}) custom-call(bf16[4,128,1152]{2,1,0:T(8,128)(2,1)S(1)} %shard_map.100.refs_5_.refs_0_, ...), custom_call_target="tpu_custom_call" | custom-call | tf_op jit(solution)/shard_map/pallas_call | solution.py:121
  117.4 4.8 %shard_map.103 = (bf16[1024,512]{1,0:T(8,128)(2,1)S(1)}, bf16[1024,512]{1,0:T(8,128)(2,1)S(1)}, bf16[1024,512]{1,0:T(8,128)(2,1)}, bf16[1024,512]{1,0:T(8,128)(2,1)S(1)}) custom-call(bf16[4,128,1152]{2,1,0:T(8,128)(2,1)S(1)} %shard_map.100.refs_5_.refs_0_, bf16[4,128,1152]{2,1,0:T(8,128)(2,1)S(1)} %collective-permute-done.21.refs_6_.refs_1_, ...), custom_call_target="tpu_custom_call" | custom-call | tf_op jit(solution)/shard_map/pallas_call | solution.py:121
  125.2 3.8 %collective-permute-done.22 = bf16[128,2048]{1,0:T(8,128)(2,1)S(1)} collective-permute-done((bf16[128,2048]{1,0:T(8,128)(2,1)S(1)}, bf16[128,2048]{1,0:T(8,128)(2,1)S(1)}, u32[]{:S(2)}, u32[]{:S(2)}) %collective-permute-start.22) | collective-permute-done | bytes 524320 | tf_op jit(solution)/shard_map/ppermute | solution.py:18
  133.0 3.2 %collective-permute-start.25 = (bf16[256,2048]{1,0:T(8,128)(2,1)}, bf16[256,2048]{1,0:T(8,128)(2,1)}, u32[]{:S(2)}, u32[]{:S(2)}) collective-permute-start(bf16[256,2048]{1,0:T(8,128)(2,1)} %fusion.1), channel_id=1, source_target_pairs={{0,96},{16,112},{32,0},{48,16},{64,32},{80,48},{96,64},{112,80},{1... | collective-permute-start | bytes 3145736 | tf_op jit(solution)/shard_map/ppermute | solution.py:18
  141.1 6.0 %collective-permute-done.26 = bf16[1024,512]{1,0:T(8,128)(2,1)S(1)} collective-permute-done((bf16[1024,512]{1,0:T(8,128)(2,1)S(1)}, bf16[1024,512]{1,0:T(8,128)(2,1)S(1)}, u32[]{:S(2)}, u32[]{:S(2)}) %collective-permute-start.26) | collective-permute-done | bytes 1048608 | tf_op jit(solution)/shard_map/ppermute | solution.py:24
  147.1 3.4 %collective-permute-done.27 = bf16[1024,512]{1,0:T(8,128)(2,1)S(1)} collective-permute-done((bf16[1024,512]{1,0:T(8,128)(2,1)S(1)}, bf16[1024,512]{1,0:T(8,128)(2,1)S(1)}, u32[]{:S(2)}, u32[]{:S(2)}) %collective-permute-start.27) | collective-permute-done | bytes 1048608 | tf_op jit(solution)/shard_map/ppermute | solution.py:24
  152.1 5.0 %all-to-all-start.1 = ((bf16[8,704,128]{2,1,0:T(8,128)(2,1)}), bf16[8,704,128]{2,1,0:T(8,128)(2,1)S(1)}, u32[]{:S(2)}, u32[]{:S(2)}) async-start(bf16[8,704,128]{2,1,0:T(8,128)(2,1)} %add_convert_fusion), calls=%async_computation.1 | async-start | bytes 2883584 | tf_op jit(solution)/shard_map/all_to_all | solution.py:544
  158.2 3.5 %collective-permute-done.25 = bf16[256,2048]{1,0:T(8,128)(2,1)} collective-permute-done((bf16[256,2048]{1,0:T(8,128)(2,1)}, bf16[256,2048]{1,0:T(8,128)(2,1)}, u32[]{:S(2)}, u32[]{:S(2)}) %collective-permute-start.25) | collective-permute-done | bytes 1048608 | tf_op jit(solution)/shard_map/ppermute | solution.py:18
  163.9 11.6 %collective-permute-done.28 = bf16[1024,512]{1,0:T(8,128)(2,1)S(1)} collective-permute-done((bf16[1024,512]{1,0:T(8,128)(2,1)}, bf16[1024,512]{1,0:T(8,128)(2,1)S(1)}, u32[]{:S(2)}, u32[]{:S(2)}) %collective-permute-start.28) | collective-permute-done | bytes 1048608 | tf_op jit(solution)/shard_map/ppermute | solution.py:24
  182.1 6.0 %collective-permute-done.30 = bf16[352,1024]{1,0:T(8,128)(2,1)} collective-permute-done((bf16[352,1024]{1,0:T(8,128)(2,1)}, bf16[352,1024]{1,0:T(8,128)(2,1)}, u32[]{:S(2)}, u32[]{:S(2)}) %collective-permute-start.30) | collective-permute-done | bytes 720928 | tf_op jit(solution)/shard_map/ppermute | solution.py:32
  196.8 3.7 %collective-permute-start.37 = (bf16[128,512]{1,0:T(8,128)(2,1)S(1)}, bf16[128,512]{1,0:T(8,128)(2,1)S(1)}, u32[]{:S(2)}, u32[]{:S(2)}) collective-permute-start(bf16[128,512]{1,0:T(8,128)(2,1)S(1)} %get-tuple-element.99), channel_id=1, source_target_pairs={{0,16},{16,0},{32,48},{48,32},{64,80},{80,64},{96,112},{112,96},{1... | collective-permute-start | bytes 393224 | tf_op jit(solution)/shard_map/ppermute | solution.py:28
  (122 shorter events, 87.1 us)
Async XLA Ops:
  13.3 39.7 %all-to-all-start = ((bf16[8,704,128]{2,1,0:T(8,128)(2,1)}), bf16[8,704,128]{2,1,0:T(8,128)(2,1)S(1)}, u32[]{:S(2)}, u32[]{:S(2)}) async-start(bf16[8,704,128]{2,1,0:T(8,128)(2,1)} %shard_map.95), calls=%async_computation | async-start | bytes 2883584 | tf_op jit(solution)/shard_map/all_to_all | solution.py:452
  20.0 32.2 %collective-permute-start.9 = (bf16[352,1024]{1,0:T(8,128)(2,1)}, bf16[352,1024]{1,0:T(8,128)(2,1)S(1)}, u32[]{:S(2)}, u32[]{:S(2)}) collective-permute-start(bf16[352,1024]{1,0:T(8,128)(2,1)} %refs_2_.3), channel_id=1, source_target_pairs={{0,2},{1,3},{2,0},{3,1},{4,6},{5,7},{6,4},{7,5},{8,10},{9,11},{10,... | collective-permute-start | bytes 2162696 | tf_op jit(solution)/shard_map/ppermute | solution.py:32
  25.6 12.8 %collective-permute-start.4 = (bf16[256,512]{1,0:T(8,128)(2,1)S(1)}, bf16[256,512]{1,0:T(8,128)(2,1)S(1)}, u32[]{:S(2)}, u32[]{:S(2)}) collective-permute-start(bf16[256,512]{1,0:T(8,128)(2,1)S(1)} %get-tuple-element.58.refs_0_), channel_id=1, source_target_pairs={{0,8},{4,12},{8,0},{12,4},{1,9},{5,13},{9,1},{13,5},{2,10},{6,14},... | collective-permute-start | bytes 786440 | tf_op jit(solution)/shard_map/ppermute | solution.py:24
  26.2 12.8 %collective-permute-start.3 = (bf16[256,512]{1,0:T(8,128)(2,1)S(1)}, bf16[256,512]{1,0:T(8,128)(2,1)S(1)}, u32[]{:S(2)}, u32[]{:S(2)}) collective-permute-start(bf16[256,512]{1,0:T(8,128)(2,1)S(1)} %get-tuple-element.58.refs_0_), channel_id=1, source_target_pairs={{0,4},{4,8},{8,12},{12,0},{1,5},{5,9},{9,13},{13,1},{2,6},{6,10},{... | collective-permute-start | bytes 786440 | tf_op jit(solution)/shard_map/ppermute | solution.py:24
  27.2 17.7 %collective-permute-start.8 = (bf16[256,512]{1,0:T(8,128)(2,1)S(1)}, bf16[256,512]{1,0:T(8,128)(2,1)S(1)}, u32[]{:S(2)}, u32[]{:S(2)}) collective-permute-start(bf16[256,512]{1,0:T(8,128)(2,1)S(1)} %get-tuple-element.59), channel_id=1, source_target_pairs={{0,96},{16,112},{32,0},{48,16},{64,32},{80,48},{96,64},{112,80},{1... | collective-permute-start | bytes 786440 | tf_op jit(solution)/shard_map/ppermute | solution.py:18
  53.1 23.4 %collective-permute-start.16 = (bf16[1024,512]{1,0:T(8,128)(2,1)S(1)}, bf16[1024,512]{1,0:T(8,128)(2,1)S(1)}, u32[]{:S(2)}, u32[]{:S(2)}) collective-permute-start(bf16[1024,512]{1,0:T(8,128)(2,1)S(1)} %pad_maximum_fusion.refs_0_), channel_id=1, source_target_pairs={{0,12},{4,0},{8,4},{12,8},{1,13},{5,1},{9,5},{13,9},{2,14},{6,2},{... | collective-permute-start | bytes 3145736 | tf_op jit(solution)/shard_map/ppermute | solution.py:24
  56.1 24.2 %collective-permute-start.14 = (bf16[1024,512]{1,0:T(8,128)(2,1)S(1)}, bf16[1024,512]{1,0:T(8,128)(2,1)S(1)}, u32[]{:S(2)}, u32[]{:S(2)}) collective-permute-start(bf16[1024,512]{1,0:T(8,128)(2,1)S(1)} %pad_maximum_fusion.refs_0_), channel_id=1, source_target_pairs={{0,4},{4,8},{8,12},{12,0},{1,5},{5,9},{9,13},{13,1},{2,6},{6,10},{... | collective-permute-start | bytes 3145736 | tf_op jit(solution)/shard_map/ppermute | solution.py:24
  56.1 24.4 %collective-permute-start.12 = (bf16[256,2048]{1,0:T(8,128)(2,1)S(1)}, bf16[256,2048]{1,0:T(8,128)(2,1)S(1)}, u32[]{:S(2)}, u32[]{:S(2)}) collective-permute-start(bf16[256,2048]{1,0:T(8,128)(2,1)S(1)} %shard_map.94.refs_0_), channel_id=1, source_target_pairs={{0,96},{16,112},{32,0},{48,16},{64,32},{80,48},{96,64},{112,80},{1... | collective-permute-start | bytes 3145736 | tf_op jit(solution)/shard_map/ppermute | solution.py:18
  59.0 24.2 %collective-permute-start.10 = (bf16[256,2048]{1,0:T(8,128)(2,1)S(1)}, bf16[256,2048]{1,0:T(8,128)(2,1)S(1)}, u32[]{:S(2)}, u32[]{:S(2)}) collective-permute-start(bf16[256,2048]{1,0:T(8,128)(2,1)S(1)} %shard_map.94.refs_0_), channel_id=1, source_target_pairs={{0,32},{16,48},{32,64},{48,80},{64,96},{80,112},{96,0},{112,16},{1... | collective-permute-start | bytes 3145736 | tf_op jit(solution)/shard_map/ppermute | solution.py:18
  59.1 34.8 %collective-permute-start.18 = (bf16[8,704,128]{2,1,0:T(8,128)(2,1)S(1)}, bf16[8,704,128]{2,1,0:T(8,128)(2,1)S(1)}, u32[]{:S(2)}, u32[]{:S(2)}) collective-permute-start(bf16[8,704,128]{2,1,0:T(8,128)(2,1)S(1)} %all-to-all-done.refs_3_.refs_7_.refs_2_), channel_id=1, source_target_pairs={{0,2},{1,3},{2,0},{3,1},{4,6},{5,7},{6,4},{7,5},{8,10},{9,11},{10,... | collective-permute-start | bytes 4325384 | tf_op jit(solution)/shard_map/ppermute | solution.py:32
  80.5 13.3 %collective-permute-start.13 = (bf16[128,2048]{1,0:T(8,128)(2,1)S(1)}, bf16[128,2048]{1,0:T(8,128)(2,1)S(1)}, u32[]{:S(2)}, u32[]{:S(2)}) collective-permute-start(bf16[128,2048]{1,0:T(8,128)(2,1)S(1)} %slice.41), channel_id=1, source_target_pairs={{0,96},{16,112},{32,0},{48,16},{64,32},{80,48},{96,64},{112,80},{1... | collective-permute-start | bytes 1572872 | tf_op jit(solution)/shard_map/ppermute | solution.py:18
  113.8 15.2 %collective-permute-start.22 = (bf16[128,2048]{1,0:T(8,128)(2,1)S(1)}, bf16[128,2048]{1,0:T(8,128)(2,1)S(1)}, u32[]{:S(2)}, u32[]{:S(2)}) collective-permute-start(bf16[128,2048]{1,0:T(8,128)(2,1)S(1)} %get-tuple-element.75), channel_id=1, source_target_pairs={{0,32},{16,48},{32,64},{48,80},{64,96},{80,112},{96,0},{112,16},{1... | collective-permute-start | bytes 1572872 | tf_op jit(solution)/shard_map/ppermute | solution.py:18
  114.1 36.4 %collective-permute-start.29 = (bf16[8,704,128]{2,1,0:T(8,128)(2,1)S(1)}, bf16[8,704,128]{2,1,0:T(8,128)(2,1)S(1)}, u32[]{:S(2)}, u32[]{:S(2)}) collective-permute-start(bf16[8,704,128]{2,1,0:T(8,128)(2,1)S(1)} %shard_map.101), channel_id=1, source_target_pairs={{0,2},{1,3},{2,0},{3,1},{4,6},{5,7},{6,4},{7,5},{8,10},{9,11},{10,... | collective-permute-start | bytes 4325384 | tf_op jit(solution)/shard_map/ppermute | solution.py:32
  114.5 16.5 %collective-permute-start.24 = (bf16[128,2048]{1,0:T(8,128)(2,1)S(1)}, bf16[128,2048]{1,0:T(8,128)(2,1)S(1)}, u32[]{:S(2)}, u32[]{:S(2)}) collective-permute-start(bf16[128,2048]{1,0:T(8,128)(2,1)S(1)} %get-tuple-element.77), channel_id=1, source_target_pairs={{0,96},{16,112},{32,0},{48,16},{64,32},{80,48},{96,64},{112,80},{1... | collective-permute-start | bytes 1572872 | tf_op jit(solution)/shard_map/ppermute | solution.py:18
  122.2 24.9 %collective-permute-start.26 = (bf16[1024,512]{1,0:T(8,128)(2,1)S(1)}, bf16[1024,512]{1,0:T(8,128)(2,1)S(1)}, u32[]{:S(2)}, u32[]{:S(2)}) collective-permute-start(bf16[1024,512]{1,0:T(8,128)(2,1)S(1)} %get-tuple-element.80), channel_id=1, source_target_pairs={{0,12},{4,0},{8,4},{12,8},{1,13},{5,1},{9,5},{13,9},{2,14},{6,2},{... | collective-permute-start | bytes 3145736 | tf_op jit(solution)/shard_map/ppermute | solution.py:24
  125.2 25.3 %collective-permute-start.27 = (bf16[1024,512]{1,0:T(8,128)(2,1)S(1)}, bf16[1024,512]{1,0:T(8,128)(2,1)S(1)}, u32[]{:S(2)}, u32[]{:S(2)}) collective-permute-start(bf16[1024,512]{1,0:T(8,128)(2,1)S(1)} %get-tuple-element.81), channel_id=1, source_target_pairs={{0,4},{4,8},{8,12},{12,0},{1,5},{5,9},{9,13},{13,1},{2,6},{6,10},{... | collective-permute-start | bytes 3145736 | tf_op jit(solution)/shard_map/ppermute | solution.py:24
  131.0 27.2 %collective-permute-start.23 = (bf16[256,2048]{1,0:T(8,128)(2,1)}, bf16[256,2048]{1,0:T(8,128)(2,1)}, u32[]{:S(2)}, u32[]{:S(2)}) collective-permute-start(bf16[256,2048]{1,0:T(8,128)(2,1)} %fusion), channel_id=1, source_target_pairs={{0,32},{16,48},{32,64},{48,80},{64,96},{80,112},{96,0},{112,16},{1... | collective-permute-start | bytes 3145736 | tf_op jit(solution)/shard_map/ppermute | solution.py:18
  133.0 28.7 %collective-permute-start.25 = (bf16[256,2048]{1,0:T(8,128)(2,1)}, bf16[256,2048]{1,0:T(8,128)(2,1)}, u32[]{:S(2)}, u32[]{:S(2)}) collective-permute-start(bf16[256,2048]{1,0:T(8,128)(2,1)} %fusion.1), channel_id=1, source_target_pairs={{0,96},{16,112},{32,0},{48,16},{64,32},{80,48},{96,64},{112,80},{1... | collective-permute-start | bytes 3145736 | tf_op jit(solution)/shard_map/ppermute | solution.py:18
  150.5 25.0 %collective-permute-start.28 = (bf16[1024,512]{1,0:T(8,128)(2,1)}, bf16[1024,512]{1,0:T(8,128)(2,1)S(1)}, u32[]{:S(2)}, u32[]{:S(2)}) collective-permute-start(bf16[1024,512]{1,0:T(8,128)(2,1)} %get-tuple-element.83), channel_id=1, source_target_pairs={{0,8},{4,12},{8,0},{12,4},{1,9},{5,13},{9,1},{13,5},{2,10},{6,14},... | collective-permute-start | bytes 3145736 | tf_op jit(solution)/shard_map/ppermute | solution.py:24
  152.1 28.4 %all-to-all-start.1 = ((bf16[8,704,128]{2,1,0:T(8,128)(2,1)}), bf16[8,704,128]{2,1,0:T(8,128)(2,1)S(1)}, u32[]{:S(2)}, u32[]{:S(2)}) async-start(bf16[8,704,128]{2,1,0:T(8,128)(2,1)} %add_convert_fusion), calls=%async_computation.1 | async-start | bytes 2883584 | tf_op jit(solution)/shard_map/all_to_all | solution.py:544
  157.0 31.1 %collective-permute-start.30 = (bf16[352,1024]{1,0:T(8,128)(2,1)}, bf16[352,1024]{1,0:T(8,128)(2,1)}, u32[]{:S(2)}, u32[]{:S(2)}) collective-permute-start(bf16[352,1024]{1,0:T(8,128)(2,1)} %get-tuple-element.89), channel_id=1, source_target_pairs={{0,2},{1,3},{2,0},{3,1},{4,6},{5,7},{6,4},{7,5},{8,10},{9,11},{10,... | collective-permute-start | bytes 2162696 | tf_op jit(solution)/shard_map/ppermute | solution.py:32
  178.8 17.0 %collective-permute-start.32 = (bf16[256,512]{1,0:T(8,128)(2,1)}, bf16[256,512]{1,0:T(8,128)(2,1)S(1)}, u32[]{:S(2)}, u32[]{:S(2)}) collective-permute-start(bf16[256,512]{1,0:T(8,128)(2,1)} %get-tuple-element.95), channel_id=1, source_target_pairs={{0,4},{4,8},{8,12},{12,0},{1,5},{5,9},{9,13},{13,1},{2,6},{6,10},{... | collective-permute-start | bytes 786440 | tf_op jit(solution)/shard_map/ppermute | solution.py:24
  180.2 15.7 %collective-permute-start.33 = (bf16[256,512]{1,0:T(8,128)(2,1)S(1)}, bf16[256,512]{1,0:T(8,128)(2,1)S(1)}, u32[]{:S(2)}, u32[]{:S(2)}) collective-permute-start(bf16[256,512]{1,0:T(8,128)(2,1)S(1)} %get-tuple-element.96), channel_id=1, source_target_pairs={{0,8},{4,12},{8,0},{12,4},{1,9},{5,13},{9,1},{13,5},{2,10},{6,14},... | collective-permute-start | bytes 786440 | tf_op jit(solution)/shard_map/ppermute | solution.py:24
  181.7 14.1 %collective-permute-start.36 = (bf16[256,512]{1,0:T(8,128)(2,1)S(1)}, bf16[256,512]{1,0:T(8,128)(2,1)S(1)}, u32[]{:S(2)}, u32[]{:S(2)}) collective-permute-start(bf16[256,512]{1,0:T(8,128)(2,1)S(1)} %get-tuple-element.107), channel_id=1, source_target_pairs={{0,64},{16,80},{32,96},{48,112},{64,0},{80,16},{96,32},{112,48},{1... | collective-permute-start | bytes 786440 | tf_op jit(solution)/shard_map/ppermute | solution.py:18
  (34 other events, 255.9 us)

commit v4 on v3

--- a/solution.py
+++ b/solution.py
@@ -559,7 +559,6 @@
     opposite = after(opposite, *from_y, *from_z)
     grad_input = own.astype(F32) + from_y[0].astype(F32) + from_y[1].astype(F32)
     grad_input = (grad_input + shift_y(opposite, 2).astype(F32)).astype(BF16)
-    output = after(output, grad_input)
     grad_input = after(grad_input, total)
     parts = [grad_input[2 * k * rows : 2 * (k + 1) * rows] for k in range(4)]
     input_parts = direct_scatter(shift_z, *parts)

time: 210 us -> 208 us (level)
  waiting for transfers between devices: 84.8 us -> 80.5 us
  starting transfers between devices: 65 us -> 67.2 us
  transfers between devices with their start and end apart: 42 -> 42, of which waited for: 21 -> 20; matrix products, arithmetic and copies ran while one was open for 6% -> 7% of each run, Pallas kernels for 11% -> 12%
where the time goes in v4:
time: 208 us
  waiting for transfers between devices  80.5 us (39%)
  starting transfers between devices  67.2 us (32%)
  Pallas kernels  38.5 us (19%)
  other arithmetic  12.8 us (6%)
  local copies, waits for them, and re-layouts  7.41 us (4%)
    ppermute x13, waiting for transfers between devices, shift_y(): return lax.ppermute(array, 'gy', [(i, (i + steps) % 4) for i in range(4)])  44.4 us
    pallas_call x9, Pallas kernels, assembled_call(): pl.pallas_call(body, out_shape=[jax.ShapeDtypeStruct(shape, dtype) for sh...  27.5 us
    ppermute x14, starting transfers between devices, shift_z(): lax.ppermute(array, 'gx', [(i, (i // 2 + steps) % 4 * 2 + i % 2) for i in...  23.6 us
    ppermute x13, starting transfers between devices, shift_y(): return lax.ppermute(array, 'gy', [(i, (i + steps) % 4) for i in range(4)])  18.6 us
    ppermute x14, waiting for transfers between devices, shift_z(): lax.ppermute(array, 'gx', [(i, (i // 2 + steps) % 4 * 2 + i % 2) for i in...  18.5 us
    pallas_call x9, Pallas kernels, local_call(): pl.pallas_call(body, out_shape=[jax.ShapeDtypeStruct(shape, BF16) for sha...  11.1 us
    ppermute x6, waiting for transfers between devices, swap_x_lo(): return lax.ppermute(array, 'gz', [(i, i ^ 2) for i in range(4)])  8.64 us
    all_to_all x1, starting transfers between devices, on_device(): w_near = lax.all_to_all(after(pieces, *four), 'gx', 0, 0, tiled=True)  6.69 us
  transfers between devices with their start and end apart: 42, of which 20 were waited for; matrix products, arithmetic and copies ran while one was open for 7% of the time, Pallas kernels for 12%

profile of v4, /device:TPU:0, one launch (start us, length us, event | category | flops | bytes accessed | tf_op | source)
XLA Modules:
  0.0 207.7 jit_solution(1656066033347753373)
XLA Ops:
  9.8 3.2 %shard_map.95 = bf16[8,704,128]{2,1,0:T(8,128)(2,1)} custom-call(bf16[128,2816]{1,0:T(8,128)(2,1)S(1)} %copy-done.8, bf16[128,2816]{1,0:T(8,128)(2,1)S(1)} %copy-done.9), custom_call_target="tpu_custom_call" | custom-call | tf_op jit(solution)/shard_map/pallas_call | solution.py:89
  13.3 6.7 %all-to-all-start = ((bf16[8,704,128]{2,1,0:T(8,128)(2,1)}), bf16[8,704,128]{2,1,0:T(8,128)(2,1)S(1)}, u32[]{:S(2)}, u32[]{:S(2)}) async-start(bf16[8,704,128]{2,1,0:T(8,128)(2,1)} %shard_map.95), calls=%async_computation | async-start | bytes 2883584 | tf_op jit(solution)/shard_map/all_to_all | solution.py:452
  22.5 3.1 %collective-permute-start.5 = (bf16[256,512]{1,0:T(8,128)(2,1)S(1)}, bf16[256,512]{1,0:T(8,128)(2,1)S(1)}, u32[]{:S(2)}, u32[]{:S(2)}) collective-permute-start(bf16[256,512]{1,0:T(8,128)(2,1)S(1)} %get-tuple-element.57.refs_0_), channel_id=1, source_target_pairs={{0,12},{4,0},{8,4},{12,8},{1,13},{5,1},{9,5},{13,9},{2,14},{6,2},{... | collective-permute-start | bytes 786440 | tf_op jit(solution)/shard_map/ppermute | solution.py:24
  27.2 3.2 %collective-permute-start.8 = (bf16[256,512]{1,0:T(8,128)(2,1)S(1)}, bf16[256,512]{1,0:T(8,128)(2,1)S(1)}, u32[]{:S(2)}, u32[]{:S(2)}) collective-permute-start(bf16[256,512]{1,0:T(8,128)(2,1)S(1)} %get-tuple-element.58), channel_id=1, source_target_pairs={{0,96},{16,112},{32,0},{48,16},{64,32},{80,48},{96,64},{112,80},{1... | collective-permute-start | bytes 786440 | tf_op jit(solution)/shard_map/ppermute | solution.py:18
  30.4 4.7 %collective-permute-done.5.refs_3_ = bf16[256,512]{1,0:T(8,128)(2,1)S(1)} collective-permute-done((bf16[256,512]{1,0:T(8,128)(2,1)S(1)}, bf16[256,512]{1,0:T(8,128)(2,1)S(1)}, u32[]{:S(2)}, u32[]{:S(2)}) %collective-permute-start.5) | collective-permute-done | bytes 262176 | tf_op jit(solution)/shard_map/ppermute | solution.py:24
  35.1 3.2 %collective-permute-start.7 = (bf16[256,512]{1,0:T(8,128)(2,1)S(1)}, bf16[256,512]{1,0:T(8,128)(2,1)S(1)}, u32[]{:S(2)}, u32[]{:S(2)}) collective-permute-start(bf16[256,512]{1,0:T(8,128)(2,1)S(1)} %get-tuple-element.58), channel_id=1, source_target_pairs={{0,64},{16,80},{32,96},{48,112},{64,0},{80,16},{96,32},{112,48},{1... | collective-permute-start | bytes 786440 | tf_op jit(solution)/shard_map/ppermute | solution.py:18
  39.2 5.7 %collective-permute-done.8 = bf16[256,512]{1,0:T(8,128)(2,1)S(1)} collective-permute-done((bf16[256,512]{1,0:T(8,128)(2,1)S(1)}, bf16[256,512]{1,0:T(8,128)(2,1)S(1)}, u32[]{:S(2)}, u32[]{:S(2)}) %collective-permute-start.8) | collective-permute-done | bytes 262176 | tf_op jit(solution)/shard_map/ppermute | solution.py:18
  53.1 3.0 %collective-permute-start.16 = (bf16[1024,512]{1,0:T(8,128)(2,1)S(1)}, bf16[1024,512]{1,0:T(8,128)(2,1)S(1)}, u32[]{:S(2)}, u32[]{:S(2)}) collective-permute-start(bf16[1024,512]{1,0:T(8,128)(2,1)S(1)} %pad_maximum_fusion.refs_0_), channel_id=1, source_target_pairs={{0,12},{4,0},{8,4},{12,8},{1,13},{5,1},{9,5},{13,9},{2,14},{6,2},{... | collective-permute-start | bytes 3145736 | tf_op jit(solution)/shard_map/ppermute | solution.py:24
  59.4 17.2 %collective-permute-done.16.refs_2_.refs_4_ = bf16[1024,512]{1,0:T(8,128)(2,1)S(1)} collective-permute-done((bf16[1024,512]{1,0:T(8,128)(2,1)S(1)}, bf16[1024,512]{1,0:T(8,128)(2,1)S(1)}, u32[]{:S(2)}, u32[]{:S(2)}) %collective-permute-start.16) | collective-permute-done | bytes 1048608 | tf_op jit(solution)/shard_map/ppermute | solution.py:24
  76.6 3.8 %collective-permute-start.17 = (bf16[512,512]{1,0:T(8,128)(2,1)S(1)}, bf16[512,512]{1,0:T(8,128)(2,1)S(1)}, u32[]{:S(2)}, u32[]{:S(2)}) collective-permute-start(bf16[512,512]{1,0:T(8,128)(2,1)S(1)} %slice.43), channel_id=1, source_target_pairs={{0,12},{4,0},{8,4},{12,8},{1,13},{5,1},{9,5},{13,9},{2,14},{6,2},{... | collective-permute-start | bytes 1572872 | tf_op jit(solution)/shard_map/ppermute | solution.py:24
  85.7 3.0 %shard_map.97.refs_4_ = f32[1024,352]{1,0:T(8,128)S(1)} custom-call(bf16[1024,512]{1,0:T(8,128)(2,1)S(1)} %pad_maximum_fusion.refs_0_, bf16[1024,512]{1,0:T(8,128)(2,1)S(1)} %collective-permute-done.14.refs_1_, bf16[1024,512]{1,0:T(8,128)(2,1)S(1)} %collective-permute-done.16.refs_2_.refs_4_, bf16[352,1024]{1,0:T(8,128)(2,1)} %refs_2_.3, ...), custom_call_target="tpu_custom_call" | custom-call | tf_op jit(solution)/shard_map/pallas_call | solution.py:121
  88.7 3.4 %collective-permute-done.15.refs_0_.refs_2_ = bf16[512,512]{1,0:T(8,128)(2,1)S(1)} collective-permute-done((bf16[512,512]{1,0:T(8,128)(2,1)S(1)}, bf16[512,512]{1,0:T(8,128)(2,1)S(1)}, u32[]{:S(2)}, u32[]{:S(2)}) %collective-permute-start.15) | collective-permute-done | bytes 524320 | tf_op jit(solution)/shard_map/ppermute | solution.py:24
  94.7 4.3 %shard_map.99 = (bf16[4,128,768]{2,1,0:T(8,128)(2,1)S(1)}, bf16[4,128,768]{2,1,0:T(8,128)(2,1)S(1)}) custom-call(bf16[256,2048]{1,0:T(8,128)(2,1)S(1)} %shard_map.94.refs_0_, bf16[256,2048]{1,0:T(8,128)(2,1)S(1)} %collective-permute-done.10.refs_1_, bf16[128,2048]{1,0:T(8,128)(2,1)S(1)} %collective-permute-done.11.refs_2_, ...), custom_call_target="tpu_custom_call" | custom-call | tf_op jit(solution)/shard_map/pallas_call | solution.py:121
  108.2 4.6 %shard_map.102 = (bf16[256,2048]{1,0:T(8,128)(2,1)S(1)}, bf16[256,2048]{1,0:T(8,128)(2,1)}, bf16[128,2048]{1,0:T(8,128)(2,1)S(1)}, bf16[128,2048]{1,0:T(8,128)(2,1)S(1)}, bf16[256,2048]{1,0:T(8,128)(2,1)}) custom-call(bf16[4,128,1152]{2,1,0:T(8,128)(2,1)S(1)} %shard_map.100.refs_5_.refs_0_, ...), custom_call_target="tpu_custom_call" | custom-call | tf_op jit(solution)/shard_map/pallas_call | solution.py:121
  117.4 4.8 %shard_map.104 = (bf16[1024,512]{1,0:T(8,128)(2,1)S(1)}, bf16[1024,512]{1,0:T(8,128)(2,1)S(1)}, bf16[1024,512]{1,0:T(8,128)(2,1)}, bf16[1024,512]{1,0:T(8,128)(2,1)S(1)}) custom-call(bf16[4,128,1152]{2,1,0:T(8,128)(2,1)S(1)} %shard_map.100.refs_5_.refs_0_, bf16[4,128,1152]{2,1,0:T(8,128)(2,1)S(1)} %collective-permute-done.21.refs_6_.refs_1_, ...), custom_call_target="tpu_custom_call" | custom-call | tf_op jit(solution)/shard_map/pallas_call | solution.py:121
  125.2 3.8 %collective-permute-done.22 = bf16[128,2048]{1,0:T(8,128)(2,1)S(1)} collective-permute-done((bf16[128,2048]{1,0:T(8,128)(2,1)S(1)}, bf16[128,2048]{1,0:T(8,128)(2,1)S(1)}, u32[]{:S(2)}, u32[]{:S(2)}) %collective-permute-start.22) | collective-permute-done | bytes 524320 | tf_op jit(solution)/shard_map/ppermute | solution.py:18
  133.0 3.2 %collective-permute-start.25 = (bf16[256,2048]{1,0:T(8,128)(2,1)}, bf16[256,2048]{1,0:T(8,128)(2,1)}, u32[]{:S(2)}, u32[]{:S(2)}) collective-permute-start(bf16[256,2048]{1,0:T(8,128)(2,1)} %fusion.1), channel_id=1, source_target_pairs={{0,96},{16,112},{32,0},{48,16},{64,32},{80,48},{96,64},{112,80},{1... | collective-permute-start | bytes 3145736 | tf_op jit(solution)/shard_map/ppermute | solution.py:18
  141.0 6.1 %collective-permute-done.31 = bf16[1024,512]{1,0:T(8,128)(2,1)S(1)} collective-permute-done((bf16[1024,512]{1,0:T(8,128)(2,1)S(1)}, bf16[1024,512]{1,0:T(8,128)(2,1)S(1)}, u32[]{:S(2)}, u32[]{:S(2)}) %collective-permute-start.31) | collective-permute-done | bytes 1048608 | tf_op jit(solution)/shard_map/ppermute | solution.py:24
  147.1 3.4 %collective-permute-done.32 = bf16[1024,512]{1,0:T(8,128)(2,1)S(1)} collective-permute-done((bf16[1024,512]{1,0:T(8,128)(2,1)S(1)}, bf16[1024,512]{1,0:T(8,128)(2,1)S(1)}, u32[]{:S(2)}, u32[]{:S(2)}) %collective-permute-start.32) | collective-permute-done | bytes 1048608 | tf_op jit(solution)/shard_map/ppermute | solution.py:24
  152.1 5.0 %all-to-all-start.1 = ((bf16[8,704,128]{2,1,0:T(8,128)(2,1)}), bf16[8,704,128]{2,1,0:T(8,128)(2,1)S(1)}, u32[]{:S(2)}, u32[]{:S(2)}) async-start(bf16[8,704,128]{2,1,0:T(8,128)(2,1)} %add_convert_fusion), calls=%async_computation.1 | async-start | bytes 2883584 | tf_op jit(solution)/shard_map/all_to_all | solution.py:544
  158.2 3.4 %collective-permute-done.25 = bf16[256,2048]{1,0:T(8,128)(2,1)} collective-permute-done((bf16[256,2048]{1,0:T(8,128)(2,1)}, bf16[256,2048]{1,0:T(8,128)(2,1)}, u32[]{:S(2)}, u32[]{:S(2)}) %collective-permute-start.25) | collective-permute-done | bytes 1048608 | tf_op jit(solution)/shard_map/ppermute | solution.py:18
  168.9 9.6 %collective-permute-done.33 = bf16[1024,512]{1,0:T(8,128)(2,1)} collective-permute-done((bf16[1024,512]{1,0:T(8,128)(2,1)}, bf16[1024,512]{1,0:T(8,128)(2,1)}, u32[]{:S(2)}, u32[]{:S(2)}) %collective-permute-start.33) | collective-permute-done | bytes 1048608 | tf_op jit(solution)/shard_map/ppermute | solution.py:24
  183.8 4.3 %collective-permute-done.27 = bf16[352,1024]{1,0:T(8,128)(2,1)} collective-permute-done((bf16[352,1024]{1,0:T(8,128)(2,1)}, bf16[352,1024]{1,0:T(8,128)(2,1)}, u32[]{:S(2)}, u32[]{:S(2)}) %collective-permute-start.27) | collective-permute-done | bytes 720928 | tf_op jit(solution)/shard_map/ppermute | solution.py:32
  196.2 3.7 %collective-permute-start.37 = (bf16[128,512]{1,0:T(8,128)(2,1)S(1)}, bf16[128,512]{1,0:T(8,128)(2,1)S(1)}, u32[]{:S(2)}, u32[]{:S(2)}) collective-permute-start(bf16[128,512]{1,0:T(8,128)(2,1)S(1)} %get-tuple-element.97), channel_id=1, source_target_pairs={{0,16},{16,0},{32,48},{48,32},{64,80},{80,64},{96,112},{112,96},{1... | collective-permute-start | bytes 393224 | tf_op jit(solution)/shard_map/ppermute | solution.py:28
  (122 shorter events, 90.0 us)
Async XLA Ops:
  13.3 39.7 %all-to-all-start = ((bf16[8,704,128]{2,1,0:T(8,128)(2,1)}), bf16[8,704,128]{2,1,0:T(8,128)(2,1)S(1)}, u32[]{:S(2)}, u32[]{:S(2)}) async-start(bf16[8,704,128]{2,1,0:T(8,128)(2,1)} %shard_map.95), calls=%async_computation | async-start | bytes 2883584 | tf_op jit(solution)/shard_map/all_to_all | solution.py:452
  20.0 32.2 %collective-permute-start.9 = (bf16[352,1024]{1,0:T(8,128)(2,1)}, bf16[352,1024]{1,0:T(8,128)(2,1)S(1)}, u32[]{:S(2)}, u32[]{:S(2)}) collective-permute-start(bf16[352,1024]{1,0:T(8,128)(2,1)} %refs_2_.3), channel_id=1, source_target_pairs={{0,2},{1,3},{2,0},{3,1},{4,6},{5,7},{6,4},{7,5},{8,10},{9,11},{10,... | collective-permute-start | bytes 2162696 | tf_op jit(solution)/shard_map/ppermute | solution.py:32
  27.2 17.7 %collective-permute-start.8 = (bf16[256,512]{1,0:T(8,128)(2,1)S(1)}, bf16[256,512]{1,0:T(8,128)(2,1)S(1)}, u32[]{:S(2)}, u32[]{:S(2)}) collective-permute-start(bf16[256,512]{1,0:T(8,128)(2,1)S(1)} %get-tuple-element.58), channel_id=1, source_target_pairs={{0,96},{16,112},{32,0},{48,16},{64,32},{80,48},{96,64},{112,80},{1... | collective-permute-start | bytes 786440 | tf_op jit(solution)/shard_map/ppermute | solution.py:18
  53.1 23.4 %collective-permute-start.16 = (bf16[1024,512]{1,0:T(8,128)(2,1)S(1)}, bf16[1024,512]{1,0:T(8,128)(2,1)S(1)}, u32[]{:S(2)}, u32[]{:S(2)}) collective-permute-start(bf16[1024,512]{1,0:T(8,128)(2,1)S(1)} %pad_maximum_fusion.refs_0_), channel_id=1, source_target_pairs={{0,12},{4,0},{8,4},{12,8},{1,13},{5,1},{9,5},{13,9},{2,14},{6,2},{... | collective-permute-start | bytes 3145736 | tf_op jit(solution)/shard_map/ppermute | solution.py:24
  56.1 24.2 %collective-permute-start.14 = (bf16[1024,512]{1,0:T(8,128)(2,1)S(1)}, bf16[1024,512]{1,0:T(8,128)(2,1)S(1)}, u32[]{:S(2)}, u32[]{:S(2)}) collective-permute-start(bf16[1024,512]{1,0:T(8,128)(2,1)S(1)} %pad_maximum_fusion.refs_0_), channel_id=1, source_target_pairs={{0,4},{4,8},{8,12},{12,0},{1,5},{5,9},{9,13},{13,1},{2,6},{6,10},{... | collective-permute-start | bytes 3145736 | tf_op jit(solution)/shard_map/ppermute | solution.py:24
  56.1 24.4 %collective-permute-start.12 = (bf16[256,2048]{1,0:T(8,128)(2,1)S(1)}, bf16[256,2048]{1,0:T(8,128)(2,1)S(1)}, u32[]{:S(2)}, u32[]{:S(2)}) collective-permute-start(bf16[256,2048]{1,0:T(8,128)(2,1)S(1)} %shard_map.94.refs_0_), channel_id=1, source_target_pairs={{0,96},{16,112},{32,0},{48,16},{64,32},{80,48},{96,64},{112,80},{1... | collective-permute-start | bytes 3145736 | tf_op jit(solution)/shard_map/ppermute | solution.py:18
  59.0 24.2 %collective-permute-start.10 = (bf16[256,2048]{1,0:T(8,128)(2,1)S(1)}, bf16[256,2048]{1,0:T(8,128)(2,1)S(1)}, u32[]{:S(2)}, u32[]{:S(2)}) collective-permute-start(bf16[256,2048]{1,0:T(8,128)(2,1)S(1)} %shard_map.94.refs_0_), channel_id=1, source_target_pairs={{0,32},{16,48},{32,64},{48,80},{64,96},{80,112},{96,0},{112,16},{1... | collective-permute-start | bytes 3145736 | tf_op jit(solution)/shard_map/ppermute | solution.py:18
  59.1 34.8 %collective-permute-start.18 = (bf16[8,704,128]{2,1,0:T(8,128)(2,1)S(1)}, bf16[8,704,128]{2,1,0:T(8,128)(2,1)S(1)}, u32[]{:S(2)}, u32[]{:S(2)}) collective-permute-start(bf16[8,704,128]{2,1,0:T(8,128)(2,1)S(1)} %all-to-all-done.refs_3_.refs_7_.refs_2_), channel_id=1, source_target_pairs={{0,2},{1,3},{2,0},{3,1},{4,6},{5,7},{6,4},{7,5},{8,10},{9,11},{10,... | collective-permute-start | bytes 4325384 | tf_op jit(solution)/shard_map/ppermute | solution.py:32
  80.5 13.3 %collective-permute-start.13 = (bf16[128,2048]{1,0:T(8,128)(2,1)S(1)}, bf16[128,2048]{1,0:T(8,128)(2,1)S(1)}, u32[]{:S(2)}, u32[]{:S(2)}) collective-permute-start(bf16[128,2048]{1,0:T(8,128)(2,1)S(1)} %slice.41), channel_id=1, source_target_pairs={{0,96},{16,112},{32,0},{48,16},{64,32},{80,48},{96,64},{112,80},{1... | collective-permute-start | bytes 1572872 | tf_op jit(solution)/shard_map/ppermute | solution.py:18
  113.8 15.2 %collective-permute-start.22 = (bf16[128,2048]{1,0:T(8,128)(2,1)S(1)}, bf16[128,2048]{1,0:T(8,128)(2,1)S(1)}, u32[]{:S(2)}, u32[]{:S(2)}) collective-permute-start(bf16[128,2048]{1,0:T(8,128)(2,1)S(1)} %get-tuple-element.74), channel_id=1, source_target_pairs={{0,32},{16,48},{32,64},{48,80},{64,96},{80,112},{96,0},{112,16},{1... | collective-permute-start | bytes 1572872 | tf_op jit(solution)/shard_map/ppermute | solution.py:18
  114.2 36.4 %collective-permute-start.26 = (bf16[8,704,128]{2,1,0:T(8,128)(2,1)S(1)}, bf16[8,704,128]{2,1,0:T(8,128)(2,1)S(1)}, u32[]{:S(2)}, u32[]{:S(2)}) collective-permute-start(bf16[8,704,128]{2,1,0:T(8,128)(2,1)S(1)} %shard_map.101), channel_id=1, source_target_pairs={{0,2},{1,3},{2,0},{3,1},{4,6},{5,7},{6,4},{7,5},{8,10},{9,11},{10,... | collective-permute-start | bytes 4325384 | tf_op jit(solution)/shard_map/ppermute | solution.py:32
  114.5 16.5 %collective-permute-start.24 = (bf16[128,2048]{1,0:T(8,128)(2,1)S(1)}, bf16[128,2048]{1,0:T(8,128)(2,1)S(1)}, u32[]{:S(2)}, u32[]{:S(2)}) collective-permute-start(bf16[128,2048]{1,0:T(8,128)(2,1)S(1)} %get-tuple-element.76), channel_id=1, source_target_pairs={{0,96},{16,112},{32,0},{48,16},{64,32},{80,48},{96,64},{112,80},{1... | collective-permute-start | bytes 1572872 | tf_op jit(solution)/shard_map/ppermute | solution.py:18
  122.2 24.9 %collective-permute-start.31 = (bf16[1024,512]{1,0:T(8,128)(2,1)S(1)}, bf16[1024,512]{1,0:T(8,128)(2,1)S(1)}, u32[]{:S(2)}, u32[]{:S(2)}) collective-permute-start(bf16[1024,512]{1,0:T(8,128)(2,1)S(1)} %get-tuple-element.92), channel_id=1, source_target_pairs={{0,12},{4,0},{8,4},{12,8},{1,13},{5,1},{9,5},{13,9},{2,14},{6,2},{... | collective-permute-start | bytes 3145736 | tf_op jit(solution)/shard_map/ppermute | solution.py:24
  125.2 25.3 %collective-permute-start.32 = (bf16[1024,512]{1,0:T(8,128)(2,1)S(1)}, bf16[1024,512]{1,0:T(8,128)(2,1)S(1)}, u32[]{:S(2)}, u32[]{:S(2)}) collective-permute-start(bf16[1024,512]{1,0:T(8,128)(2,1)S(1)} %get-tuple-element.93), channel_id=1, source_target_pairs={{0,4},{4,8},{8,12},{12,0},{1,5},{5,9},{9,13},{13,1},{2,6},{6,10},{... | collective-permute-start | bytes 3145736 | tf_op jit(solution)/shard_map/ppermute | solution.py:24
  131.0 27.2 %collective-permute-start.23 = (bf16[256,2048]{1,0:T(8,128)(2,1)}, bf16[256,2048]{1,0:T(8,128)(2,1)}, u32[]{:S(2)}, u32[]{:S(2)}) collective-permute-start(bf16[256,2048]{1,0:T(8,128)(2,1)} %fusion), channel_id=1, source_target_pairs={{0,32},{16,48},{32,64},{48,80},{64,96},{80,112},{96,0},{112,16},{1... | collective-permute-start | bytes 3145736 | tf_op jit(solution)/shard_map/ppermute | solution.py:18
  133.0 28.6 %collective-permute-start.25 = (bf16[256,2048]{1,0:T(8,128)(2,1)}, bf16[256,2048]{1,0:T(8,128)(2,1)}, u32[]{:S(2)}, u32[]{:S(2)}) collective-permute-start(bf16[256,2048]{1,0:T(8,128)(2,1)} %fusion.1), channel_id=1, source_target_pairs={{0,96},{16,112},{32,0},{48,16},{64,32},{80,48},{96,64},{112,80},{1... | collective-permute-start | bytes 3145736 | tf_op jit(solution)/shard_map/ppermute | solution.py:18
  150.5 28.0 %collective-permute-start.33 = (bf16[1024,512]{1,0:T(8,128)(2,1)}, bf16[1024,512]{1,0:T(8,128)(2,1)}, u32[]{:S(2)}, u32[]{:S(2)}) collective-permute-start(bf16[1024,512]{1,0:T(8,128)(2,1)} %get-tuple-element.94), channel_id=1, source_target_pairs={{0,8},{4,12},{8,0},{12,4},{1,9},{5,13},{9,1},{13,5},{2,10},{6,14},... | collective-permute-start | bytes 3145736 | tf_op jit(solution)/shard_map/ppermute | solution.py:24
  152.1 29.2 %all-to-all-start.1 = ((bf16[8,704,128]{2,1,0:T(8,128)(2,1)}), bf16[8,704,128]{2,1,0:T(8,128)(2,1)S(1)}, u32[]{:S(2)}, u32[]{:S(2)}) async-start(bf16[8,704,128]{2,1,0:T(8,128)(2,1)} %add_convert_fusion), calls=%async_computation.1 | async-start | bytes 2883584 | tf_op jit(solution)/shard_map/all_to_all | solution.py:544
  157.0 31.1 %collective-permute-start.27 = (bf16[352,1024]{1,0:T(8,128)(2,1)}, bf16[352,1024]{1,0:T(8,128)(2,1)}, u32[]{:S(2)}, u32[]{:S(2)}) collective-permute-start(bf16[352,1024]{1,0:T(8,128)(2,1)} %get-tuple-element.83), channel_id=1, source_target_pairs={{0,2},{1,3},{2,0},{3,1},{4,6},{5,7},{6,4},{7,5},{8,10},{9,11},{10,... | collective-permute-start | bytes 2162696 | tf_op jit(solution)/shard_map/ppermute | solution.py:32
  164.9 17.8 %collective-permute-start.28 = (bf16[256,512]{1,0:T(8,128)(2,1)}, bf16[256,512]{1,0:T(8,128)(2,1)S(1)}, u32[]{:S(2)}, u32[]{:S(2)}) collective-permute-start(bf16[256,512]{1,0:T(8,128)(2,1)} %get-tuple-element.88), channel_id=1, source_target_pairs={{0,12},{4,0},{8,4},{12,8},{1,13},{5,1},{9,5},{13,9},{2,14},{6,2},{... | collective-permute-start | bytes 786440 | tf_op jit(solution)/shard_map/ppermute | solution.py:24
  167.3 28.2 %collective-permute-start.29 = (bf16[256,512]{1,0:T(8,128)(2,1)}, bf16[256,512]{1,0:T(8,128)(2,1)S(1)}, u32[]{:S(2)}, u32[]{:S(2)}) collective-permute-start(bf16[256,512]{1,0:T(8,128)(2,1)} %get-tuple-element.89), channel_id=1, source_target_pairs={{0,4},{4,8},{8,12},{12,0},{1,5},{5,9},{9,13},{13,1},{2,6},{6,10},{... | collective-permute-start | bytes 786440 | tf_op jit(solution)/shard_map/ppermute | solution.py:24
  167.3 28.2 %collective-permute-start.30 = (bf16[256,512]{1,0:T(8,128)(2,1)S(1)}, bf16[256,512]{1,0:T(8,128)(2,1)S(1)}, u32[]{:S(2)}, u32[]{:S(2)}) collective-permute-start(bf16[256,512]{1,0:T(8,128)(2,1)S(1)} %get-tuple-element.90), channel_id=1, source_target_pairs={{0,8},{4,12},{8,0},{12,4},{1,9},{5,13},{9,1},{13,5},{2,10},{6,14},... | collective-permute-start | bytes 786440 | tf_op jit(solution)/shard_map/ppermute | solution.py:24
  182.6 13.0 %collective-permute-start.36 = (bf16[256,512]{1,0:T(8,128)(2,1)S(1)}, bf16[256,512]{1,0:T(8,128)(2,1)S(1)}, u32[]{:S(2)}, u32[]{:S(2)}) collective-permute-start(bf16[256,512]{1,0:T(8,128)(2,1)S(1)} %get-tuple-element.105), channel_id=1, source_target_pairs={{0,64},{16,80},{32,96},{48,112},{64,0},{80,16},{96,32},{112,48},{1... | collective-permute-start | bytes 786440 | tf_op jit(solution)/shard_map/ppermute | solution.py:18
  182.7 12.9 %collective-permute-start.35 = (bf16[256,512]{1,0:T(8,128)(2,1)S(1)}, bf16[256,512]{1,0:T(8,128)(2,1)S(1)}, u32[]{:S(2)}, u32[]{:S(2)}) collective-permute-start(bf16[256,512]{1,0:T(8,128)(2,1)S(1)} %get-tuple-element.106), channel_id=1, source_target_pairs={{0,32},{16,48},{32,64},{48,80},{64,96},{80,112},{96,0},{112,16},{1... | collective-permute-start | bytes 786440 | tf_op jit(solution)/shard_map/ppermute | solution.py:18
  (34 other events, 267.6 us)

commit v5 on v4

--- a/solution.py
+++ b/solution.py
@@ -444,11 +444,11 @@
     loss_scale = 1.0 / math.sqrt(tok_rows * 8)
     rows, columns = tok_rows // 2, 2 * tok_columns
 
-    mine, theirs = local_call(split_rows, [(rows, columns)] * 2, [tokens, grad_output])
+    mine, theirs = local_call(split_rows, [(rows, columns)] * 2, [tokens, grad_output], vmem=58)
     four = [mine, swap_x_lo(theirs), swap_x_hi(mine), swap_x(theirs)]
     t_block, g_block = local_call(arrange_rows, [(2 * rows, columns)] * 2, four)
 
-    (pieces,) = local_call(split_pair, [(8, 2 * own, rows_in)], [w_gate, w_up])
+    (pieces,) = local_call(split_pair, [(8, 2 * own, rows_in)], [w_gate, w_up], vmem=58)
     w_near = lax.all_to_all(after(pieces, *four), "gx", 0, 0, tiled=True)
     d_near, d_far = w_down, swap_x_lo(after(w_down, *four))
 

time: 208 us -> 207 us (level)
  local copies, waits for them, and re-layouts: 7.41 us -> 3.41 us
  starting transfers between devices: 67.2 us -> 69.6 us
  Pallas kernels: 38.5 us -> 40.6 us
    unnamed x32 -> x34, local copies, waits for them, and re-layouts: 5.93 us -> 1.93 us
    ppermute x14, waiting for transfers between devices: 18.5 us -> 15.7 us  [shift_z(): lax.ppermute(array, 'gx', [(i, (i // 2 + steps) % 4 * 2 + i % 2) for i in...]
  transfers between devices with their start and end apart: 42 -> 42, of which waited for: 20 -> 21; matrix products, arithmetic and copies ran while one was open for 7% -> 7% of each run, Pallas kernels for 12% -> 12%
where the time goes in v5:
time: 207 us
  waiting for transfers between devices  79 us (38%)
  starting transfers between devices  69.6 us (34%)
  Pallas kernels  40.6 us (20%)
  other arithmetic  12.8 us (6%)
  local copies, waits for them, and re-layouts  3.41 us (2%)
    ppermute x13, waiting for transfers between devices, shift_y(): return lax.ppermute(array, 'gy', [(i, (i + steps) % 4) for i in range(4)])  45.1 us
    pallas_call x9, Pallas kernels, assembled_call(): pl.pallas_call(body, out_shape=[jax.ShapeDtypeStruct(shape, dtype) for sh...  27.7 us
    ppermute x14, starting transfers between devices, shift_z(): lax.ppermute(array, 'gx', [(i, (i // 2 + steps) % 4 * 2 + i % 2) for i in...  23.6 us
    ppermute x13, starting transfers between devices, shift_y(): return lax.ppermute(array, 'gy', [(i, (i + steps) % 4) for i in range(4)])  20.5 us
    ppermute x14, waiting for transfers between devices, shift_z(): lax.ppermute(array, 'gx', [(i, (i // 2 + steps) % 4 * 2 + i % 2) for i in...  15.7 us
    pallas_call x9, Pallas kernels, local_call(): pl.pallas_call(body, out_shape=[jax.ShapeDtypeStruct(shape, BF16) for sha...  13 us
    ppermute x6, waiting for transfers between devices, swap_x_lo(): return lax.ppermute(array, 'gz', [(i, i ^ 2) for i in range(4)])  8.33 us
    all_to_all x1, starting transfers between devices, on_device(): w_near = lax.all_to_all(after(pieces, *four), 'gx', 0, 0, tiled=True)  6.73 us
  transfers between devices with their start and end apart: 42, of which 21 were waited for; matrix products, arithmetic and copies ran while one was open for 7% of the time, Pallas kernels for 12%

profile of v5, /device:TPU:0, one launch (start us, length us, event | category | flops | bytes accessed | tf_op | source)
XLA Modules:
  0.0 206.6 jit_solution(7518177676196392357)
XLA Ops:
  7.1 3.8 %shard_map.95 = bf16[8,704,128]{2,1,0:T(8,128)(2,1)} custom-call(bf16[128,2816]{1,0:T(8,128)(2,1)} %refs_0_.3, bf16[128,2816]{1,0:T(8,128)(2,1)} %refs_1_.3), custom_call_target="tpu_custom_call" | custom-call | tf_op jit(solution)/shard_map/pallas_call | solution.py:89
  13.1 6.7 %all-to-all-start = ((bf16[8,704,128]{2,1,0:T(8,128)(2,1)}), bf16[8,704,128]{2,1,0:T(8,128)(2,1)S(1)}, u32[]{:S(2)}, u32[]{:S(2)}) async-start(bf16[8,704,128]{2,1,0:T(8,128)(2,1)} %shard_map.95), calls=%async_computation | async-start | bytes 2883584 | tf_op jit(solution)/shard_map/all_to_all | solution.py:452
  22.3 3.1 %collective-permute-start.5 = (bf16[256,512]{1,0:T(8,128)(2,1)S(1)}, bf16[256,512]{1,0:T(8,128)(2,1)S(1)}, u32[]{:S(2)}, u32[]{:S(2)}) collective-permute-start(bf16[256,512]{1,0:T(8,128)(2,1)S(1)} %get-tuple-element.57.refs_0_), channel_id=1, source_target_pairs={{0,12},{4,0},{8,4},{12,8},{1,13},{5,1},{9,5},{13,9},{2,14},{6,2},{... | collective-permute-start | bytes 786440 | tf_op jit(solution)/shard_map/ppermute | solution.py:24
  26.9 3.2 %collective-permute-start.8 = (bf16[256,512]{1,0:T(8,128)(2,1)S(1)}, bf16[256,512]{1,0:T(8,128)(2,1)S(1)}, u32[]{:S(2)}, u32[]{:S(2)}) collective-permute-start(bf16[256,512]{1,0:T(8,128)(2,1)S(1)} %get-tuple-element.58), channel_id=1, source_target_pairs={{0,96},{16,112},{32,0},{48,16},{64,32},{80,48},{96,64},{112,80},{1... | collective-permute-start | bytes 786440 | tf_op jit(solution)/shard_map/ppermute | solution.py:18
  30.2 4.3 %collective-permute-done.5.refs_3_ = bf16[256,512]{1,0:T(8,128)(2,1)S(1)} collective-permute-done((bf16[256,512]{1,0:T(8,128)(2,1)S(1)}, bf16[256,512]{1,0:T(8,128)(2,1)S(1)}, u32[]{:S(2)}, u32[]{:S(2)}) %collective-permute-start.5) | collective-permute-done | bytes 262176 | tf_op jit(solution)/shard_map/ppermute | solution.py:24
  34.5 3.2 %collective-permute-start.7 = (bf16[256,512]{1,0:T(8,128)(2,1)S(1)}, bf16[256,512]{1,0:T(8,128)(2,1)S(1)}, u32[]{:S(2)}, u32[]{:S(2)}) collective-permute-start(bf16[256,512]{1,0:T(8,128)(2,1)S(1)} %get-tuple-element.58), channel_id=1, source_target_pairs={{0,64},{16,80},{32,96},{48,112},{64,0},{80,16},{96,32},{112,48},{1... | collective-permute-start | bytes 786440 | tf_op jit(solution)/shard_map/ppermute | solution.py:18
  38.6 6.1 %collective-permute-done.8 = bf16[256,512]{1,0:T(8,128)(2,1)S(1)} collective-permute-done((bf16[256,512]{1,0:T(8,128)(2,1)S(1)}, bf16[256,512]{1,0:T(8,128)(2,1)S(1)}, u32[]{:S(2)}, u32[]{:S(2)}) %collective-permute-start.8) | collective-permute-done | bytes 262176 | tf_op jit(solution)/shard_map/ppermute | solution.py:18
  52.4 3.0 %collective-permute-start.16 = (bf16[1024,512]{1,0:T(8,128)(2,1)S(1)}, bf16[1024,512]{1,0:T(8,128)(2,1)S(1)}, u32[]{:S(2)}, u32[]{:S(2)}) collective-permute-start(bf16[1024,512]{1,0:T(8,128)(2,1)S(1)} %pad_maximum_fusion.refs_0_), channel_id=1, source_target_pairs={{0,12},{4,0},{8,4},{12,8},{1,13},{5,1},{9,5},{13,9},{2,14},{6,2},{... | collective-permute-start | bytes 3145736 | tf_op jit(solution)/shard_map/ppermute | solution.py:24
  59.1 16.3 %collective-permute-done.16.refs_2_.refs_4_ = bf16[1024,512]{1,0:T(8,128)(2,1)S(1)} collective-permute-done((bf16[1024,512]{1,0:T(8,128)(2,1)S(1)}, bf16[1024,512]{1,0:T(8,128)(2,1)S(1)}, u32[]{:S(2)}, u32[]{:S(2)}) %collective-permute-start.16) | collective-permute-done | bytes 1048608 | tf_op jit(solution)/shard_map/ppermute | solution.py:24
  75.5 3.7 %collective-permute-start.17 = (bf16[512,512]{1,0:T(8,128)(2,1)S(1)}, bf16[512,512]{1,0:T(8,128)(2,1)S(1)}, u32[]{:S(2)}, u32[]{:S(2)}) collective-permute-start(bf16[512,512]{1,0:T(8,128)(2,1)S(1)} %slice.43), channel_id=1, source_target_pairs={{0,12},{4,0},{8,4},{12,8},{1,13},{5,1},{9,5},{13,9},{2,14},{6,2},{... | collective-permute-start | bytes 1572872 | tf_op jit(solution)/shard_map/ppermute | solution.py:24
  84.6 3.0 %shard_map.97.refs_4_ = f32[1024,352]{1,0:T(8,128)S(1)} custom-call(bf16[1024,512]{1,0:T(8,128)(2,1)S(1)} %pad_maximum_fusion.refs_0_, bf16[1024,512]{1,0:T(8,128)(2,1)S(1)} %collective-permute-done.14.refs_1_, bf16[1024,512]{1,0:T(8,128)(2,1)S(1)} %collective-permute-done.16.refs_2_.refs_4_, bf16[352,1024]{1,0:T(8,128)(2,1)} %refs_2_.3, ...), custom_call_target="tpu_custom_call" | custom-call | tf_op jit(solution)/shard_map/pallas_call | solution.py:121
  87.6 3.0 %collective-permute-done.15.refs_0_.refs_2_ = bf16[512,512]{1,0:T(8,128)(2,1)S(1)} collective-permute-done((bf16[512,512]{1,0:T(8,128)(2,1)S(1)}, bf16[512,512]{1,0:T(8,128)(2,1)S(1)}, u32[]{:S(2)}, u32[]{:S(2)}) %collective-permute-start.15) | collective-permute-done | bytes 524320 | tf_op jit(solution)/shard_map/ppermute | solution.py:24
  93.2 4.3 %shard_map.99 = (bf16[4,128,768]{2,1,0:T(8,128)(2,1)S(1)}, bf16[4,128,768]{2,1,0:T(8,128)(2,1)S(1)}) custom-call(bf16[256,2048]{1,0:T(8,128)(2,1)S(1)} %shard_map.94.refs_0_, bf16[256,2048]{1,0:T(8,128)(2,1)S(1)} %collective-permute-done.10.refs_1_, bf16[128,2048]{1,0:T(8,128)(2,1)S(1)} %collective-permute-done.11.refs_2_, ...), custom_call_target="tpu_custom_call" | custom-call | tf_op jit(solution)/shard_map/pallas_call | solution.py:121
  106.7 4.7 %shard_map.102 = (bf16[256,2048]{1,0:T(8,128)(2,1)S(1)}, bf16[256,2048]{1,0:T(8,128)(2,1)}, bf16[128,2048]{1,0:T(8,128)(2,1)S(1)}, bf16[128,2048]{1,0:T(8,128)(2,1)S(1)}, bf16[256,2048]{1,0:T(8,128)(2,1)}) custom-call(bf16[4,128,1152]{2,1,0:T(8,128)(2,1)S(1)} %shard_map.100.refs_5_.refs_0_, ...), custom_call_target="tpu_custom_call" | custom-call | tf_op jit(solution)/shard_map/pallas_call | solution.py:121
  117.1 4.8 %shard_map.104 = (bf16[1024,512]{1,0:T(8,128)(2,1)S(1)}, bf16[1024,512]{1,0:T(8,128)(2,1)S(1)}, bf16[1024,512]{1,0:T(8,128)(2,1)}, bf16[1024,512]{1,0:T(8,128)(2,1)S(1)}) custom-call(bf16[4,128,1152]{2,1,0:T(8,128)(2,1)S(1)} %shard_map.100.refs_5_.refs_0_, bf16[4,128,1152]{2,1,0:T(8,128)(2,1)S(1)} %collective-permute-done.21.refs_6_.refs_1_, ...), custom_call_target="tpu_custom_call" | custom-call | tf_op jit(solution)/shard_map/pallas_call | solution.py:121
  122.0 3.0 %collective-permute-start.31 = (bf16[1024,512]{1,0:T(8,128)(2,1)S(1)}, bf16[1024,512]{1,0:T(8,128)(2,1)S(1)}, u32[]{:S(2)}, u32[]{:S(2)}) collective-permute-start(bf16[1024,512]{1,0:T(8,128)(2,1)S(1)} %get-tuple-element.92), channel_id=1, source_target_pairs={{0,12},{4,0},{8,4},{12,8},{1,13},{5,1},{9,5},{13,9},{2,14},{6,2},{... | collective-permute-start | bytes 3145736 | tf_op jit(solution)/shard_map/ppermute | solution.py:24
  131.5 3.2 %collective-permute-start.25 = (bf16[256,2048]{1,0:T(8,128)(2,1)}, bf16[256,2048]{1,0:T(8,128)(2,1)}, u32[]{:S(2)}, u32[]{:S(2)}) collective-permute-start(bf16[256,2048]{1,0:T(8,128)(2,1)} %fusion.1), channel_id=1, source_target_pairs={{0,96},{16,112},{32,0},{48,16},{64,32},{80,48},{96,64},{112,80},{1... | collective-permute-start | bytes 3145736 | tf_op jit(solution)/shard_map/ppermute | solution.py:18
  139.6 7.3 %collective-permute-done.31 = bf16[1024,512]{1,0:T(8,128)(2,1)S(1)} collective-permute-done((bf16[1024,512]{1,0:T(8,128)(2,1)S(1)}, bf16[1024,512]{1,0:T(8,128)(2,1)S(1)}, u32[]{:S(2)}, u32[]{:S(2)}) %collective-permute-start.31) | collective-permute-done | bytes 1048608 | tf_op jit(solution)/shard_map/ppermute | solution.py:24
  146.9 3.4 %collective-permute-done.32 = bf16[1024,512]{1,0:T(8,128)(2,1)S(1)} collective-permute-done((bf16[1024,512]{1,0:T(8,128)(2,1)S(1)}, bf16[1024,512]{1,0:T(8,128)(2,1)S(1)}, u32[]{:S(2)}, u32[]{:S(2)}) %collective-permute-start.32) | collective-permute-done | bytes 1048608 | tf_op jit(solution)/shard_map/ppermute | solution.py:24
  151.8 4.4 %all-to-all-start.1 = ((bf16[8,704,128]{2,1,0:T(8,128)(2,1)}), bf16[8,704,128]{2,1,0:T(8,128)(2,1)S(1)}, u32[]{:S(2)}, u32[]{:S(2)}) async-start(bf16[8,704,128]{2,1,0:T(8,128)(2,1)} %add_convert_fusion), calls=%async_computation.1 | async-start | bytes 2883584 | tf_op jit(solution)/shard_map/all_to_all | solution.py:544
  161.5 4.4 %collective-permute-start.28 = (bf16[256,512]{1,0:T(8,128)(2,1)}, bf16[256,512]{1,0:T(8,128)(2,1)S(1)}, u32[]{:S(2)}, u32[]{:S(2)}) collective-permute-start(bf16[256,512]{1,0:T(8,128)(2,1)} %get-tuple-element.88), channel_id=1, source_target_pairs={{0,12},{4,0},{8,4},{12,8},{1,13},{5,1},{9,5},{13,9},{2,14},{6,2},{... | collective-permute-start | bytes 786440 | tf_op jit(solution)/shard_map/ppermute | solution.py:24
  167.5 10.8 %collective-permute-done.33 = bf16[1024,512]{1,0:T(8,128)(2,1)} collective-permute-done((bf16[1024,512]{1,0:T(8,128)(2,1)}, bf16[1024,512]{1,0:T(8,128)(2,1)}, u32[]{:S(2)}, u32[]{:S(2)}) %collective-permute-start.33) | collective-permute-done | bytes 1048608 | tf_op jit(solution)/shard_map/ppermute | solution.py:24
  183.6 3.5 %collective-permute-done.27 = bf16[352,1024]{1,0:T(8,128)(2,1)} collective-permute-done((bf16[352,1024]{1,0:T(8,128)(2,1)}, bf16[352,1024]{1,0:T(8,128)(2,1)}, u32[]{:S(2)}, u32[]{:S(2)}) %collective-permute-start.27) | collective-permute-done | bytes 720928 | tf_op jit(solution)/shard_map/ppermute | solution.py:32
  195.1 3.7 %collective-permute-start.37 = (bf16[128,512]{1,0:T(8,128)(2,1)S(1)}, bf16[128,512]{1,0:T(8,128)(2,1)S(1)}, u32[]{:S(2)}, u32[]{:S(2)}) collective-permute-start(bf16[128,512]{1,0:T(8,128)(2,1)S(1)} %get-tuple-element.97), channel_id=1, source_target_pairs={{0,16},{16,0},{32,48},{48,32},{64,80},{80,64},{96,112},{112,96},{1... | collective-permute-start | bytes 393224 | tf_op jit(solution)/shard_map/ppermute | solution.py:28
  (124 shorter events, 88.4 us)
Async XLA Ops:
  13.1 39.3 %all-to-all-start = ((bf16[8,704,128]{2,1,0:T(8,128)(2,1)}), bf16[8,704,128]{2,1,0:T(8,128)(2,1)S(1)}, u32[]{:S(2)}, u32[]{:S(2)}) async-start(bf16[8,704,128]{2,1,0:T(8,128)(2,1)} %shard_map.95), calls=%async_computation | async-start | bytes 2883584 | tf_op jit(solution)/shard_map/all_to_all | solution.py:452
  19.8 31.7 %collective-permute-start.9 = (bf16[352,1024]{1,0:T(8,128)(2,1)}, bf16[352,1024]{1,0:T(8,128)(2,1)S(1)}, u32[]{:S(2)}, u32[]{:S(2)}) collective-permute-start(bf16[352,1024]{1,0:T(8,128)(2,1)} %refs_2_.3), channel_id=1, source_target_pairs={{0,2},{1,3},{2,0},{3,1},{4,6},{5,7},{6,4},{7,5},{8,10},{9,11},{10,... | collective-permute-start | bytes 2162696 | tf_op jit(solution)/shard_map/ppermute | solution.py:32
  25.3 12.4 %collective-permute-start.4 = (bf16[256,512]{1,0:T(8,128)(2,1)S(1)}, bf16[256,512]{1,0:T(8,128)(2,1)S(1)}, u32[]{:S(2)}, u32[]{:S(2)}) collective-permute-start(bf16[256,512]{1,0:T(8,128)(2,1)S(1)} %get-tuple-element.57.refs_0_), channel_id=1, source_target_pairs={{0,8},{4,12},{8,0},{12,4},{1,9},{5,13},{9,1},{13,5},{2,10},{6,14},... | collective-permute-start | bytes 786440 | tf_op jit(solution)/shard_map/ppermute | solution.py:24
  26.0 12.3 %collective-permute-start.3 = (bf16[256,512]{1,0:T(8,128)(2,1)S(1)}, bf16[256,512]{1,0:T(8,128)(2,1)S(1)}, u32[]{:S(2)}, u32[]{:S(2)}) collective-permute-start(bf16[256,512]{1,0:T(8,128)(2,1)S(1)} %get-tuple-element.57.refs_0_), channel_id=1, source_target_pairs={{0,4},{4,8},{8,12},{12,0},{1,5},{5,9},{9,13},{13,1},{2,6},{6,10},{... | collective-permute-start | bytes 786440 | tf_op jit(solution)/shard_map/ppermute | solution.py:24
  26.9 17.7 %collective-permute-start.8 = (bf16[256,512]{1,0:T(8,128)(2,1)S(1)}, bf16[256,512]{1,0:T(8,128)(2,1)S(1)}, u32[]{:S(2)}, u32[]{:S(2)}) collective-permute-start(bf16[256,512]{1,0:T(8,128)(2,1)S(1)} %get-tuple-element.58), channel_id=1, source_target_pairs={{0,96},{16,112},{32,0},{48,16},{64,32},{80,48},{96,64},{112,80},{1... | collective-permute-start | bytes 786440 | tf_op jit(solution)/shard_map/ppermute | solution.py:18
  52.4 23.1 %collective-permute-start.16 = (bf16[1024,512]{1,0:T(8,128)(2,1)S(1)}, bf16[1024,512]{1,0:T(8,128)(2,1)S(1)}, u32[]{:S(2)}, u32[]{:S(2)}) collective-permute-start(bf16[1024,512]{1,0:T(8,128)(2,1)S(1)} %pad_maximum_fusion.refs_0_), channel_id=1, source_target_pairs={{0,12},{4,0},{8,4},{12,8},{1,13},{5,1},{9,5},{13,9},{2,14},{6,2},{... | collective-permute-start | bytes 3145736 | tf_op jit(solution)/shard_map/ppermute | solution.py:24
  55.4 23.8 %collective-permute-start.14 = (bf16[1024,512]{1,0:T(8,128)(2,1)S(1)}, bf16[1024,512]{1,0:T(8,128)(2,1)S(1)}, u32[]{:S(2)}, u32[]{:S(2)}) collective-permute-start(bf16[1024,512]{1,0:T(8,128)(2,1)S(1)} %pad_maximum_fusion.refs_0_), channel_id=1, source_target_pairs={{0,4},{4,8},{8,12},{12,0},{1,5},{5,9},{9,13},{13,1},{2,6},{6,10},{... | collective-permute-start | bytes 3145736 | tf_op jit(solution)/shard_map/ppermute | solution.py:24
  55.4 23.9 %collective-permute-start.12 = (bf16[256,2048]{1,0:T(8,128)(2,1)S(1)}, bf16[256,2048]{1,0:T(8,128)(2,1)S(1)}, u32[]{:S(2)}, u32[]{:S(2)}) collective-permute-start(bf16[256,2048]{1,0:T(8,128)(2,1)S(1)} %shard_map.94.refs_0_), channel_id=1, source_target_pairs={{0,96},{16,112},{32,0},{48,16},{64,32},{80,48},{96,64},{112,80},{1... | collective-permute-start | bytes 3145736 | tf_op jit(solution)/shard_map/ppermute | solution.py:18
  58.4 23.8 %collective-permute-start.10 = (bf16[256,2048]{1,0:T(8,128)(2,1)S(1)}, bf16[256,2048]{1,0:T(8,128)(2,1)S(1)}, u32[]{:S(2)}, u32[]{:S(2)}) collective-permute-start(bf16[256,2048]{1,0:T(8,128)(2,1)S(1)} %shard_map.94.refs_0_), channel_id=1, source_target_pairs={{0,32},{16,48},{32,64},{48,80},{64,96},{80,112},{96,0},{112,16},{1... | collective-permute-start | bytes 3145736 | tf_op jit(solution)/shard_map/ppermute | solution.py:18
  58.4 34.1 %collective-permute-start.18 = (bf16[8,704,128]{2,1,0:T(8,128)(2,1)S(1)}, bf16[8,704,128]{2,1,0:T(8,128)(2,1)S(1)}, u32[]{:S(2)}, u32[]{:S(2)}) collective-permute-start(bf16[8,704,128]{2,1,0:T(8,128)(2,1)S(1)} %all-to-all-done.refs_3_.refs_7_.refs_2_), channel_id=1, source_target_pairs={{0,2},{1,3},{2,0},{3,1},{4,6},{5,7},{6,4},{7,5},{8,10},{9,11},{10,... | collective-permute-start | bytes 4325384 | tf_op jit(solution)/shard_map/ppermute | solution.py:32
  79.4 13.1 %collective-permute-start.13 = (bf16[128,2048]{1,0:T(8,128)(2,1)S(1)}, bf16[128,2048]{1,0:T(8,128)(2,1)S(1)}, u32[]{:S(2)}, u32[]{:S(2)}) collective-permute-start(bf16[128,2048]{1,0:T(8,128)(2,1)S(1)} %slice.41), channel_id=1, source_target_pairs={{0,96},{16,112},{32,0},{48,16},{64,32},{80,48},{96,64},{112,80},{1... | collective-permute-start | bytes 1572872 | tf_op jit(solution)/shard_map/ppermute | solution.py:18
  112.3 15.2 %collective-permute-start.22 = (bf16[128,2048]{1,0:T(8,128)(2,1)S(1)}, bf16[128,2048]{1,0:T(8,128)(2,1)S(1)}, u32[]{:S(2)}, u32[]{:S(2)}) collective-permute-start(bf16[128,2048]{1,0:T(8,128)(2,1)S(1)} %get-tuple-element.74), channel_id=1, source_target_pairs={{0,32},{16,48},{32,64},{48,80},{64,96},{80,112},{96,0},{112,16},{1... | collective-permute-start | bytes 1572872 | tf_op jit(solution)/shard_map/ppermute | solution.py:18
  112.9 37.4 %collective-permute-start.26 = (bf16[8,704,128]{2,1,0:T(8,128)(2,1)S(1)}, bf16[8,704,128]{2,1,0:T(8,128)(2,1)S(1)}, u32[]{:S(2)}, u32[]{:S(2)}) collective-permute-start(bf16[8,704,128]{2,1,0:T(8,128)(2,1)S(1)} %shard_map.101), channel_id=1, source_target_pairs={{0,2},{1,3},{2,0},{3,1},{4,6},{5,7},{6,4},{7,5},{8,10},{9,11},{10,... | collective-permute-start | bytes 4325384 | tf_op jit(solution)/shard_map/ppermute | solution.py:32
  114.4 15.1 %collective-permute-start.24 = (bf16[128,2048]{1,0:T(8,128)(2,1)S(1)}, bf16[128,2048]{1,0:T(8,128)(2,1)S(1)}, u32[]{:S(2)}, u32[]{:S(2)}) collective-permute-start(bf16[128,2048]{1,0:T(8,128)(2,1)S(1)} %get-tuple-element.76), channel_id=1, source_target_pairs={{0,96},{16,112},{32,0},{48,16},{64,32},{80,48},{96,64},{112,80},{1... | collective-permute-start | bytes 1572872 | tf_op jit(solution)/shard_map/ppermute | solution.py:18
  122.0 24.9 %collective-permute-start.31 = (bf16[1024,512]{1,0:T(8,128)(2,1)S(1)}, bf16[1024,512]{1,0:T(8,128)(2,1)S(1)}, u32[]{:S(2)}, u32[]{:S(2)}) collective-permute-start(bf16[1024,512]{1,0:T(8,128)(2,1)S(1)} %get-tuple-element.92), channel_id=1, source_target_pairs={{0,12},{4,0},{8,4},{12,8},{1,13},{5,1},{9,5},{13,9},{2,14},{6,2},{... | collective-permute-start | bytes 3145736 | tf_op jit(solution)/shard_map/ppermute | solution.py:24
  125.0 25.3 %collective-permute-start.32 = (bf16[1024,512]{1,0:T(8,128)(2,1)S(1)}, bf16[1024,512]{1,0:T(8,128)(2,1)S(1)}, u32[]{:S(2)}, u32[]{:S(2)}) collective-permute-start(bf16[1024,512]{1,0:T(8,128)(2,1)S(1)} %get-tuple-element.93), channel_id=1, source_target_pairs={{0,4},{4,8},{8,12},{12,0},{1,5},{5,9},{9,13},{13,1},{2,6},{6,10},{... | collective-permute-start | bytes 3145736 | tf_op jit(solution)/shard_map/ppermute | solution.py:24
  129.5 27.2 %collective-permute-start.23 = (bf16[256,2048]{1,0:T(8,128)(2,1)}, bf16[256,2048]{1,0:T(8,128)(2,1)}, u32[]{:S(2)}, u32[]{:S(2)}) collective-permute-start(bf16[256,2048]{1,0:T(8,128)(2,1)} %fusion), channel_id=1, source_target_pairs={{0,32},{16,48},{32,64},{48,80},{64,96},{80,112},{96,0},{112,16},{1... | collective-permute-start | bytes 3145736 | tf_op jit(solution)/shard_map/ppermute | solution.py:18
  131.5 26.7 %collective-permute-start.25 = (bf16[256,2048]{1,0:T(8,128)(2,1)}, bf16[256,2048]{1,0:T(8,128)(2,1)}, u32[]{:S(2)}, u32[]{:S(2)}) collective-permute-start(bf16[256,2048]{1,0:T(8,128)(2,1)} %fusion.1), channel_id=1, source_target_pairs={{0,96},{16,112},{32,0},{48,16},{64,32},{80,48},{96,64},{112,80},{1... | collective-permute-start | bytes 3145736 | tf_op jit(solution)/shard_map/ppermute | solution.py:18
  150.3 28.0 %collective-permute-start.33 = (bf16[1024,512]{1,0:T(8,128)(2,1)}, bf16[1024,512]{1,0:T(8,128)(2,1)}, u32[]{:S(2)}, u32[]{:S(2)}) collective-permute-start(bf16[1024,512]{1,0:T(8,128)(2,1)} %get-tuple-element.94), channel_id=1, source_target_pairs={{0,8},{4,12},{8,0},{12,4},{1,9},{5,13},{9,1},{13,5},{2,10},{6,14},... | collective-permute-start | bytes 3145736 | tf_op jit(solution)/shard_map/ppermute | solution.py:24
  151.8 29.2 %all-to-all-start.1 = ((bf16[8,704,128]{2,1,0:T(8,128)(2,1)}), bf16[8,704,128]{2,1,0:T(8,128)(2,1)S(1)}, u32[]{:S(2)}, u32[]{:S(2)}) async-start(bf16[8,704,128]{2,1,0:T(8,128)(2,1)} %add_convert_fusion), calls=%async_computation.1 | async-start | bytes 2883584 | tf_op jit(solution)/shard_map/all_to_all | solution.py:544
  156.2 30.9 %collective-permute-start.27 = (bf16[352,1024]{1,0:T(8,128)(2,1)}, bf16[352,1024]{1,0:T(8,128)(2,1)}, u32[]{:S(2)}, u32[]{:S(2)}) collective-permute-start(bf16[352,1024]{1,0:T(8,128)(2,1)} %get-tuple-element.83), channel_id=1, source_target_pairs={{0,2},{1,3},{2,0},{3,1},{4,6},{5,7},{6,4},{7,5},{8,10},{9,11},{10,... | collective-permute-start | bytes 2162696 | tf_op jit(solution)/shard_map/ppermute | solution.py:32
  161.5 20.9 %collective-permute-start.28 = (bf16[256,512]{1,0:T(8,128)(2,1)}, bf16[256,512]{1,0:T(8,128)(2,1)S(1)}, u32[]{:S(2)}, u32[]{:S(2)}) collective-permute-start(bf16[256,512]{1,0:T(8,128)(2,1)} %get-tuple-element.88), channel_id=1, source_target_pairs={{0,12},{4,0},{8,4},{12,8},{1,13},{5,1},{9,5},{13,9},{2,14},{6,2},{... | collective-permute-start | bytes 786440 | tf_op jit(solution)/shard_map/ppermute | solution.py:24
  165.9 28.6 %collective-permute-start.29 = (bf16[256,512]{1,0:T(8,128)(2,1)}, bf16[256,512]{1,0:T(8,128)(2,1)S(1)}, u32[]{:S(2)}, u32[]{:S(2)}) collective-permute-start(bf16[256,512]{1,0:T(8,128)(2,1)} %get-tuple-element.89), channel_id=1, source_target_pairs={{0,4},{4,8},{8,12},{12,0},{1,5},{5,9},{9,13},{13,1},{2,6},{6,10},{... | collective-permute-start | bytes 786440 | tf_op jit(solution)/shard_map/ppermute | solution.py:24
  165.9 28.6 %collective-permute-start.30 = (bf16[256,512]{1,0:T(8,128)(2,1)S(1)}, bf16[256,512]{1,0:T(8,128)(2,1)S(1)}, u32[]{:S(2)}, u32[]{:S(2)}) collective-permute-start(bf16[256,512]{1,0:T(8,128)(2,1)S(1)} %get-tuple-element.90), channel_id=1, source_target_pairs={{0,8},{4,12},{8,0},{12,4},{1,9},{5,13},{9,1},{13,5},{2,10},{6,14},... | collective-permute-start | bytes 786440 | tf_op jit(solution)/shard_map/ppermute | solution.py:24
  (35 other events, 296.7 us)
